TPU v7x, 32 devices: a whole 2x2x4 slice. The times are simulated.
32 devices in a mesh: seq: 4 (over x, core), batch: 2 (over y), mp: 4 (over z).
Axes of the slice: x: 2, y: 2, z: 4, core: 2. Of those that a mesh axis runs over, the one named last changes fastest.
Arguments:
- xs: bfloat16 [2, 1536, 8192], P('batch', 'seq', 'mp'), may hold values from -6 to 6
- gate_z: bfloat16 [2, 1536, 8192], P('batch', 'seq', 'mp'), may hold values from -16 to 16
- b_in: bfloat16 [2, 1536, 128], P('batch', 'seq'), may hold values from -1.796875 to 1.796875
- c_in: bfloat16 [2, 1536, 128], P('batch', 'seq'), may hold values from -1.796875 to 1.796875
- log_decay: float32 [2, 1536, 128], P('batch', 'seq', 'mp'), may hold values from -4 to 0
- d_skip: float32 [128], P('mp'), may hold values from 0.5 to 2
- norm_gain: float32 [8192], P('mp'), may hold values from 0.5 to 1.5
- queries: bfloat16 [2, 1536, 4096], P('batch', 'seq', 'mp'), may hold values from -6 to 6
- keys_new: bfloat16 [2, 1536, 1024], P('batch', 'seq', 'mp'), may hold values from -6 to 6
- values_new: bfloat16 [2, 1536, 1024], P('batch', 'seq', 'mp'), may hold values from -6 to 6
- kv_pool: bfloat16 [64, 2, 64, 1024], P('batch', None, None, 'mp'), may hold values from -6 to 6
- state_pool: bfloat16 [128, 128, 16, 128], P('batch', 'mp'), may hold values from -6 to 6
- new_len: int32 [2], P('batch'), may hold values from 384 to 1536, as said below
- cached_blocks: int32 [2], P('batch'), may hold values from 1 to 4, 6 in all
- kv_owner: int32 [2, 4, 1], P('batch'), may hold values from 0 to 1; in each aligned block of 4 rows (0 to 3, 4 to 7, ..., all dimensions but the last counted through in order) at most 3 rows name the same one
- kv_slot: int32 [2, 4], P('batch'), may hold values from 0 to 31
- state_owner: int32 [2, 4, 1], P('batch'), may hold values from 0 to 1; in each aligned block of 4 rows (0 to 3, 4 to 7, ..., all dimensions but the last counted through in order) at most 3 rows name the same one
- state_slot: int32 [2, 4], P('batch'), may hold values from 0 to 63
Outputs:
- ssm_out: bfloat16 [2, 1536, 8192], P('batch', 'seq', 'mp')
- attn_out: bfloat16 [2, 1536, 4096], P('batch', 'seq', 'mp')
Inputs may be any that keep to these rules, and one draw needn't show every extreme that they name: `new_len`: at least 384; some prompt has exactly 1536. `kv_owner`: among the 4 entries of one prompt's list no owner appears more than 3 times. `state_owner`: among the 4 pieces of one prompt no owner appears more than 3 times.
All inputs are finite; a program needn't handle non-finite values. No bound on the sum of `cached_blocks` on one device may be relied on, other than what follows from the above.
Results may differ from a plain program's by a relative error of at most 0.0085.
Values may be sent and summed in bfloat16 or wider, within the bound.
No kernel may reach another device: no remote copies, remote signals or barrier semaphores. Data moves between devices by JAX's collectives and lax.ppermute only.
A program may use at most 128 MiB of HBM per device.

v0:
```python
import math

import jax
import jax.numpy as jnp
from jax import lax
from jax.sharding import PartitionSpec as P

H = 128
P_SIZE = 64
HD = 128
BQ = 128
CAP = 3


PRECISE = lax.Precision.HIGHEST
EPSILON = 1e-05
NEGATIVE = -1e30


def passed_along(value, axis, by):
    size = lax.axis_size(axis)
    pairs = [(i, i + by) for i in range(size) if 0 <= i + by < size]
    return lax.ppermute(value, axis, pairs)


def block_scan(state_in, inputs_x, inputs_b, inputs_c, decay_part):
    running = jnp.cumsum(decay_part, axis=0)
    span_here = decay_part.shape[0]
    lower = jnp.arange(span_here)[:, None] >= jnp.arange(span_here)[None, :]
    spread = running.T[:, :, None] - running.T[:, None, :]
    factors = jnp.where(lower[None], jnp.exp(jnp.minimum(spread, 0.0)), 0.0)
    intersections = jnp.dot(inputs_c, inputs_b.T, precision=PRECISE)
    inner = jnp.einsum("hts,shp->thp", factors * intersections[None], inputs_x, precision=PRECISE)
    carried = (
        jnp.einsum("tn,hpn->thp", inputs_c, state_in, precision=PRECISE)
        * jnp.exp(running)[:, :, None]
    )
    remain = jnp.exp(running[-1][None, :] - running)
    state_out = jnp.exp(running[-1])[:, None, None] * state_in + jnp.einsum(
        "shp,sn->hpn", inputs_x * remain[:, :, None], inputs_b, precision=PRECISE
    )
    return (state_out, inner + carried)


def owner_ranks(owners, usable):
    ordinal = jnp.arange(owners.shape[0])
    matches = (
        (owners[:, None] == owners[None, :])
        & (ordinal[:, None] > ordinal[None, :])
        & usable[None, :]
    )
    return jnp.sum(matches.astype(jnp.int32), axis=1)


def request_table(owners, ranking, slots, usable, owner_total):
    target = owners * CAP + ranking
    matched = (jnp.arange(owner_total * CAP)[:, None] == target[None, :]) & usable[None, :]
    flat_table = jnp.sum(jnp.where(matched, slots[None, :] + 1, 0), axis=1) - 1
    return flat_table.reshape(owner_total, CAP)


def lookup_records(source, requests):
    picked = source[jnp.maximum(requests, 0)]
    present = (requests >= 0).reshape(requests.shape + (1,) * (source.ndim - 1))
    return jnp.where(present, picked, jnp.zeros_like(picked))


def absorb_keys(carry, query_block, key_block, value_block, allowed):
    highest, totals, summed = carry
    scores = jnp.einsum(
        "tkgd,skd->kgts", query_block, key_block, preferred_element_type=jnp.float32
    ) * HD ** (-0.5)
    scores = jnp.where(allowed[None, None], scores, NEGATIVE)
    raised = jnp.maximum(highest, jnp.max(scores, axis=-1))
    probs_here = jnp.where(allowed[None, None], jnp.exp(scores - raised[..., None]), 0.0)
    shrink = jnp.exp(highest - raised)
    totals = totals * shrink + jnp.sum(probs_here, axis=-1)
    summed = summed * shrink[..., None] + jnp.einsum(
        "kgts,skd->kgtd",
        probs_here.astype(jnp.bfloat16),
        value_block,
        preferred_element_type=jnp.float32,
    )
    return (raised, totals, summed)


def per_device(
    xs,
    gate_z,
    b_in,
    c_in,
    log_decay,
    d_skip,
    norm_gain,
    queries,
    keys_new,
    values_new,
    kv_pool,
    state_pool,
    new_len,
    cached_blocks,
    kv_owner,
    kv_slot,
    state_owner,
    state_slot,
):
    seq_index = lax.axis_index("seq")
    seq_count = lax.axis_size("seq")
    owner_total = lax.axis_size("batch")
    span_local = xs.shape[1]
    heads_here = d_skip.shape[0]
    prompt_len = new_len[0]
    positions = seq_index * span_local + jnp.arange(span_local)
    valid = (positions < prompt_len).astype(jnp.float32)
    block_owners = kv_owner[0, :, 0]
    usable_block_flags = jnp.arange(kv_slot.shape[1]) < cached_blocks[0]
    block_ranks = owner_ranks(block_owners, usable_block_flags)
    piece_owners = state_owner[0, :, 0]
    piece_usable = jnp.ones((state_slot.shape[1],), dtype=bool)
    piece_ranks = owner_ranks(piece_owners, piece_usable)
    block_requests = request_table(
        block_owners, block_ranks, kv_slot[0], usable_block_flags, owner_total
    )
    piece_requests = request_table(
        piece_owners, piece_ranks, state_slot[0], piece_usable, owner_total
    )
    block_records = lookup_records(
        kv_pool, lax.all_to_all(block_requests, "batch", split_axis=0, concat_axis=0, tiled=True)
    )
    piece_records = lookup_records(
        state_pool, lax.all_to_all(piece_requests, "batch", split_axis=0, concat_axis=0, tiled=True)
    )
    block_records, piece_records = (
        lax.all_to_all(block_records, "batch", split_axis=0, concat_axis=0, tiled=True),
        lax.all_to_all(piece_records, "batch", split_axis=0, concat_axis=0, tiled=True),
    )
    inputs_x = (
        xs[0].astype(jnp.float32).reshape(span_local, heads_here, P_SIZE) * valid[:, None, None]
    )
    decay_in = log_decay[0] * valid[:, None]
    inputs_b = b_in[0].astype(jnp.float32)
    inputs_c = c_in[0].astype(jnp.float32)
    state_size = inputs_b.shape[1]
    block_count = span_local // BQ
    flat_width = heads_here * P_SIZE

    def advance(state, blocked):
        state_next, produced = block_scan(state, blocked[0], blocked[1], blocked[2], blocked[3])
        return (state_next, produced.reshape(BQ, flat_width))

    empty_state = jnp.zeros((heads_here, P_SIZE, state_size), jnp.float32)
    local_end, outputs = lax.scan(
        advance,
        empty_state,
        (
            inputs_x.reshape(block_count, BQ, heads_here, P_SIZE),
            inputs_b.reshape(block_count, BQ, state_size),
            inputs_c.reshape(block_count, BQ, state_size),
            decay_in.reshape(block_count, BQ, heads_here),
        ),
    )
    running = jnp.cumsum(decay_in, axis=0)
    through = jnp.exp(running[-1])
    flat_pieces = piece_records.reshape((owner_total * CAP,) + piece_records.shape[2:])
    pieces = flat_pieces[jnp.minimum(piece_owners * CAP + piece_ranks, owner_total * CAP - 1)]
    start_state = (
        jnp.transpose(pieces, (1, 0, 2, 3))
        .reshape(heads_here, P_SIZE, state_size)
        .astype(jnp.float32)
    )
    incoming = jnp.where(seq_index == 0, start_state, 0.0)
    for repeat in range(seq_count - 1):
        passed = passed_along(
            (through[:, None, None] * incoming + local_end).astype(jnp.bfloat16), "seq", 1
        ).astype(jnp.float32)
        incoming = jnp.where(seq_index == 0, start_state, passed)
    scan_out = outputs.reshape(span_local, heads_here, P_SIZE)
    scan_out = scan_out + jnp.exp(running)[:, :, None] * jnp.einsum(
        "tn,hpn->thp", inputs_c, incoming, precision=PRECISE
    )
    scan_out = scan_out + d_skip[None, :, None] * inputs_x
    gated = scan_out * jax.nn.silu(
        gate_z[0].astype(jnp.float32).reshape(span_local, heads_here, P_SIZE)
    )
    squares_local = jnp.sum(gated * gated, axis=(1, 2))
    squares_total = lax.psum(squares_local, "mp")
    square_mean = squares_total / (H * P_SIZE)
    normed = (
        gated
        * lax.rsqrt(square_mean + EPSILON)[:, None, None]
        * norm_gain.reshape(heads_here, P_SIZE)
    )
    ssm_out = (normed * valid[:, None, None]).reshape(span_local, flat_width).astype(jnp.bfloat16)
    kv_heads = keys_new.shape[2] // HD
    groups = queries.shape[2] // keys_new.shape[2]
    query_block = queries[0].reshape(span_local, kv_heads, groups, HD)
    flat_blocks = block_records.reshape((owner_total * CAP,) + block_records.shape[2:])
    blocks = flat_blocks[jnp.minimum(block_owners * CAP + block_ranks, owner_total * CAP - 1)]
    block_rows = blocks.shape[2]
    cached_len = blocks.shape[0] * block_rows
    portion = math.gcd(512, cached_len)
    portions = cached_len // portion
    cached_keys = blocks[:, 0].reshape(portions, portion, kv_heads, HD)
    cached_values = blocks[:, 1].reshape(portions, portion, kv_heads, HD)
    cached_usable = (jnp.arange(cached_len) // block_rows < cached_blocks[0]).reshape(
        portions, portion
    )
    start_carry = (
        jnp.full((kv_heads, groups, span_local), NEGATIVE, jnp.float32),
        jnp.zeros((kv_heads, groups, span_local), jnp.float32),
        jnp.zeros((kv_heads, groups, span_local, HD), jnp.float32),
    )

    def cached_step(carry, bundle):
        key_part, value_part, usable_part = bundle
        allowed = jnp.broadcast_to(usable_part[None, :], (span_local, portion))
        return (absorb_keys(carry, query_block, key_part, value_part, allowed), None)

    carry, unused = lax.scan(cached_step, start_carry, (cached_keys, cached_values, cached_usable))
    fresh_pair = (
        keys_new[0].reshape(span_local, kv_heads, HD),
        values_new[0].reshape(span_local, kv_heads, HD),
    )
    key_part = lax.all_gather(fresh_pair[0], "seq", axis=0, tiled=True)
    value_part = lax.all_gather(fresh_pair[1], "seq", axis=0, tiled=True)
    key_position = jnp.arange(key_part.shape[0])
    allowed = (key_position[None, :] <= positions[:, None]) & (key_position < prompt_len)[None, :]
    highest, totals, summed = absorb_keys(carry, query_block, key_part, value_part, allowed)
    attended = summed / totals[..., None]
    attended = jnp.transpose(attended, (2, 0, 1, 3)).reshape(span_local, kv_heads * groups * HD)
    attn_out = (attended * valid[:, None]).astype(jnp.bfloat16)
    return (ssm_out[None], attn_out[None])


def solution(mesh):
    in_specs = (
        P("batch", "seq", "mp"),
        P("batch", "seq", "mp"),
        P("batch", "seq", None),
        P("batch", "seq", None),
        P("batch", "seq", "mp"),
        P("mp"),
        P("mp"),
        P("batch", "seq", "mp"),
        P("batch", "seq", "mp"),
        P("batch", "seq", "mp"),
        P("batch", None, None, "mp"),
        P("batch", "mp", None, None),
        P("batch"),
        P("batch"),
        P("batch", None, None),
        P("batch", None),
        P("batch", None, None),
        P("batch", None),
    )
    out_specs = (P("batch", "seq", "mp"), P("batch", "seq", "mp"))
    return jax.shard_map(
        per_device, mesh=mesh, in_specs=in_specs, out_specs=out_specs, check_vma=False
    )
```

profile of v0, /device:TPU:0, one launch (start us, length us, event | category | flops | bytes accessed | tf_op | source)
XLA Modules:
  0.0 331.9 jit_solution(709291628127314930)
XLA Ops:
  1.5 0.9 convert_reduce_fusion
  4.4 4.2 %all-to-all-start.2 = ((s32[2,1,3]{2,1,0:T(1,128)}), s32[2,1,3]{2,1,0:T(1,128)}, u32[]{:S(2)}, u32[]{:S(2)}) async-start(s32[2,1,3]{2,1,0:T(1,128)} %bitcast.26), calls=%async_computation.2 | async-start | bytes 2048 | tf_op jit(solution)/shard_map/all_to_all | solution.py:128
  9.3 0.9 convert_reduce_fusion.1
  10.9 1.2 fusion.94
  13.4 0.9 copy.140
  15.2 0.9 reduce-window.6
  20.2 2.6 reshape_squeeze.11
  23.4 1.1 copy.155
  25.3 11.2 %all_gather.6 = bf16[1536,2,128]{2,0,1:T(8,128)(2,1)} all-gather(bf16[384,2,128]{2,0,1:T(8,128)(2,1)} %copy.156), channel_id=1, replica_groups=mesh['seq'=4,'batch'=2,'mp'=4] {'seq'}, dimensions={0}, use_global_device_ids=true | all-gather | bytes 983040 | tf_op jit(solution)/shard_map/all_gather | solution.py:224
  36.5 1.1 copy.158
  37.6 9.3 %all_gather.7 = bf16[1536,2,128]{0,2,1:T(8,128)(2,1)} all-gather(bf16[384,2,128]{0,2,1:T(8,128)(2,1)S(1)} %bitcast.275), channel_id=1, replica_groups=mesh['seq'=4,'batch'=2,'mp'=4] {'seq'}, dimensions={0}, use_global_device_ids=true | all-gather | bytes 983040 | tf_op jit(solution)/shard_map/all_gather | solution.py:225
  47.0 1.4 fusion.83
  48.3 3.1 copy.141
  51.4 5.7 %reshape.407 = f32[3,128,32,64]{1,0,3,2:T(4,128)} reshape(f32[1,384,2048]{1,2,0:T(8,128)} %copy.141) | data formatting | bytes 6291456 | tf_op jit(solution)/shard_map/convert_element_type | solution.py:138
  57.2 5.5 %broadcast_multiply_fusion = f32[3,128,32,64]{1,0,3,2:T(4,128)} fusion(f32[3,128,32,64]{1,0,3,2:T(4,128)} %reshape.407, f32[3,128]{1,0:T(4,128)S(1)} %fusion.90), kind=kLoop, calls=%fused_computation.67 | loop fusion | flops 786432 | bytes 6292992 | tf_op jit(solution)/shard_map/mul | solution.py:138
  64.2 139.5 %while.3 = (s32[]{:T(128)}, f32[32,64,128]{2,1,0:T(8,128)S(1)}, f32[3,128,2048]{1,0,2:T(4,128)}, f32[3,128,32]{2,1,0:T(8,128)}, f32[3,128,32,64]{1,0,3,2:T(4,128...) while((s32[]{:T(128)}, f32[32,64,128]{2,1,0:T(8,128)S(1)}, ...), condition=%wide.region_2.3_spmd.clone, body=%wide.region_0.2_spmd.clone.sunk | while | flops 1237598208 | bytes 17468192 | solution.py:152
  65.3 2.9 convolution_multiply_fusion.2
  68.3 1.1 fusion.134
  69.4 3.3 constant_dynamic-slice_fusion.2
  72.8 0.9 copy-done.2
  73.7 6.5 %fusion.135 = f32[128,32,64]{0,2,1:T(8,128)} fusion(f32[128,32,64]{0,2,1:T(8,128)} %convolution_multiply_fusion.2, f32[128,32,64]{0,2,1:T(8,128)S(1)} %bitcast.261, f32[128,128]{1,0:T(8,128)S(1)} %fusion.134, f32[32,128]{1,0:T(8,128)S(1)} %copy.211, pred[128,128]{1,0:T(8,128)(4,1)S(1)} %iota_compare_fusion.8), kind=kOutput, calls=%fused_computation.11.clone.1 | convolution fusion | flops 405012480 | bytes 3244032 | tf_op jit(solution)/shard_map/while/body/eval_jaxpr/hts,shp->thp/dot_general | solution.py:33
  80.2 27.6 %dynamic_update_slice.6 = f32[3,128,2048]{1,0,2:T(4,128)} dynamic-update-slice(f32[3,128,2048]{1,0,2:T(4,128)} %get-tuple-element.227, f32[1,128,2048]{1,0,2:T(1,128)} %bitcast.263, s32[]{:T(128)} %get-tuple-element.225, s32[]{:T(128)} %constant.55.clone.1..sunk, s32[]{:T(128)} %constant.55.clone.1..sunk) | dynamic-update-slice | bytes 2097156 | tf_op jit(solution)/shard_map/while/body/jit(dynamic_update_index_in_dim)/dynamic_update_slice | solution.py:152
  107.9 2.8 convolution_add_fusion.2
  111.8 2.9 convolution_multiply_fusion.2
  114.8 1.1 fusion.134
  115.9 3.3 constant_dynamic-slice_fusion.2
  119.3 0.9 copy-done.2
  120.2 6.5 %fusion.135 = f32[128,32,64]{0,2,1:T(8,128)} fusion(f32[128,32,64]{0,2,1:T(8,128)} %convolution_multiply_fusion.2, f32[128,32,64]{0,2,1:T(8,128)S(1)} %bitcast.261, f32[128,128]{1,0:T(8,128)S(1)} %fusion.134, f32[32,128]{1,0:T(8,128)S(1)} %copy.211, pred[128,128]{1,0:T(8,128)(4,1)S(1)} %iota_compare_fusion.8), kind=kOutput, calls=%fused_computation.11.clone.1 | convolution fusion | flops 405012480 | bytes 3244032 | tf_op jit(solution)/shard_map/while/body/eval_jaxpr/hts,shp->thp/dot_general | solution.py:33
  126.7 27.6 %dynamic_update_slice.6 = f32[3,128,2048]{1,0,2:T(4,128)} dynamic-update-slice(f32[3,128,2048]{1,0,2:T(4,128)} %get-tuple-element.227, f32[1,128,2048]{1,0,2:T(1,128)} %bitcast.263, s32[]{:T(128)} %get-tuple-element.225, s32[]{:T(128)} %constant.55.clone.1..sunk, s32[]{:T(128)} %constant.55.clone.1..sunk) | dynamic-update-slice | bytes 2097156 | tf_op jit(solution)/shard_map/while/body/jit(dynamic_update_index_in_dim)/dynamic_update_slice | solution.py:152
  154.4 2.8 convolution_add_fusion.2
  158.3 2.9 convolution_multiply_fusion.2
  161.3 1.1 fusion.134
  162.5 3.3 constant_dynamic-slice_fusion.2
  165.8 0.9 copy-done.2
  166.7 6.5 %fusion.135 = f32[128,32,64]{0,2,1:T(8,128)} fusion(f32[128,32,64]{0,2,1:T(8,128)} %convolution_multiply_fusion.2, f32[128,32,64]{0,2,1:T(8,128)S(1)} %bitcast.261, f32[128,128]{1,0:T(8,128)S(1)} %fusion.134, f32[32,128]{1,0:T(8,128)S(1)} %copy.211, pred[128,128]{1,0:T(8,128)(4,1)S(1)} %iota_compare_fusion.8), kind=kOutput, calls=%fused_computation.11.clone.1 | convolution fusion | flops 405012480 | bytes 3244032 | tf_op jit(solution)/shard_map/while/body/eval_jaxpr/hts,shp->thp/dot_general | solution.py:33
  173.3 27.6 %dynamic_update_slice.6 = f32[3,128,2048]{1,0,2:T(4,128)} dynamic-update-slice(f32[3,128,2048]{1,0,2:T(4,128)} %get-tuple-element.227, f32[1,128,2048]{1,0,2:T(1,128)} %bitcast.263, s32[]{:T(128)} %get-tuple-element.225, s32[]{:T(128)} %constant.55.clone.1..sunk, s32[]{:T(128)} %constant.55.clone.1..sunk) | dynamic-update-slice | bytes 2097156 | tf_op jit(solution)/shard_map/while/body/jit(dynamic_update_index_in_dim)/dynamic_update_slice | solution.py:152
  200.9 2.8 convolution_add_fusion.2
  203.7 1.3 pad_clamp_fusion.2
  205.0 6.0 %reshape.401 = f32[384,32,64]{0,2,1:T(8,128)} reshape(f32[3,128,2048]{1,0,2:T(4,128)} %get-tuple-element.64) | data formatting | bytes 6291456 | tf_op jit(solution)/shard_map/reshape | solution.py:177
  211.0 3.1 copy.149
  215.4 11.5 %fusion.38 = (f32[2,4,384]{2,1,0:T(4,128)}, f32[2,1536,384,4]{2,1,3,0:T(8,128)}) fusion(pred[384,1536]{0,1:T(8,128)(4,1)S(1)} %fusion.49, bf16[384,2,4,128]{3,2,1,0:T(4,128)(2,1)} %reshape_squeeze.11, bf16[1536,2,128]{2,0,1:T(8,128)(2,1)} %all_gather.6), kind=kOutput, calls=%fused_computation.47 | convolution fusion | flops 1222112256 | bytes 21049344 | tf_op jit(solution)/shard_map/tkgd,skd->kgts/dot_general | solution.py:70
  227.0 6.5 %all_to_all.22 = s32[2,1,3]{2,1,0:T(1,128)S(1)} all-to-all(s32[2,1,3]{2,1,0:T(1,128)S(1)} %bitcast.283), channel_id=1, replica_groups=mesh['seq'=4,'batch'=2,'mp'=4] {'batch'}, dimensions={0} | all-to-all | bytes 48 | tf_op jit(solution)/shard_map/all_to_all | solution.py:131
  233.5 1.2 maximum_reduce_fusion
  237.3 1.5 broadcast_select_fusion.1
  238.8 3.5 %all-to-all-start.3 = ((bf16[2,3,2,64,256]{4,3,2,1,0:T(8,128)(2,1)}), bf16[2,3,2,64,256]{4,3,2,1,0:T(8,128)(2,1)S(1)}, u32[]{:S(2)}, u32[]{:S(2)}) async-start(bf16[2,3,2,64,256]{4,3,2,1,0:T(8,128)(2,1)} %broadcast_select_fusion.1), calls=%async_computation.3 | async-start | bytes 786432 | tf_op jit(solution)/shard_map/all_to_all | solution.py:134
  243.7 4.1 %gather_fusion = bf16[6,32,16,128]{3,2,1,0:T(8,128)(2,1)S(1)} fusion(bf16[64,32,16,128]{3,2,1,0:T(8,128)(2,1)} %param.31, s32[1024]{0:T(1024)S(1)} %pad_clamp_fusion.3), kind=kCustom, calls=%fused_computation | custom fusion | bytes 1572888 | tf_op jit(solution)/shard_map/gather | solution.py:63
  247.7 1.0 broadcast_select_fusion
  248.7 3.7 %all-to-all-start.1 = ((bf16[2,3,32,16,128]{4,3,2,1,0:T(8,128)(2,1)}), bf16[2,3,32,16,128]{4,3,2,1,0:T(8,128)(2,1)S(1)}, u32[]{:S(2)}, u32[]{:S(2)}) async-start(bf16[2,3,32,16,128]{4,3,2,1,0:T(8,128)(2,1)} %broadcast_select_fusion), calls=%async_computation.1 | async-start | bytes 1572864 | tf_op jit(solution)/shard_map/all_to_all | solution.py:135
  253.2 2.4 bitcast_reduce_fusion
  255.6 6.9 %all-to-all-done.1 = bf16[2,3,32,16,128]{4,3,2,1,0:T(8,128)(2,1)S(1)} async-done(((bf16[2,3,32,16,128]{4,3,2,1,0:T(8,128)(2,1)}), bf16[2,3,32,16,128]{4,3,2,1,0:T(8,128)(2,1)S(1)}, u32[]{:S(2)}, u32[]{:S(2)}) %all-to-all-start.1) | async-done | bytes 786464 | tf_op jit(solution)/shard_map/all_to_all | solution.py:135
  263.8 1.3 collective-permute-start
  265.1 11.0 %fusion.39 = f32[2,4,384]{2,1,0:T(4,128)S(1)} fusion(f32[2,1536,384,4]{2,1,3,0:T(8,128)} %get-tuple-element.163, f32[2,4,384]{2,1,0:T(4,128)S(1)} %get-tuple-element.158, pred[384,1536]{0,1:T(8,128)(4,1)} %copy-done.6), kind=kLoop, calls=%fused_computation.48 | loop fusion | flops 23589888 | bytes 19488768 | tf_op jit(solution)/shard_map/reduce_sum | solution.py:77
  276.2 2.9 fusion.50
  279.3 3.3 collective-permute-start.1
  282.7 1.0 fusion.52
  283.9 1.0 fusion.72
  284.9 6.5 %collective-permute-start.2 = (bf16[32,64,128]{2,1,0:T(8,128)(2,1)}, bf16[32,64,128]{2,1,0:T(8,128)(2,1)S(1)}, u32[]{:S(2)}, u32[]{:S(2)}) collective-permute-start(bf16[32,64,128]{2,1,0:T(8,128)(2,1)} %fusion.72), channel_id=1, source_target_pairs={{0,8},{8,16},{16,24},{1,9},{9,17},{17,25},{2,10},{10,18},{18,26},{... | collective-permute-start | bytes 1572872 | tf_op jit(solution)/shard_map/ppermute | solution.py:23
  291.4 10.6 %fusion.54 = f32[384,2,4,128]{0,3,2,1:T(8,128)} fusion(f32[2,4,384,128]{2,3,1,0:T(8,128)S(1)} %fusion.52, f32[2,1536,384,4]{2,1,3,0:T(8,128)} %get-tuple-element.163, f32[2,4,384]{2,1,0:T(4,128)S(1)} %get-tuple-element.158, pred[384,1536]{0,1:T(8,128)(4,1)S(1)} %copy-done.7, bf16[1536,2,128]{0,2,1:T(8,128)(2,1)S(1)} %copy-done.8, ...), kind=kOutput, calls=%fused_computation.70 | convolution fusion | flops 1233125376 | bytes 23445504 | tf_op jit(solution)/shard_map/kgts,skd->kgtd/dot_general | solution.py:78
  302.0 3.0 copy.160
  305.1 2.6 multiply_convert_fusion.1
  307.9 5.7 %multiply_reduce_fusion = (f32[384]{0:T(512)S(1)}, f32[384,32,64]{0,2,1:T(8,128)}) fusion(f32[384,32,64]{0,2,1:T(8,128)} %bitcast.267, f32[384,32,64]{0,2,1:T(8,128)S(1)} %bitcast.265, f32[384]{0:T(512)S(1)} %copy-done.16, f32[32]{0:T(128)S(1)} %copy-done.25, f32[384,32,64]{0,2,1:T(8,128)} %reshape.401, f32[32,64,128]{2,1,0:T(8,128)S(1)} %bitcast_select_fusion.1, ...), kind=kOutput, calls=%fused_computation.62 | convolution fusion | flops 1217396352 | bytes 13782144 | tf_op jit(solution)/shard_map/tn,hpn->thp/dot_general | solution.py:178
  313.6 12.0 %psum.7 = f32[384]{0:T(512)S(1)} all-reduce(f32[384]{0:T(512)S(1)} %get-tuple-element.160), channel_id=1, replica_groups=mesh['seq'=4,'batch'=2,'mp'=4] {'mp'}, use_global_device_ids=true, to_apply=%region_8.9 | all-reduce | flops 384 | bytes 3072 | tf_op jit(solution)/shard_map/psum | solution.py:186
  325.7 3.7 %multiply_convert_fusion = bf16[384,32,64]{0,2,1:T(8,128)(2,1)} fusion(f32[384,32,64]{0,2,1:T(8,128)} %get-tuple-element.161, f32[32,64]{1,0:T(8,128)S(1)} %mul.266, f32[384]{0:T(512)S(1)} %add_rsqrt_fusion, f32[384]{0:T(512)S(1)} %copy-done.16), kind=kLoop, calls=%fused_computation.61 | loop fusion | flops 3145728 | bytes 4729856 | tf_op jit(solution)/shard_map/convert_element_type | solution.py:193
  329.3 2.6 copy.161
  (138 shorter events, 23.5 us)
Async XLA Ops:
  0.6 236.0 %copy-start = (bf16[32,2,64,256]{3,2,1,0:T(8,128)(2,1)S(1)}, bf16[32,2,64,256]{3,2,1,0:T(8,128)(2,1)}, u32[]{:S(2)}) copy-start(bf16[32,2,64,256]{3,2,1,0:T(8,128)(2,1)} %param.30) | copy-start | bytes 6291460
  4.4 222.5 %all-to-all-start.2 = ((s32[2,1,3]{2,1,0:T(1,128)}), s32[2,1,3]{2,1,0:T(1,128)}, u32[]{:S(2)}, u32[]{:S(2)}) async-start(s32[2,1,3]{2,1,0:T(1,128)} %bitcast.26), calls=%async_computation.2 | async-start | bytes 2048 | tf_op jit(solution)/shard_map/all_to_all | solution.py:128
  13.4 0.9 copy-start.15
  57.2 6.3 %copy-start.9 = (bf16[1,384,128]{2,1,0:T(8,128)(2,1)S(1)}, bf16[1,384,128]{2,1,0:T(8,128)(2,1)}, u32[]{:S(2)}) copy-start(bf16[1,384,128]{2,1,0:T(8,128)(2,1)} %param.22) | copy-start | bytes 294916
  57.2 6.3 %copy-start.10 = (bf16[1,384,128]{2,1,0:T(8,128)(2,1)S(1)}, bf16[1,384,128]{2,1,0:T(8,128)(2,1)}, u32[]{:S(2)}) copy-start(bf16[1,384,128]{2,1,0:T(8,128)(2,1)} %param.23) | copy-start | bytes 294916
  72.7 1.0 copy-start.2
  119.3 1.0 copy-start.2
  165.8 1.0 copy-start.2
  211.0 3.1 copy-start.21
  211.0 3.2 copy-start.19
  211.0 3.2 copy-start.20
  214.6 0.8 copy-start.6
  215.4 11.5 %copy-start.24 = (s32[2,1,3]{2,0,1:T(2,128)S(1)}, s32[2,1,3]{2,0,1:T(2,128)}, u32[]{:S(2)}) copy-start(s32[2,1,3]{2,0,1:T(2,128)} %sub.87) | copy-start | bytes 76
  233.5 2.6 copy-start.17
  238.8 10.0 %all-to-all-start.3 = ((bf16[2,3,2,64,256]{4,3,2,1,0:T(8,128)(2,1)}), bf16[2,3,2,64,256]{4,3,2,1,0:T(8,128)(2,1)S(1)}, u32[]{:S(2)}, u32[]{:S(2)}) async-start(bf16[2,3,2,64,256]{4,3,2,1,0:T(8,128)(2,1)} %broadcast_select_fusion.1), calls=%async_computation.3 | async-start | bytes 786432 | tf_op jit(solution)/shard_map/all_to_all | solution.py:134
  242.2 10.9 %copy-start.5 = (bf16[384,2,4,128]{3,2,1,0:T(4,128)(2,1)S(1)}, bf16[384,2,4,128]{3,2,1,0:T(4,128)(2,1)}, u32[]{:S(2)}) copy-start(bf16[384,2,4,128]{3,2,1,0:T(4,128)(2,1)} %reshape_squeeze.11) | copy-start | bytes 2359300
  242.3 10.9 %copy-start.22 = (pred[256]{0:T(512)(128)(4,1)S(1)}, pred[256]{0:T(512)(128)(4,1)}, u32[]{:S(2)}) copy-start(pred[256]{0:T(512)(128)(4,1)} %fusion.93) | copy-start | bytes 772
  248.7 6.9 %copy-start.13 = (f32[2,4,384]{2,1,0:T(4,128)S(1)}, f32[2,4,384]{2,1,0:T(4,128)}, u32[]{:S(2)}) copy-start(f32[2,4,384]{2,1,0:T(4,128)} %get-tuple-element.162) | copy-start | bytes 36868
  248.7 13.8 %all-to-all-start.1 = ((bf16[2,3,32,16,128]{4,3,2,1,0:T(8,128)(2,1)}), bf16[2,3,32,16,128]{4,3,2,1,0:T(8,128)(2,1)S(1)}, u32[]{:S(2)}, u32[]{:S(2)}) async-start(bf16[2,3,32,16,128]{4,3,2,1,0:T(8,128)(2,1)} %broadcast_select_fusion), calls=%async_computation.1 | async-start | bytes 1572864 | tf_op jit(solution)/shard_map/all_to_all | solution.py:135
  255.6 8.0 %copy-start.18 = (f32[32]{0:T(128)S(1)}, f32[32]{0:T(128)}, u32[]{:S(2)}) copy-start(f32[32]{0:T(128)} %fusion.83) | copy-start | bytes 388
  263.8 15.3 %collective-permute-start = (bf16[32,64,128]{2,1,0:T(8,128)(2,1)S(1)}, bf16[32,64,128]{2,1,0:T(8,128)(2,1)S(1)}, u32[]{:S(2)}, u32[]{:S(2)}) collective-permute-start(bf16[32,64,128]{2,1,0:T(8,128)(2,1)S(1)} %fusion.66), channel_id=1, source_target_pairs={{0,8},{8,16},{16,24},{1,9},{9,17},{17,25},{2,10},{10,18},{18,26},{... | collective-permute-start | bytes 1572872 | tf_op jit(solution)/shard_map/ppermute | solution.py:23
  265.1 11.0 %copy-start.23 = (pred[256]{0:T(512)(128)(4,1)S(1)}, pred[256]{0:T(512)(128)(4,1)}, u32[]{:S(2)}) copy-start(pred[256]{0:T(512)(128)(4,1)} %fusion.93) | copy-start | bytes 772
  276.2 6.5 %copy-start.14 = (f32[2,4,384]{2,1,0:T(4,128)S(1)}, f32[2,4,384]{2,1,0:T(4,128)}, u32[]{:S(2)}) copy-start(f32[2,4,384]{2,1,0:T(4,128)} %get-tuple-element.162) | copy-start | bytes 36868
  276.2 6.5 %copy-start.4 = (f32[2,256,384,4]{2,1,3,0:T(8,128)S(1)}, f32[2,256,384,4]{2,1,3,0:T(8,128)}, u32[]{:S(2)}) copy-start(f32[2,256,384,4]{2,1,3,0:T(8,128)} %get-tuple-element.165) | copy-start | bytes 9437188
  279.3 4.5 %collective-permute-start.1 = (bf16[32,64,128]{2,1,0:T(8,128)(2,1)S(1)}, bf16[32,64,128]{2,1,0:T(8,128)(2,1)S(1)}, u32[]{:S(2)}, u32[]{:S(2)}) collective-permute-start(bf16[32,64,128]{2,1,0:T(8,128)(2,1)S(1)} %fusion.69), channel_id=1, source_target_pairs={{0,8},{8,16},{16,24},{1,9},{9,17},{17,25},{2,10},{10,18},{18,26},{... | collective-permute-start | bytes 1572872 | tf_op jit(solution)/shard_map/ppermute | solution.py:23
  282.7 8.7 %copy-start.7 = (pred[384,1536]{0,1:T(8,128)(4,1)S(1)}, pred[384,1536]{0,1:T(8,128)(4,1)}, u32[]{:S(2)}) copy-start(pred[384,1536]{0,1:T(8,128)(4,1)} %copy-done.6) | copy-start | bytes 1769476
  282.7 8.7 %copy-start.8 = (bf16[1536,2,128]{0,2,1:T(8,128)(2,1)S(1)}, bf16[1536,2,128]{0,2,1:T(8,128)(2,1)}, u32[]{:S(2)}) copy-start(bf16[1536,2,128]{0,2,1:T(8,128)(2,1)} %all_gather.7) | copy-start | bytes 2359300
  284.9 22.8 %collective-permute-start.2 = (bf16[32,64,128]{2,1,0:T(8,128)(2,1)}, bf16[32,64,128]{2,1,0:T(8,128)(2,1)S(1)}, u32[]{:S(2)}, u32[]{:S(2)}) collective-permute-start(bf16[32,64,128]{2,1,0:T(8,128)(2,1)} %fusion.72), channel_id=1, source_target_pairs={{0,8},{8,16},{16,24},{1,9},{9,17},{17,25},{2,10},{10,18},{18,26},{... | collective-permute-start | bytes 1572872 | tf_op jit(solution)/shard_map/ppermute | solution.py:23
  302.0 3.0 copy-start.16
  305.1 2.8 copy-start.3
  305.1 2.8 copy-start.11
  305.1 2.8 copy-start.12
  305.1 2.8 copy-start.25
  325.7 6.2 %copy-start.1 = (bf16[32,2,64,256]{3,2,1,0:T(8,128)(2,1)S(1)}, bf16[32,2,64,256]{3,2,1,0:T(8,128)(2,1)}, u32[]{:S(2)}) copy-start(bf16[32,2,64,256]{3,2,1,0:T(8,128)(2,1)} %param.30) | copy-start | bytes 6291460
where the time goes:
time: 336 us; the launch traced here: 332 us
  local copies, waits for them, and re-layouts  140 us (42%)
  matrix products  71.2 us (21%)
  other arithmetic  48.8 us (15%)
  blocking collectives  39.1 us (12%)
  starting transfers between devices  22.5 us (7%)
  waiting for transfers between devices  7.12 us (2%)
    dynamic_update_slice x3, local copies, waits for them, and re-layouts, per_device(): lax.scan(advance, empty_state, (inputs_x.reshape(block_count, BQ, heads_h...  82.8 us
    dot_general x3, matrix products, block_scan(): jnp.einsum('hts,shp->thp', factors * intersections[None], inputs_x, preci...  19.5 us
    dot_general x2, matrix products, absorb_keys(): jnp.einsum('tkgd,skd->kgts', query_block, key_block, preferred_element_ty...  13.9 us
    reduce_sum x2, other arithmetic, absorb_keys(): totals = totals * shrink + jnp.sum(probs_here, axis=-1)  13.9 us
    psum x1, blocking collectives, per_device(): squares_total = lax.psum(squares_local, 'mp')  12 us
    dot_general x2, matrix products, absorb_keys(): jnp.einsum('kgts,skd->kgtd', probs_here.astype(jnp.bfloat16), value_block...  11.6 us
    all_gather x1, blocking collectives, per_device(): key_part = lax.all_gather(fresh_pair[0], 'seq', axis=0, tiled=True)  11.2 us
    ppermute x3, starting transfers between devices, passed_along(): return lax.ppermute(value, axis, pairs)  11.2 us
  transfers between devices with their start and end apart: 6, of which 2 were waited for; matrix products, arithmetic and copies ran while one was open for 70% of the time, Pallas kernels for 0%

commit v1 on v0

v1 whole, which is shorter than its diff:
```python
import functools

import jax
import jax.numpy as jnp
from jax import lax
from jax.experimental import pallas as pl
from jax.experimental.pallas import tpu as pltpu
from jax.sharding import PartitionSpec as P

P_SIZE = 64
HD = 128
CAP = 3
EPSILON = 1e-05
NEGATIVE = -1e30
HIGHEST = lax.Precision.HIGHEST
F32 = jnp.float32
BF16 = jnp.bfloat16
VMEM_LIMIT = 48 * 1024 * 1024

SMEM = pl.BlockSpec(memory_space=pltpu.SMEM)
ANY = pl.BlockSpec(memory_space=pl.ANY)


def params():
    return pltpu.CompilerParams(vmem_limit_bytes=VMEM_LIMIT)


def cost(flops, moved, exps=0):
    return pl.CostEstimate(flops=int(flops), bytes_accessed=int(moved), transcendentals=int(exps))


def mm(a, b, precision=None):
    return jnp.dot(a, b, preferred_element_type=F32, precision=precision)


def mm_nt(a, b):
    return lax.dot_general(a, b, (((1,), (1,)), ((), ())), preferred_element_type=F32)


def mm_tn(a, b):
    return lax.dot_general(a, b, (((0,), (0,)), ((), ())), preferred_element_type=F32)


def split(value, terms):
    parts = []
    rest = value
    for term in range(terms):
        part = rest.astype(BF16)
        parts.append(part)
        if term + 1 < terms:
            rest = rest - part.astype(F32)
    return jnp.concatenate(parts, axis=1)


def spread_matrix(heads, terms, width, first_head):
    row = lax.broadcasted_iota(jnp.int32, (terms * heads, width), 0)
    lane = lax.broadcasted_iota(jnp.int32, (terms * heads, width), 1)
    head = lane // P_SIZE + first_head
    return jnp.where(row % heads == head, 1.0, 0.0).astype(BF16)


def request_kernel(total, kv_owner, kv_slot, st_owner, st_slot, ask, kv_place, st_place):
    me = lax.axis_index("batch")
    for shift in range(total - 1):
        for k in range(2 * CAP):
            ask[shift, k] = 0

    def fill(owner_ref, slot_ref, place_ref, base):
        count = slot_ref.shape[1]

        def entry(e, unused):
            owner = owner_ref[0, e, 0]
            slot = slot_ref[0, e]
            rank = lax.fori_loop(
                0, e, lambda f, n: n + jnp.where(owner_ref[0, f, 0] == owner, 1, 0), jnp.int32(0)
            )
            shift = owner - me
            shift = jnp.where(shift < 0, shift + total, shift)

            @pl.when(shift == 0)
            def _():
                place_ref[0, e] = slot
                place_ref[1, e] = -1

            @pl.when(shift > 0)
            def _():
                ask[shift - 1, base + rank] = slot
                place_ref[0, e] = 0
                place_ref[1, e] = (shift - 1) * CAP + rank

            return unused

        lax.fori_loop(0, count, entry, 0)

    fill(kv_owner, kv_slot, kv_place, 0)
    fill(st_owner, st_slot, st_place, CAP)


def make_requests(total, kv_owner, kv_slot, st_owner, st_slot):
    i32 = jnp.int32
    return pl.pallas_call(
        functools.partial(request_kernel, total),
        out_shape=(
            jax.ShapeDtypeStruct((max(total - 1, 1), 2 * CAP), i32),
            jax.ShapeDtypeStruct((2, kv_slot.shape[1]), i32),
            jax.ShapeDtypeStruct((2, st_slot.shape[1]), i32),
        ),
        in_specs=[SMEM] * 4,
        out_specs=(SMEM,) * 3,
        name="requests",
    )(kv_owner, kv_slot, st_owner, st_slot)


def lookup_kernel(asked, kv_pool, st_pool, kv_out, st_out, sems):
    copies = []
    for k in range(CAP):
        copies.append(pltpu.make_async_copy(st_pool.at[asked[0, CAP + k]], st_out.at[k], sems.at[k]))
    for k in range(CAP):
        copies.append(pltpu.make_async_copy(kv_pool.at[asked[0, k]], kv_out.at[k], sems.at[CAP + k]))
    for copy in copies:
        copy.start()
    for copy in copies:
        copy.wait()


def look_up(asked, kv_pool, st_pool):
    return pl.pallas_call(
        lookup_kernel,
        out_shape=(
            jax.ShapeDtypeStruct((CAP,) + kv_pool.shape[1:], BF16),
            jax.ShapeDtypeStruct((CAP,) + st_pool.shape[1:], BF16),
        ),
        in_specs=[SMEM, ANY, ANY],
        out_specs=(ANY, ANY),
        scratch_shapes=[pltpu.SemaphoreType.DMA((2 * CAP,))],
        name="look_up",
    )(asked, kv_pool, st_pool)


def end_state_kernel(heads, new_len, decay, b_in, xs, end, through, running, remain, lasting, b_t):
    step = pl.program_id(0)
    span = decay.shape[0]
    width = xs.shape[1]
    first = lax.axis_index("seq") * span

    @pl.when(step == 0)
    def _():
        position = first + lax.broadcasted_iota(jnp.int32, (span, 1), 0)
        valid = position < new_len[0]
        dec = jnp.where(valid, decay[...], 0.0)
        row = lax.broadcasted_iota(jnp.int32, (span, span), 0)
        col = lax.broadcasted_iota(jnp.int32, (span, span), 1)
        lower = jnp.where(row >= col, 1.0, 0.0).astype(BF16)
        r3 = mm(lower, split(dec, 3))
        r = r3[:, :heads] + r3[:, heads : 2 * heads] + r3[:, 2 * heads :]
        running[...] = r
        last = r[span - 1 :, :]
        remain[...] = split(jnp.exp(last - r), 2)
        lasting[...] = split(jnp.broadcast_to(jnp.exp(last), (8, heads)), 3)
        b = jnp.where(valid, b_in[...].astype(F32), 0.0)
        b_t[...] = b.T.astype(BF16)

    first_head = step * (width // P_SIZE)
    factor = mm(remain[...], spread_matrix(heads, 2, width, first_head))
    weighted = (xs[...].astype(F32) * factor).astype(BF16)
    end[...] = mm(b_t[...], weighted)
    through[...] = mm(lasting[...], spread_matrix(heads, 3, width, first_head))


def end_state(new_len, decay, b_in, xs):
    span, channels = xs.shape
    heads = decay.shape[1]
    n = b_in.shape[1]
    width = min(512, channels)
    return pl.pallas_call(
        functools.partial(end_state_kernel, heads),
        grid=(channels // width,),
        out_shape=(
            jax.ShapeDtypeStruct((n, channels), F32),
            jax.ShapeDtypeStruct((8, channels), F32),
            jax.ShapeDtypeStruct((span, heads), F32),
        ),
        in_specs=[
            SMEM,
            pl.BlockSpec((span, heads), lambda i: (0, 0)),
            pl.BlockSpec((span, n), lambda i: (0, 0)),
            pl.BlockSpec((span, width), lambda i: (0, i)),
        ],
        out_specs=(
            pl.BlockSpec((n, width), lambda i: (0, i)),
            pl.BlockSpec((8, width), lambda i: (0, i)),
            pl.BlockSpec((span, heads), lambda i: (0, 0)),
        ),
        scratch_shapes=[
            pltpu.VMEM((span, 2 * heads), BF16),
            pltpu.VMEM((8, 3 * heads), BF16),
            pltpu.VMEM((n, span), BF16),
        ],
        compiler_params=params(),
        cost_estimate=cost(2 * span * channels * n, span * channels * 2 + n * channels * 4),
        name="end_state",
    )(new_len, decay, b_in, xs)


def local_scan_kernel(heads, new_len, running, b_in, c_in, xs, d_skip, out, cols, rows, inter):
    step = pl.program_id(0)
    span, width = xs.shape
    first = lax.axis_index("seq") * span
    group = width // P_SIZE
    bq = 128
    blocks = span // bq

    @pl.when(step == 0)
    def _():
        r = running[...]
        for g in range(heads // group):
            cols[g] = r[:, g * group : (g + 1) * group]
        rows[...] = r.T
        position = first + lax.broadcasted_iota(jnp.int32, (span, 1), 0)
        b = jnp.where(position < new_len[0], b_in[...].astype(F32), 0.0).astype(BF16)
        inter[...] = mm_nt(c_in[...], b)

    col = cols[step]
    row = rows[pl.ds(pl.multiple_of(step * group, group), group), :]
    skip = mm(split(d_skip[...], 3), spread_matrix(heads, 3, width, step * group))
    lower = lax.broadcasted_iota(jnp.int32, (bq, bq), 0) >= lax.broadcasted_iota(
        jnp.int32, (bq, bq), 1
    )
    left = lax.broadcasted_iota(jnp.int32, (span, 2 * P_SIZE), 1) < P_SIZE
    for pair in range(group // 2):
        lanes = slice(pair * 2 * P_SIZE, (pair + 1) * 2 * P_SIZE)
        x_pair = xs[:, lanes]
        zero = jnp.zeros_like(x_pair)
        sides = (jnp.where(left, x_pair, zero), jnp.where(left, zero, x_pair))
        for i in range(blocks):
            here = slice(i * bq, (i + 1) * bq)
            lhs, rhs = [], []
            for side in range(2):
                h = pair * 2 + side
                at_t = jnp.broadcast_to(col[here, h : h + 1], (bq, bq))
                for j in range(i + 1):
                    there = slice(j * bq, (j + 1) * bq)
                    gap = at_t - row[h : h + 1, there]
                    if j == i:
                        gap = jnp.where(lower, gap, NEGATIVE)
                    lhs.append((jnp.exp(gap) * inter[here, there]).astype(BF16))
                    rhs.append(sides[side][there])
            y = mm(jnp.concatenate(lhs, axis=1), jnp.concatenate(rhs, axis=0))
            out[here, lanes] = y + skip[:1, lanes] * x_pair[here].astype(F32)


def local_scan(new_len, running, b_in, c_in, xs, d_skip):
    span, channels = xs.shape
    heads = running.shape[1]
    n = b_in.shape[1]
    width = min(512, channels)
    group = width // P_SIZE
    whole = lambda *shape: pl.BlockSpec(shape, lambda i: (0,) * len(shape))
    return pl.pallas_call(
        functools.partial(local_scan_kernel, heads),
        grid=(channels // width,),
        out_shape=jax.ShapeDtypeStruct((span, channels), F32),
        in_specs=[
            SMEM,
            whole(span, heads),
            whole(span, n),
            whole(span, n),
            pl.BlockSpec((span, width), lambda i: (0, i)),
            whole(1, heads),
        ],
        out_specs=pl.BlockSpec((span, width), lambda i: (0, i)),
        scratch_shapes=[
            pltpu.VMEM((heads // group, span, group), F32),
            pltpu.VMEM((heads, span), F32),
            pltpu.VMEM((span, span), F32),
        ],
        compiler_params=params(),
        cost_estimate=cost(
            2 * span * span * channels, span * channels * 6, span * span * heads // 2
        ),
        name="local_scan",
    )(new_len, running, b_in, c_in, xs, d_skip)


def start_kernel(pieces, place, pool, received, end, through, start, state, gathered, sems):
    here = lax.axis_index("seq") == 0

    @pl.when(here)
    def _():
        for j in range(pieces):
            slot, taken = place[0, j], place[1, j]

            @pl.when(taken < 0)
            def _():
                pltpu.make_async_copy(pool.at[slot], gathered.at[j], sems.at[j]).start()

            @pl.when(taken >= 0)
            def _():
                pltpu.make_async_copy(received.at[taken], gathered.at[j], sems.at[j]).start()

        for j in range(pieces):
            pltpu.make_async_copy(pool.at[0], gathered.at[j], sems.at[j]).wait()
        heads = gathered.shape[1]
        for h in range(0, heads, 2):
            parts = [gathered[j, h + k] for k in range(2) for j in range(pieces)]
            block = jnp.concatenate(parts, axis=0).astype(F32).T
            lanes = slice(h * P_SIZE, (h + 2) * P_SIZE)
            start[:, lanes] = block.astype(BF16)
            state[:, lanes] = (through[:1, lanes] * block + end[:, lanes]).astype(BF16)


def start_state(place, pool, received, end, through):
    n, channels = end.shape
    pieces = place.shape[1]
    shape = jax.ShapeDtypeStruct((n, channels), BF16)
    whole = pl.BlockSpec(memory_space=pltpu.VMEM)
    return pl.pallas_call(
        functools.partial(start_kernel, pieces),
        out_shape=(shape, shape),
        in_specs=[SMEM, ANY, ANY, whole, whole],
        out_specs=(whole, whole),
        scratch_shapes=[
            pltpu.VMEM((pieces,) + pool.shape[1:], BF16),
            pltpu.SemaphoreType.DMA((pieces,)),
        ],
        compiler_params=params(),
        cost_estimate=cost(n * channels * 4, n * channels * 8),
        name="start_state",
    )(place, pool, received, end, through)


def assembled_start(place, pool, received):
    local = pool[place[0]]
    taken = received[jnp.maximum(place[1], 0)]
    pieces = jnp.where((place[1] < 0)[:, None, None, None], local, taken)
    pieces = jnp.transpose(pieces, (1, 0, 2, 3))
    heads = pieces.shape[0]
    return pieces.reshape(heads * P_SIZE, pieces.shape[-1]).T


def advance_kernel(turn, state_in, end, through, state):
    @pl.when(lax.axis_index("seq") == turn)
    def _():
        state[...] = (through[:1, :] * state_in[...].astype(F32) + end[...]).astype(BF16)


def advance(turn, state_in, end, through):
    n, channels = end.shape
    whole = pl.BlockSpec(memory_space=pltpu.VMEM)
    return pl.pallas_call(
        functools.partial(advance_kernel, turn),
        out_shape=jax.ShapeDtypeStruct((n, channels), BF16),
        in_specs=[whole] * 3,
        out_specs=whole,
        compiler_params=params(),
        cost_estimate=cost(n * channels * 2, n * channels * 8),
        name="advance_state",
    )(state_in, end, through)


def gate_kernel(heads, running, c_in, local, gate, *rest):
    states = rest[:4]
    gated, squares, incoming, factors, summed, sem = rest[4:]
    step = pl.program_id(0)
    span, width = local.shape
    seq = lax.axis_index("seq")

    @pl.when(step == 0)
    def _():
        for turn in range(4):

            @pl.when(seq == turn)
            def _():
                pltpu.make_async_copy(states[turn], incoming, sem).start()

        factors[...] = split(jnp.exp(running[...]), 3)
        summed[...] = jnp.zeros_like(summed)
        pltpu.make_async_copy(states[0], incoming, sem).wait()

    factor = mm(factors[...], spread_matrix(heads, 3, width, step * (width // P_SIZE)))
    lanes = pl.ds(pl.multiple_of(step * width, width), width)
    carried = mm(c_in[...], incoming[:, lanes])
    z = gate[...].astype(F32)
    value = (local[...] + factor * carried) * (z / (1.0 + jnp.exp(-z)))
    gated[...] = value
    square = value * value
    total = square[:, :128]
    for k in range(1, width // 128):
        total = total + square[:, k * 128 : (k + 1) * 128]
    summed[...] += total

    @pl.when(step == pl.num_programs(0) - 1)
    def _():
        ones = jnp.ones((8, 128), F32)
        squares[...] = lax.dot_general(
            ones, summed[...], (((1,), (1,)), ((), ())), precision=HIGHEST, preferred_element_type=F32
        )


def gate_output(running, c_in, local, gate, states):
    span, channels = local.shape
    heads = running.shape[1]
    n = c_in.shape[1]
    width = min(512, channels)
    return pl.pallas_call(
        functools.partial(gate_kernel, heads),
        grid=(channels // width,),
        out_shape=(
            jax.ShapeDtypeStruct((span, channels), F32),
            jax.ShapeDtypeStruct((8, span), F32),
        ),
        in_specs=[
            pl.BlockSpec((span, heads), lambda i: (0, 0)),
            pl.BlockSpec((span, n), lambda i: (0, 0)),
            pl.BlockSpec((span, width), lambda i: (0, i)),
            pl.BlockSpec((span, width), lambda i: (0, i)),
        ]
        + [ANY] * 4,
        out_specs=(
            pl.BlockSpec((span, width), lambda i: (0, i)),
            pl.BlockSpec((8, span), lambda i: (0, 0)),
        ),
        scratch_shapes=[
            pltpu.VMEM((n, channels), BF16),
            pltpu.VMEM((span, 3 * heads), BF16),
            pltpu.VMEM((span, 128), F32),
            pltpu.SemaphoreType.DMA,
        ],
        compiler_params=params(),
        cost_estimate=cost(2 * span * channels * n, span * channels * 10, span * channels),
        name="gate",
    )(running, c_in, local, gate, *states)


def norm_kernel(all_channels, new_len, gated, gain, *rest):
    sums, out = rest[:-1], rest[-1]
    span = gated.shape[0]
    total = sums[0][...]
    for part in sums[1:]:
        total = total + part[...]
    scale = lax.rsqrt(total / all_channels + EPSILON).T[:, :1]
    position = lax.axis_index("seq") * span + lax.broadcasted_iota(jnp.int32, (span, 1), 0)
    scale = jnp.where(position < new_len[0], scale, 0.0)
    out[...] = (gated[...] * scale * gain[...]).astype(BF16)


def norm_output(new_len, gated, gain, sums, all_channels):
    span, channels = gated.shape
    width = min(512, channels)
    return pl.pallas_call(
        functools.partial(norm_kernel, all_channels),
        grid=(channels // width,),
        out_shape=jax.ShapeDtypeStruct((span, channels), BF16),
        in_specs=[
            SMEM,
            pl.BlockSpec((span, width), lambda i: (0, i)),
            pl.BlockSpec((1, width), lambda i: (0, i)),
        ]
        + [pl.BlockSpec((8, span), lambda i: (0, 0))] * len(sums),
        out_specs=pl.BlockSpec((span, width), lambda i: (0, i)),
        compiler_params=params(),
        cost_estimate=cost(span * channels * 3, span * channels * 6),
        name="norm",
    )(new_len, gated, gain, *sums)


def attention_kernel(
    kv_head, new_len, cached, place, q, own_k, own_v, near, far_a, far_b, pool, received, out,
    cache_k, cache_v, acc, top, sems,
):
    span = q.shape[0]
    groups = q.shape[1] // HD
    entries = place.shape[1]
    rows_each = pool.shape[2]
    seq = lax.axis_index("seq")
    scale = HD ** (-0.5)
    lanes = pl.ds(kv_head * HD, HD)
    for e in range(entries):
        slot, taken = place[0, e], place[1, e]
        rows = pl.ds(e * rows_each, rows_each)
        for which, target in ((0, cache_k), (1, cache_v)):

            @pl.when(taken < 0)
            def _():
                pltpu.make_async_copy(
                    pool.at[slot, which, :, lanes], target.at[rows], sems.at[which, e]
                ).start()

            @pl.when(taken >= 0)
            def _():
                pltpu.make_async_copy(
                    received.at[taken, which, :, lanes], target.at[rows], sems.at[which, e]
                ).start()

    bq = 128
    blocks = span // bq

    def widened(v):
        return jnp.concatenate([v, jnp.ones_like(v)], axis=1)

    lower = lax.broadcasted_iota(jnp.int32, (bq, bq), 0) >= lax.broadcasted_iota(
        jnp.int32, (bq, bq), 1
    )
    for g in range(groups):
        for i in range(blocks):
            here = slice(i * bq, (i + 1) * bq)
            s = mm_nt(q[here, g * HD : (g + 1) * HD], own_k[: (i + 1) * bq, :]) * scale
            tail = jnp.where(lower, s[:, i * bq :], NEGATIVE)
            s = tail if i == 0 else jnp.concatenate([s[:, : i * bq], tail], axis=1)
            high = jnp.max(s, axis=1, keepdims=True)
            p = jnp.exp(s - high).astype(BF16)
            at = slice(g * span + i * bq, g * span + (i + 1) * bq)
            acc[at] = mm(p, widened(own_v[: (i + 1) * bq, :]))
            top[at] = jnp.broadcast_to(high, (bq, HD))

    def absorb(keys, values, mask=None):
        values = widened(values)
        for g in range(groups):
            for i in range(blocks):
                here = slice(i * bq, (i + 1) * bq)
                at = slice(g * span + i * bq, g * span + (i + 1) * bq)
                s = mm_nt(q[here, g * HD : (g + 1) * HD], keys) * scale
                if mask is not None:
                    s = jnp.where(mask, s, NEGATIVE)
                before = top[at]
                high = jnp.maximum(before[:, :1], jnp.max(s, axis=1, keepdims=True))
                p = jnp.exp(s - high).astype(BF16)
                shrink = jnp.exp(before - high)
                acc[at] = acc[at] * jnp.concatenate([shrink, shrink], axis=1) + mm(p, values)
                top[at] = jnp.broadcast_to(high, (bq, HD))

    @pl.when(seq % 2 == 1)
    def _():
        absorb(near[0], near[1])

    for e in range(entries):
        for which, target in ((0, cache_k), (1, cache_v)):
            rows = pl.ds(e * rows_each, rows_each)
            pltpu.make_async_copy(
                pool.at[0, which, :, lanes], target.at[rows], sems.at[which, e]
            ).wait()
    portion = min(entries, 4) * rows_each

    def cached_portion(k, unused):
        begin = k * portion
        rows = pl.ds(pl.multiple_of(begin, portion), portion)
        key = begin + lax.broadcasted_iota(jnp.int32, (bq, portion), 1)
        absorb(cache_k[rows, :], cache_v[rows, :], key < cached[0] * rows_each)
        return unused

    if entries * rows_each == portion:
        cached_portion(0, 0)
    else:
        lax.fori_loop(0, entries * rows_each // portion, cached_portion, 0)

    @pl.when(seq >= 2)
    def _():
        absorb(far_a[0], far_a[1])
        absorb(far_b[0], far_b[1])

    position = seq * span + lax.broadcasted_iota(jnp.int32, (span, 1), 0)
    valid = position < new_len[0]
    for g in range(groups):
        at = slice(g * span, (g + 1) * span)
        ratio = acc[at, :HD] / acc[at, HD:]
        out[:, g * HD : (g + 1) * HD] = jnp.where(valid, ratio, 0.0).astype(BF16)


def attention(kv_head, new_len, cached, place, q, keys, values, near, far_a, far_b, pool, received):
    span = q.shape[0]
    kv_heads = keys.shape[1] // HD
    width = q.shape[1] // kv_heads
    entries = place.shape[1]
    rows_each = pool.shape[2]
    groups = width // HD
    pick = pl.BlockSpec((span, HD), lambda i: (0, kv_head))
    pick2 = pl.BlockSpec((2, span, HD), lambda i: (0, 0, kv_head))
    return pl.pallas_call(
        functools.partial(attention_kernel, kv_head),
        grid=(1,),
        out_shape=jax.ShapeDtypeStruct((span, width), BF16),
        in_specs=[
            SMEM,
            SMEM,
            SMEM,
            pl.BlockSpec((span, width), lambda i: (0, kv_head)),
            pick,
            pick,
            pick2,
            pick2,
            pick2,
            ANY,
            ANY,
        ],
        out_specs=pl.BlockSpec((span, width), lambda i: (0, 0)),
        scratch_shapes=[
            pltpu.VMEM((entries * rows_each, HD), BF16),
            pltpu.VMEM((entries * rows_each, HD), BF16),
            pltpu.VMEM((groups * span, 2 * HD), F32),
            pltpu.VMEM((groups * span, HD), F32),
            pltpu.SemaphoreType.DMA((2, entries)),
        ],
        compiler_params=params(),
        cost_estimate=cost(
            4 * groups * span * 1792 * HD, span * width * 4 + 4 * span * HD * 4, groups * span * 1792
        ),
        name="attention",
    )(new_len, cached, place, q, keys, values, near, far_a, far_b, pool, received)


def per_device(
    xs, gate_z, b_in, c_in, log_decay, d_skip, norm_gain, queries, keys_new, values_new, kv_pool,
    state_pool, new_len, cached_blocks, kv_owner, kv_slot, state_owner, state_slot,
):
    total = lax.axis_size("batch")
    channels_all = xs.shape[2] * lax.axis_size("mp")
    xs, gate_z, b_in, c_in, decay = xs[0], gate_z[0], b_in[0], c_in[0], log_decay[0]
    queries, keys_new, values_new = queries[0], keys_new[0], values_new[0]

    fresh = jnp.stack([keys_new, values_new])
    far_a = lax.ppermute(fresh, "seq", [(0, 2), (1, 3)])
    near = lax.ppermute(fresh, "seq", [(0, 1), (2, 3)])

    ask, kv_place, st_place = make_requests(total, kv_owner, kv_slot, state_owner, state_slot)
    kv_received, st_received = [], []
    for shift in range(1, total):
        there = [(i, (i + shift) % total) for i in range(total)]
        back = [(j, i) for i, j in there]
        asked = lax.ppermute(ask[shift - 1 : shift], "batch", there)
        kv_found, st_found = look_up(asked, kv_pool, state_pool)
        st_received.append(lax.ppermute(st_found, "batch", back))
        kv_received.append(lax.ppermute(kv_found, "batch", back))
    if total > 2:
        kv_received = jnp.concatenate(kv_received, axis=0)
        st_received = jnp.concatenate(st_received, axis=0)
    else:
        kv_received, st_received = kv_received[0], st_received[0]

    end, through, running = end_state(new_len, decay, b_in, xs)
    local = local_scan(new_len, running, b_in, c_in, xs, d_skip[None])

    if state_pool.shape[2] % 16 == 0:
        start, state = start_state(st_place, state_pool, st_received, end, through)
    else:
        start = assembled_start(st_place, state_pool, st_received)
        state = advance(0, start, end, through)
    states = [start]
    far_b = lax.ppermute(far_a, "seq", [(2, 3), (3, 2)])
    states.append(lax.ppermute(state, "seq", [(0, 1)]))
    state = advance(1, states[1], end, through)
    states.append(lax.ppermute(state, "seq", [(1, 2)]))
    state = advance(2, states[2], end, through)
    states.append(lax.ppermute(state, "seq", [(2, 3)]))

    kv_heads = keys_new.shape[1] // HD
    attended = [
        attention(
            head, new_len, cached_blocks, kv_place, queries, keys_new, values_new, near, far_a,
            far_b, kv_pool, kv_received,
        )
        for head in range(kv_heads)
    ]

    gated, squares = gate_output(running, c_in, local, gate_z, states)
    sums = [squares]
    mp = lax.axis_size("mp")
    for shift in range(1, mp):
        sums.append(lax.ppermute(squares, "mp", [(i, (i + shift) % mp) for i in range(mp)]))
    ssm_out = norm_output(new_len, gated, norm_gain[None], sums, channels_all)
    return (ssm_out[None], jnp.concatenate(attended, axis=1)[None])


def solution(mesh):
    in_specs = (
        P("batch", "seq", "mp"),
        P("batch", "seq", "mp"),
        P("batch", "seq", None),
        P("batch", "seq", None),
        P("batch", "seq", "mp"),
        P("mp"),
        P("mp"),
        P("batch", "seq", "mp"),
        P("batch", "seq", "mp"),
        P("batch", "seq", "mp"),
        P("batch", None, None, "mp"),
        P("batch", "mp", None, None),
        P("batch"),
        P("batch"),
        P("batch", None, None),
        P("batch", None),
        P("batch", None, None),
        P("batch", None),
    )
    out_specs = (P("batch", "seq", "mp"), P("batch", "seq", "mp"))
    return jax.shard_map(
        per_device, mesh=mesh, in_specs=in_specs, out_specs=out_specs, check_vma=False
    )
```

time: 336 us -> 105 us (0.31)
  the two profiles are of different devices: /device:TPU:0 before, /device:TPU:3 now
where the time goes in v1:
time: 105 us
  Pallas kernels  59.5 us (57%)
  starting transfers between devices  22.6 us (22%)
  waiting for transfers between devices  12.8 us (12%)
  local copies, waits for them, and re-layouts  6.91 us (7%)
  between operations  2.32 us (2%)
    pallas_call x2, Pallas kernels, attention(): pl.pallas_call(functools.partial(attention_kernel, kv_head), grid=(1,), o...  22.2 us
    pallas_call x1, Pallas kernels, look_up(): pl.pallas_call(lookup_kernel, out_shape=(jax.ShapeDtypeStruct((CAP,) + kv...  19.7 us
    ppermute x1, starting transfers between devices, per_device(): far_b = lax.ppermute(far_a, 'seq', [(2, 3), (3, 2)])  8.53 us
    unnamed x38, local copies, waits for them, and re-layouts  6.89 us
    ppermute x1, waiting for transfers between devices, per_device(): far_a = lax.ppermute(fresh, 'seq', [(0, 2), (1, 3)])  6.4 us
    pallas_call x1, Pallas kernels, gate_output(): pl.pallas_call(functools.partial(gate_kernel, heads), grid=(channels // w...  5.72 us
    ppermute x3, starting transfers between devices, per_device(): lax.ppermute(squares, 'mp', [(i, (i + shift) % mp) for i in range(mp)])  4.73 us
    pallas_call x1, Pallas kernels, local_scan(): pl.pallas_call(functools.partial(local_scan_kernel, heads), grid=(channel...  4.62 us
  transfers between devices with their start and end apart: 12, of which 4 were waited for; matrix products, arithmetic and copies ran while one was open for 1% of the time, Pallas kernels for 28%

profile of v1, /device:TPU:3, one launch (start us, length us, event | category | flops | bytes accessed | tf_op | source)
XLA Modules:
  0.0 105.1 jit_solution(3695364502632479741)
XLA Ops:
  0.6 1.3 %copy.21.kv_owner = s32[1,4,1]{2,1,0:T(4,128)} copy(s32[1,4,1]{1,2,0:T(1,128)} %param.32) | data formatting | bytes 32 | tf_op args[14]
  1.9 1.3 %copy.22.st_owner = s32[1,4,1]{2,1,0:T(4,128)} copy(s32[1,4,1]{1,2,0:T(1,128)} %param.34) | data formatting | bytes 32 | tf_op args[16]
  3.3 1.6 %requests.1 = (s32[1,6]{1,0:T(1,128)}, s32[2,4]{1,0:T(2,128)}, s32[2,4]{1,0:T(2,128)}) custom-call(s32[1,4,1]{2,1,0:T(4,128)} %copy.21.kv_owner, s32[1,4]{1,0:T(1,128)} %kv_slot.1, s32[1,4,1]{2,1,0:T(4,128)} %copy.22.st_owner, s32[1,4]{1,0:T(1,128)} %st_slot.1), custom_call_target="tpu_custom_call" | custom-call | tf_op jit(solution)/shard_map/requests/pallas_call | solution.py:101
  4.8 0.0 copy-start.14
  4.8 0.0 copy-start.1
  4.8 0.0 copy-start.6
  4.9 1.3 %collective-permute-start = (s32[1,6]{1,0:T(1,128)}, s32[1,6]{1,0:T(1,128)S(1)}, u32[]{:S(2)}, u32[]{:S(2)}) collective-permute-start(s32[1,6]{1,0:T(1,128)} %get-tuple-element.16), channel_id=1, source_target_pairs={{0,4},{4,0},{1,5},{5,1},{2,6},{6,2},{3,7},{7,3},{8,12},{12,8},{9,1... | collective-permute-start | bytes 80 | tf_op jit(solution)/shard_map/ppermute | solution.py:629
  6.2 1.4 %collective-permute-done.asked = s32[1,6]{1,0:T(1,128)S(1)} collective-permute-done((s32[1,6]{1,0:T(1,128)}, s32[1,6]{1,0:T(1,128)S(1)}, u32[]{:S(2)}, u32[]{:S(2)}) %collective-permute-start) | collective-permute-done | bytes 56 | tf_op jit(solution)/shard_map/ppermute | solution.py:629
  7.5 0.5 copy-done.15
  8.1 19.7 %look_up.1 = (bf16[3,2,64,256]{3,2,1,0:T(8,128)(2,1)}, bf16[3,32,16,128]{3,2,1,0:T(8,128)(2,1)}) custom-call(s32[1,6]{1,0:T(1,128)} %copy-done.15, bf16[32,2,64,256]{3,2,1,0:T(8,128)(2,1)} %pool.5, bf16[64,32,16,128]{3,2,1,0:T(8,128)(2,1)} %pool.3), custom_call_target="tpu_custom_call" | custom-call | tf_op jit(solution)/shard_map/look_up/pallas_call | solution.py:127
  27.8 0.0 copy-start.10
  27.8 1.3 %collective-permute-start.1 = (bf16[3,32,16,128]{3,2,1,0:T(8,128)(2,1)}, bf16[3,32,16,128]{3,2,1,0:T(8,128)(2,1)S(1)}, u32[]{:S(2)}, u32[]{:S(2)}) collective-permute-start(bf16[3,32,16,128]{3,2,1,0:T(8,128)(2,1)} %get-tuple-element.17), channel_id=1, source_target_pairs={{4,0},{0,4},{5,1},{1,5},{6,2},{2,6},{7,3},{3,7},{12,8},{8,12},{13,... | collective-permute-start | bytes 1179656 | tf_op jit(solution)/shard_map/ppermute | solution.py:631
  29.7 0.0 copy-done.14
  29.7 0.1 copy.20
  29.9 0.0 copy-done.1
  29.9 0.0 copy-done.6
  29.9 2.5 %end_state.1 = (f32[128,2048]{1,0:T(8,128)S(1)}, f32[8,2048]{1,0:T(8,128)S(1)}, f32[384,32]{1,0:T(8,128)S(1)}) custom-call(s32[1]{0:T(128)S(6)} %copy.24.new_len, f32[384,32]{1,0:T(8,128)S(1)} %bitcast.16, bf16[384,128]{1,0:T(8,128)(2,1)S(1)} %bitcast.19, bf16[384,2048]{1,0:T(8,128)(2,1)S(1)} %bitcast.13), custom_call_target="tpu_custom_call" | custom-call | flops 201326592 | bytes 2621440 | tf_op jit(solution)/shard_map/end_state/pallas_call | solution.py:175
  32.4 4.5 %collective-permute-done.1.received = bf16[3,32,16,128]{3,2,1,0:T(8,128)(2,1)S(1)} collective-permute-done((bf16[3,32,16,128]{3,2,1,0:T(8,128)(2,1)}, bf16[3,32,16,128]{3,2,1,0:T(8,128)(2,1)S(1)}, u32[]{:S(2)}, u32[]{:S(2)}) %collective-permute-start.1) | collective-permute-done | bytes 393248 | tf_op jit(solution)/shard_map/ppermute | solution.py:631
  37.0 0.0 copy-done.10
  37.0 0.6 start_state.1
  37.6 0.7 collective-permute-start.2
  38.3 0.0 copy-done.7
  38.3 0.0 copy-done.8
  38.4 1.3 %collective-permute-start.9 = (bf16[2,384,256]{2,1,0:T(8,128)(2,1)S(1)}, bf16[2,384,256]{2,1,0:T(8,128)(2,1)S(1)}, u32[]{:S(2)}, u32[]{:S(2)}) collective-permute-start(bf16[2,384,256]{2,1,0:T(8,128)(2,1)S(1)} %constant_dynamic-update-slice_fusion), channel_id=1, source_target_pairs={{0,16},{8,24},{1,17},{9,25},{2,18},{10,26},{3,19},{11,27},{4,20},{... | collective-permute-start | bytes 1179656 | tf_op jit(solution)/shard_map/ppermute | solution.py:621
  39.7 0.0 collective-permute-done.2.state_in.rest_1_
  39.7 0.0 copy-start.16
  39.7 0.0 copy-start.5
  39.7 0.0 copy-start.11
  39.7 0.8 collective-permute-start.3
  40.6 1.3 %collective-permute-start.8 = (bf16[2,384,256]{2,1,0:T(8,128)(2,1)S(1)}, bf16[2,384,256]{2,1,0:T(8,128)(2,1)S(1)}, u32[]{:S(2)}, u32[]{:S(2)}) collective-permute-start(bf16[2,384,256]{2,1,0:T(8,128)(2,1)S(1)} %constant_dynamic-update-slice_fusion), channel_id=1, source_target_pairs={{0,8},{16,24},{1,9},{17,25},{2,10},{18,26},{3,11},{19,27},{4,12},{... | collective-permute-start | bytes 1179656 | tf_op jit(solution)/shard_map/ppermute | solution.py:622
  41.9 6.4 %collective-permute-done.9.far_a = bf16[2,384,256]{2,1,0:T(8,128)(2,1)S(1)} collective-permute-done((bf16[2,384,256]{2,1,0:T(8,128)(2,1)S(1)}, bf16[2,384,256]{2,1,0:T(8,128)(2,1)S(1)}, u32[]{:S(2)}, u32[]{:S(2)}) %collective-permute-start.9) | collective-permute-done | bytes 393248 | tf_op jit(solution)/shard_map/ppermute | solution.py:621
  48.3 8.5 %collective-permute-start.10 = (bf16[2,384,256]{2,1,0:T(8,128)(2,1)S(1)}, bf16[2,384,256]{2,1,0:T(8,128)(2,1)S(1)}, u32[]{:S(2)}, u32[]{:S(2)}) collective-permute-start(bf16[2,384,256]{2,1,0:T(8,128)(2,1)S(1)} %collective-permute-done.9.far_a), channel_id=1, source_target_pairs={{16,24},{24,16},{17,25},{25,17},{18,26},{26,18},{19,27},{27,19},{2... | collective-permute-start | bytes 1179656 | tf_op jit(solution)/shard_map/ppermute | solution.py:648
  56.8 0.0 collective-permute-done.3.state_in.rest_2_
  56.8 1.3 %collective-permute-start.4 = (bf16[128,2048]{1,0:T(8,128)(2,1)S(1)}, bf16[128,2048]{1,0:T(8,128)(2,1)S(1)}, u32[]{:S(2)}, u32[]{:S(2)}) collective-permute-start(bf16[128,2048]{1,0:T(8,128)(2,1)S(1)} %advance_state.3), channel_id=1, source_target_pairs={{16,24},{17,25},{18,26},{19,27},{20,28},{21,29},{22,30},{23,31}} | collective-permute-start | bytes 1572872 | tf_op jit(solution)/shard_map/ppermute | solution.py:653
  58.1 0.0 copy-done.16
  58.1 1.3 %collective-permute-start.11 = (bf16[3,2,64,256]{3,2,1,0:T(8,128)(2,1)S(1)}, bf16[3,2,64,256]{3,2,1,0:T(8,128)(2,1)S(1)}, u32[]{:S(2)}, u32[]{:S(2)}) collective-permute-start(bf16[3,2,64,256]{3,2,1,0:T(8,128)(2,1)S(1)} %copy-done.16), channel_id=1, source_target_pairs={{4,0},{0,4},{5,1},{1,5},{6,2},{2,6},{7,3},{3,7},{12,8},{8,12},{13,... | collective-permute-start | bytes 589832 | tf_op jit(solution)/shard_map/ppermute | solution.py:632
  60.1 0.0 copy-done.5
  60.1 0.0 copy-done.11
  60.1 0.0 copy-start.3
  60.1 0.0 copy-start.12
  60.1 0.0 copy-start.13
  60.2 4.6 %local_scan.1.local = f32[384,2048]{1,0:T(8,128)S(1)} custom-call(s32[1]{0:T(128)S(6)} %copy.24.new_len, f32[384,32]{1,0:T(8,128)S(1)} %get-tuple-element.14.running, bf16[384,128]{1,0:T(8,128)(2,1)S(1)} %bitcast.20, bf16[384,128]{1,0:T(8,128)(2,1)S(1)} %bitcast.17, bf16[384,2048]{1,0:T(8,128)(2,1)S(1)} %bitcast.14, f32[1,32]{1,0:T(1,128)S(1)} %bitcast.26), custom_call_target="tpu_custom_call" | custom-call | flops 603979776 | bytes 4718592 | tf_op jit(solution)/shard_map/local_scan/pallas_call | solution.py:259
  64.8 0.0 copy-start
  64.8 1.6 %copy-done = f32[384,2048]{1,0:T(8,128)} copy-done((f32[384,2048]{1,0:T(8,128)}, f32[384,2048]{1,0:T(8,128)S(1)}, u32[]{:S(2)}) %copy-start) | copy-done | bytes 3145752
  66.4 0.0 collective-permute-done.11.received
  66.4 0.0 collective-permute-done.8.near
  66.4 0.0 collective-permute-done.10.far_b
  66.4 0.0 copy-done.3
  66.5 11.2 %attention.2 = bf16[384,512]{1,0:T(8,128)(2,1)S(1)} custom-call(s32[1]{0:T(128)S(6)} %copy.24.new_len, s32[1]{0:T(128)S(6)} %copy.25.cached, s32[2,4]{1,0:T(2,128)S(1)} %copy-done.13, bf16[384,1024]{1,0:T(8,128)(2,1)S(1)} %bitcast.27, bf16[384,256]{1,0:T(8,128)(2,1)S(1)} %bitcast.21, bf16[384,256]{1,0:T(8,128)(2,1)S(1)} %bitcast.23, ...), custom_call_target="tpu_custom_call" | custom-call | flops 1409286144 | bytes 1572864 | tf_op jit(solution)/shard_map/attention/pallas_call | solution.py:578
  77.6 0.0 copy-start.4
  77.6 11.0 %attention.3 = bf16[384,512]{1,0:T(8,128)(2,1)S(1)} custom-call(s32[1]{0:T(128)S(6)} %copy.24.new_len, s32[1]{0:T(128)S(6)} %copy.25.cached, s32[2,4]{1,0:T(2,128)S(1)} %copy-done.13, bf16[384,1024]{1,0:T(8,128)(2,1)S(1)} %bitcast.28, bf16[384,256]{1,0:T(8,128)(2,1)S(1)} %bitcast.22, bf16[384,256]{1,0:T(8,128)(2,1)S(1)} %bitcast.24, ...), custom_call_target="tpu_custom_call" | custom-call | flops 1409286144 | bytes 1572864 | tf_op jit(solution)/shard_map/attention/pallas_call | solution.py:578
  88.7 0.0 collective-permute-done.4.rest_3_
  88.7 5.7 %gate.1 = (f32[384,2048]{1,0:T(8,128)}, f32[8,384]{1,0:T(8,128)S(1)}) custom-call(f32[384,32]{1,0:T(8,128)S(1)} %get-tuple-element.14.running, bf16[384,128]{1,0:T(8,128)(2,1)S(1)} %bitcast.18, f32[384,2048]{1,0:T(8,128)} %copy-done, bf16[384,2048]{1,0:T(8,128)(2,1)S(1)} %bitcast.15, bf16[128,2048]{1,0:T(8,128)(2,1)S(1)} %get-tuple-element.20.rest_0_, ...), custom_call_target="tpu_custom_call" | custom-call | flops 201326592 | bytes 7864320 | tf_op jit(solution)/shard_map/gate/pallas_call | solution.py:405
  94.4 0.0 copy-start.9
  94.4 1.4 %collective-permute-start.5 = (f32[8,384]{1,0:T(8,128)S(1)}, f32[8,384]{1,0:T(8,128)S(1)}, u32[]{:S(2)}, u32[]{:S(2)}) collective-permute-start(f32[8,384]{1,0:T(8,128)S(1)} %get-tuple-element.23.rest_0_), channel_id=1, source_target_pairs={{0,1},{1,2},{2,3},{3,0},{4,5},{5,6},{6,7},{7,4},{8,9},{9,10},{10,1... | collective-permute-start | bytes 36872 | tf_op jit(solution)/shard_map/ppermute | solution.py:668
  95.8 2.3 %collective-permute-start.6 = (f32[8,384]{1,0:T(8,128)S(1)}, f32[8,384]{1,0:T(8,128)S(1)}, u32[]{:S(2)}, u32[]{:S(2)}) collective-permute-start(f32[8,384]{1,0:T(8,128)S(1)} %get-tuple-element.23.rest_0_), channel_id=1, source_target_pairs={{0,2},{1,3},{2,0},{3,1},{4,6},{5,7},{6,4},{7,5},{8,10},{9,11},{10,... | collective-permute-start | bytes 36872 | tf_op jit(solution)/shard_map/ppermute | solution.py:668
  98.1 1.1 %collective-permute-start.7 = (f32[8,384]{1,0:T(8,128)S(1)}, f32[8,384]{1,0:T(8,128)S(1)}, u32[]{:S(2)}, u32[]{:S(2)}) collective-permute-start(f32[8,384]{1,0:T(8,128)S(1)} %get-tuple-element.23.rest_0_), channel_id=1, source_target_pairs={{0,3},{1,0},{2,1},{3,2},{4,7},{5,4},{6,5},{7,6},{8,11},{9,8},{10,9... | collective-permute-start | bytes 36872 | tf_op jit(solution)/shard_map/ppermute | solution.py:668
  99.2 1.0 maximum_bitcast_fusion
  100.1 0.0 collective-permute-done.5.rest_1_
  100.1 0.0 collective-permute-done.6.rest_2_
  100.1 0.5 collective-permute-done.7.rest_3_
  100.6 0.0 copy-done.9
  100.6 1.9 %copy-done.2 = f32[384,2048]{1,0:T(8,128)S(1)} copy-done((f32[384,2048]{1,0:T(8,128)S(1)}, f32[384,2048]{1,0:T(8,128)}, u32[]{:S(2)}) %copy-start.2) | copy-done | bytes 3145752
  102.5 2.5 %norm.1 = bf16[384,2048]{1,0:T(8,128)(2,1)} custom-call(s32[1]{0:T(128)S(6)} %copy.24.new_len, f32[384,2048]{1,0:T(8,128)S(1)} %copy-done.2, f32[1,2048]{1,0:T(1,128)S(1)} %bitcast.25, f32[8,384]{1,0:T(8,128)S(1)} %get-tuple-element.23.rest_0_, f32[8,384]{1,0:T(8,128)S(1)} %collective-permute-done.5.rest_1_, f32[8,384]{1,0:T(8,128)S(1)} %collective-permute-done.6.rest_2_, ...), custom_call_target="tpu_custom_call" | custom-call | flops 2359296 | bytes 4718592 | tf_op jit(solution)/shard_map/norm/pallas_call | solution.py:450
  (11 shorter events, 0.1 us)
Async XLA Ops:
  4.8 24.9 %copy-start.14 = (f32[1,384,32]{1,2,0:T(8,128)S(1)}, f32[1,384,32]{1,2,0:T(8,128)}, u32[]{:S(2)}) copy-start(f32[1,384,32]{1,2,0:T(8,128)} %param.22) | copy-start | bytes 147460
  4.8 25.0 %copy-start.1 = (bf16[1,384,2048]{2,1,0:T(8,128)(2,1)S(1)}, bf16[1,384,2048]{2,1,0:T(8,128)(2,1)}, u32[]{:S(2)}) copy-start(bf16[1,384,2048]{2,1,0:T(8,128)(2,1)} %param.18) | copy-start | bytes 4718596
  4.8 25.0 %copy-start.6 = (bf16[1,384,128]{2,1,0:T(8,128)(2,1)S(1)}, bf16[1,384,128]{2,1,0:T(8,128)(2,1)}, u32[]{:S(2)}) copy-start(bf16[1,384,128]{2,1,0:T(8,128)(2,1)} %param.20) | copy-start | bytes 294916
  4.9 2.7 %collective-permute-start = (s32[1,6]{1,0:T(1,128)}, s32[1,6]{1,0:T(1,128)S(1)}, u32[]{:S(2)}, u32[]{:S(2)}) collective-permute-start(s32[1,6]{1,0:T(1,128)} %get-tuple-element.16), channel_id=1, source_target_pairs={{0,4},{4,0},{1,5},{5,1},{2,6},{6,2},{3,7},{7,3},{8,12},{12,8},{9,1... | collective-permute-start | bytes 80 | tf_op jit(solution)/shard_map/ppermute | solution.py:629
  7.5 0.5 copy-start.15
  27.8 9.2 %copy-start.10 = (s32[2,4]{1,0:T(2,128)S(1)}, s32[2,4]{1,0:T(2,128)}, u32[]{:S(2)}) copy-start(s32[2,4]{1,0:T(2,128)} %get-tuple-element.15.place) | copy-start | bytes 100
  27.8 9.2 %collective-permute-start.1 = (bf16[3,32,16,128]{3,2,1,0:T(8,128)(2,1)}, bf16[3,32,16,128]{3,2,1,0:T(8,128)(2,1)S(1)}, u32[]{:S(2)}, u32[]{:S(2)}) collective-permute-start(bf16[3,32,16,128]{3,2,1,0:T(8,128)(2,1)} %get-tuple-element.17), channel_id=1, source_target_pairs={{4,0},{0,4},{5,1},{1,5},{6,2},{2,6},{7,3},{3,7},{12,8},{8,12},{13,... | collective-permute-start | bytes 1179656 | tf_op jit(solution)/shard_map/ppermute | solution.py:631
  37.0 1.3 %copy-start.7 = (bf16[1,384,256]{2,1,0:T(8,128)(2,1)S(1)}, bf16[1,384,256]{2,1,0:T(8,128)(2,1)}, u32[]{:S(2)}) copy-start(bf16[1,384,256]{2,1,0:T(8,128)(2,1)} %param.26) | copy-start | bytes 589828
  37.0 1.3 %copy-start.8 = (bf16[1,384,256]{2,1,0:T(8,128)(2,1)S(1)}, bf16[1,384,256]{2,1,0:T(8,128)(2,1)}, u32[]{:S(2)}) copy-start(bf16[1,384,256]{2,1,0:T(8,128)(2,1)} %param.27) | copy-start | bytes 589828
  37.6 2.1 %collective-permute-start.2 = (bf16[128,2048]{1,0:T(8,128)(2,1)S(1)}, bf16[128,2048]{1,0:T(8,128)(2,1)S(1)}, u32[]{:S(2)}, u32[]{:S(2)}) collective-permute-start(bf16[128,2048]{1,0:T(8,128)(2,1)S(1)} %get-tuple-element.21), channel_id=1, source_target_pairs={{0,8},{1,9},{2,10},{3,11},{4,12},{5,13},{6,14},{7,15}} | collective-permute-start | bytes 1572872 | tf_op jit(solution)/shard_map/ppermute | solution.py:649
  38.4 9.9 %collective-permute-start.9 = (bf16[2,384,256]{2,1,0:T(8,128)(2,1)S(1)}, bf16[2,384,256]{2,1,0:T(8,128)(2,1)S(1)}, u32[]{:S(2)}, u32[]{:S(2)}) collective-permute-start(bf16[2,384,256]{2,1,0:T(8,128)(2,1)S(1)} %constant_dynamic-update-slice_fusion), channel_id=1, source_target_pairs={{0,16},{8,24},{1,17},{9,25},{2,18},{10,26},{3,19},{11,27},{4,20},{... | collective-permute-start | bytes 1179656 | tf_op jit(solution)/shard_map/ppermute | solution.py:621
  39.7 18.4 %copy-start.16 = (bf16[3,2,64,256]{3,2,1,0:T(8,128)(2,1)S(1)}, bf16[3,2,64,256]{3,2,1,0:T(8,128)(2,1)}, u32[]{:S(2)}) copy-start(bf16[3,2,64,256]{3,2,1,0:T(8,128)(2,1)} %get-tuple-element.25) | copy-start | bytes 589828
  39.7 20.4 %copy-start.5 = (bf16[1,384,128]{2,1,0:T(8,128)(2,1)S(1)}, bf16[1,384,128]{2,1,0:T(8,128)(2,1)}, u32[]{:S(2)}) copy-start(bf16[1,384,128]{2,1,0:T(8,128)(2,1)} %param.21) | copy-start | bytes 294916
  39.7 20.4 %copy-start.11 = (f32[32]{0:T(128)S(1)}, f32[32]{0:T(128)}, u32[]{:S(2)}) copy-start(f32[32]{0:T(128)} %param.23) | copy-start | bytes 388
  39.7 17.1 %collective-permute-start.3 = (bf16[128,2048]{1,0:T(8,128)(2,1)S(1)}, bf16[128,2048]{1,0:T(8,128)(2,1)S(1)}, u32[]{:S(2)}, u32[]{:S(2)}) collective-permute-start(bf16[128,2048]{1,0:T(8,128)(2,1)S(1)} %advance_state.2), channel_id=1, source_target_pairs={{8,16},{9,17},{10,18},{11,19},{12,20},{13,21},{14,22},{15,23}} | collective-permute-start | bytes 1572872 | tf_op jit(solution)/shard_map/ppermute | solution.py:651
  40.6 25.9 %collective-permute-start.8 = (bf16[2,384,256]{2,1,0:T(8,128)(2,1)S(1)}, bf16[2,384,256]{2,1,0:T(8,128)(2,1)S(1)}, u32[]{:S(2)}, u32[]{:S(2)}) collective-permute-start(bf16[2,384,256]{2,1,0:T(8,128)(2,1)S(1)} %constant_dynamic-update-slice_fusion), channel_id=1, source_target_pairs={{0,8},{16,24},{1,9},{17,25},{2,10},{18,26},{3,11},{19,27},{4,12},{... | collective-permute-start | bytes 1179656 | tf_op jit(solution)/shard_map/ppermute | solution.py:622
  48.3 18.2 %collective-permute-start.10 = (bf16[2,384,256]{2,1,0:T(8,128)(2,1)S(1)}, bf16[2,384,256]{2,1,0:T(8,128)(2,1)S(1)}, u32[]{:S(2)}, u32[]{:S(2)}) collective-permute-start(bf16[2,384,256]{2,1,0:T(8,128)(2,1)S(1)} %collective-permute-done.9.far_a), channel_id=1, source_target_pairs={{16,24},{24,16},{17,25},{25,17},{18,26},{26,18},{19,27},{27,19},{2... | collective-permute-start | bytes 1179656 | tf_op jit(solution)/shard_map/ppermute | solution.py:648
  56.8 31.8 %collective-permute-start.4 = (bf16[128,2048]{1,0:T(8,128)(2,1)S(1)}, bf16[128,2048]{1,0:T(8,128)(2,1)S(1)}, u32[]{:S(2)}, u32[]{:S(2)}) collective-permute-start(bf16[128,2048]{1,0:T(8,128)(2,1)S(1)} %advance_state.3), channel_id=1, source_target_pairs={{16,24},{17,25},{18,26},{19,27},{20,28},{21,29},{22,30},{23,31}} | collective-permute-start | bytes 1572872 | tf_op jit(solution)/shard_map/ppermute | solution.py:653
  58.1 8.3 %collective-permute-start.11 = (bf16[3,2,64,256]{3,2,1,0:T(8,128)(2,1)S(1)}, bf16[3,2,64,256]{3,2,1,0:T(8,128)(2,1)S(1)}, u32[]{:S(2)}, u32[]{:S(2)}) collective-permute-start(bf16[3,2,64,256]{3,2,1,0:T(8,128)(2,1)S(1)} %copy-done.16), channel_id=1, source_target_pairs={{4,0},{0,4},{5,1},{1,5},{6,2},{2,6},{7,3},{3,7},{12,8},{8,12},{13,... | collective-permute-start | bytes 589832 | tf_op jit(solution)/shard_map/ppermute | solution.py:632
  60.1 6.3 %copy-start.3 = (bf16[32,2,64,256]{3,2,1,0:T(8,128)(2,1)S(1)}, bf16[32,2,64,256]{3,2,1,0:T(8,128)(2,1)}, u32[]{:S(2)}) copy-start(bf16[32,2,64,256]{3,2,1,0:T(8,128)(2,1)} %pool.5) | copy-start | bytes 6291460
  60.1 6.3 %copy-start.12 = (bf16[1,384,1024]{2,1,0:T(8,128)(2,1)S(1)}, bf16[1,384,1024]{2,1,0:T(8,128)(2,1)}, u32[]{:S(2)}) copy-start(bf16[1,384,1024]{2,1,0:T(8,128)(2,1)} %param.25) | copy-start | bytes 2359300
  60.1 6.3 %copy-start.13 = (s32[2,4]{1,0:T(2,128)S(1)}, s32[2,4]{1,0:T(2,128)}, u32[]{:S(2)}) copy-start(s32[2,4]{1,0:T(2,128)} %get-tuple-element.24.place) | copy-start | bytes 100
  64.8 1.6 %copy-start = (f32[384,2048]{1,0:T(8,128)}, f32[384,2048]{1,0:T(8,128)S(1)}, u32[]{:S(2)}) copy-start(f32[384,2048]{1,0:T(8,128)S(1)} %local_scan.1.local) | copy-start | bytes 9437188
  77.6 11.1 %copy-start.4 = (bf16[1,384,2048]{2,1,0:T(8,128)(2,1)S(1)}, bf16[1,384,2048]{2,1,0:T(8,128)(2,1)}, u32[]{:S(2)}) copy-start(bf16[1,384,2048]{2,1,0:T(8,128)(2,1)} %param.19) | copy-start | bytes 4718596
  94.4 6.2 %copy-start.9 = (f32[2048]{0:T(1024)S(1)}, f32[2048]{0:T(1024)}, u32[]{:S(2)}) copy-start(f32[2048]{0:T(1024)} %param.24) | copy-start | bytes 24580
  94.4 5.7 %collective-permute-start.5 = (f32[8,384]{1,0:T(8,128)S(1)}, f32[8,384]{1,0:T(8,128)S(1)}, u32[]{:S(2)}, u32[]{:S(2)}) collective-permute-start(f32[8,384]{1,0:T(8,128)S(1)} %get-tuple-element.23.rest_0_), channel_id=1, source_target_pairs={{0,1},{1,2},{2,3},{3,0},{4,5},{5,6},{6,7},{7,4},{8,9},{9,10},{10,1... | collective-permute-start | bytes 36872 | tf_op jit(solution)/shard_map/ppermute | solution.py:668
  95.8 4.4 %collective-permute-start.6 = (f32[8,384]{1,0:T(8,128)S(1)}, f32[8,384]{1,0:T(8,128)S(1)}, u32[]{:S(2)}, u32[]{:S(2)}) collective-permute-start(f32[8,384]{1,0:T(8,128)S(1)} %get-tuple-element.23.rest_0_), channel_id=1, source_target_pairs={{0,2},{1,3},{2,0},{3,1},{4,6},{5,7},{6,4},{7,5},{8,10},{9,11},{10,... | collective-permute-start | bytes 36872 | tf_op jit(solution)/shard_map/ppermute | solution.py:668
  98.1 2.5 %collective-permute-start.7 = (f32[8,384]{1,0:T(8,128)S(1)}, f32[8,384]{1,0:T(8,128)S(1)}, u32[]{:S(2)}, u32[]{:S(2)}) collective-permute-start(f32[8,384]{1,0:T(8,128)S(1)} %get-tuple-element.23.rest_0_), channel_id=1, source_target_pairs={{0,3},{1,0},{2,1},{3,2},{4,7},{5,4},{6,5},{7,6},{8,11},{9,8},{10,9... | collective-permute-start | bytes 36872 | tf_op jit(solution)/shard_map/ppermute | solution.py:668
  100.6 1.9 %copy-start.2 = (f32[384,2048]{1,0:T(8,128)S(1)}, f32[384,2048]{1,0:T(8,128)}, u32[]{:S(2)}) copy-start(f32[384,2048]{1,0:T(8,128)} %get-tuple-element.22.gated) | copy-start | bytes 9437188

commit v2 on v0

v2 whole, which is shorter than its diff:
```python
import functools

import jax
import jax.numpy as jnp
from jax import lax
from jax.experimental import pallas as pl
from jax.experimental.pallas import tpu as pltpu
from jax.sharding import PartitionSpec as P

P_SIZE = 64
HD = 128
CAP = 3
BQ = 128
EPSILON = 1e-05
NEGATIVE = -1e30
LOG2E = 1.4426950408889634
HIGHEST = lax.Precision.HIGHEST
F32 = jnp.float32
BF16 = jnp.bfloat16

SMEM = pl.BlockSpec(memory_space=pltpu.SMEM)
ANY = pl.BlockSpec(memory_space=pl.ANY)
VMEM = pl.BlockSpec(memory_space=pltpu.VMEM)
HBM = pl.BlockSpec(memory_space=pltpu.HBM)


def call(kernel, name, out, ins, outs, scratch=(), mib=16, aliases=None, after=()):
    count = len(ins)

    def body(*refs):
        kernel(*refs[:count], *refs[count + len(after) :])

    run = pl.pallas_call(
        body,
        out_shape=out,
        in_specs=list(ins) + [ANY] * len(after),
        out_specs=outs,
        scratch_shapes=list(scratch),
        input_output_aliases=aliases or {},
        compiler_params=pltpu.CompilerParams(vmem_limit_bytes=mib * 1024 * 1024),
        cost_estimate=pl.CostEstimate(flops=10**10, bytes_accessed=10**7, transcendentals=0),
        name=name,
    )
    return lambda *operands: run(*operands, *after)


def struct(*shape, dtype=F32):
    return jax.ShapeDtypeStruct(shape, dtype)


def mm(a, b):
    return jnp.dot(a, b, preferred_element_type=F32)


def mm_nt(a, b):
    return lax.dot_general(a, b, (((1,), (1,)), ((), ())), preferred_element_type=F32)


def split(value, terms, axis=1):
    parts = []
    rest = value
    for term in range(terms):
        part = rest.astype(BF16)
        parts.append(part)
        if term + 1 < terms:
            rest = rest - part.astype(F32)
    return jnp.concatenate(parts, axis=axis)


def spread_matrix(heads, terms, first_head, width):
    row = lax.broadcasted_iota(jnp.int32, (heads, width), 0)
    lane = lax.broadcasted_iota(jnp.int32, (heads, width), 1)
    one = jnp.where(row == (lane >> 6) + first_head, 1.0, 0.0).astype(BF16)
    return jnp.concatenate([one] * terms, axis=0)


def valid_rows(new_len, span):
    position = lax.axis_index("seq") * span + lax.broadcasted_iota(jnp.int32, (span, 1), 0)
    return position < new_len[0]


def slots_of(lists, base, count, owner):
    found, seen = [jnp.int32(0)] * CAP, jnp.int32(0)
    for e in range(count):
        match = lists[base + e] == owner
        slot = lists[base + count + e]
        found = [jnp.where(match & (seen == k), slot, at) for k, at in enumerate(found)]
        seen = seen + match.astype(jnp.int32)
    return found


def place_of(lists, base, count, e, total):
    owner = lists[base + e]
    shift = owner - lax.axis_index("batch")
    shift = jnp.where(shift < 0, shift + total, shift)
    rank = lax.fori_loop(
        0, e, lambda f, n: n + (lists[base + f] == owner).astype(jnp.int32), jnp.int32(0)
    )
    mine = shift == 0
    taken = (shift - 1) * CAP + jnp.minimum(rank, CAP - 1)
    return mine, jnp.where(mine, 0, taken)


def lookup_kernel(entries, pieces, asked, lists, kv_pool, st_pool, *outs):
    me = lax.axis_index("batch")
    for k, slot in enumerate(slots_of(asked, 0, entries, me)):
        outs[0][k] = kv_pool[slot]
    for k, slot in enumerate(slots_of(asked, 2 * entries, pieces, me)):
        outs[1][k] = st_pool[slot]
    if len(outs) > 2:
        for e in range(entries):
            outs[2][e] = kv_pool[lists[entries + e]]
        for e in range(pieces):
            outs[3][e] = st_pool[lists[2 * entries + pieces + e]]


def look_up(asked, lists, entries, pieces, kv_pool, st_pool, own, after):
    kv, st = kv_pool.shape[1:], st_pool.shape[1:]
    out = [struct(CAP, *kv, dtype=BF16), struct(CAP, *st, dtype=BF16)]
    if own:
        out += [struct(entries, *kv, dtype=BF16), struct(pieces, *st, dtype=BF16)]
    return call(
        functools.partial(lookup_kernel, entries, pieces),
        "look_up",
        tuple(out),
        [SMEM, SMEM, VMEM, VMEM],
        (VMEM,) * len(out),
        after=after,
    )(asked, lists, kv_pool, st_pool)


def zeros_kernel(out):
    out[...] = jnp.zeros_like(out)


def zeros(count):
    return call(zeros_kernel, "zeros", struct(1, count, dtype=jnp.int32), [], VMEM)()[0]


def laid_kernel(count, *refs):
    out = refs[count]
    begin = 0
    for ref in refs[:count]:
        if len(ref.shape) == 2:
            out[begin] = ref[...]
            begin += 1
        else:
            out[begin : begin + ref.shape[0]] = ref[...]
            begin += ref.shape[0]


def laid_together(parts, after):
    rows = sum(part.shape[0] if part.ndim == 3 else 1 for part in parts)
    return call(
        functools.partial(laid_kernel, len(parts)),
        "laid_together",
        struct(rows, *parts[0].shape[-2:], dtype=BF16),
        [VMEM] * len(parts),
        VMEM,
        after=after,
    )(*parts)


def end_state_kernel(new_len, decay_t, b_in, xs, sent, end, through, running, running_t):
    span, channels = xs.shape
    heads = decay_t.shape[0]
    n = b_in.shape[1]
    lane = lax.axis_index("seq") * span + lax.broadcasted_iota(jnp.int32, (1, span), 1)
    dec = jnp.where(lane < new_len[0], decay_t[...], 0.0)
    row = lax.broadcasted_iota(jnp.int32, (span, span), 0)
    col = lax.broadcasted_iota(jnp.int32, (span, span), 1)
    upper = jnp.where(row <= col, 1.0, 0.0).astype(BF16)
    r3 = mm(split(dec, 3, 0), upper)
    r_t = r3[:heads] + r3[heads : 2 * heads] + r3[2 * heads :]
    running_t[...] = r_t
    r = r_t.T
    running[...] = r
    last = r[span - 1 :, :]
    remain = split(jnp.exp(last - r), 2)
    lasting = split(jnp.broadcast_to(jnp.exp(last), (8, heads)), 3)
    b_t = jnp.where(valid_rows(new_len, span), b_in[...].astype(F32), 0.0).T.astype(BF16)
    width = min(512, channels)
    for begin in range(0, channels, width):
        lanes = slice(begin, begin + width)
        spread = spread_matrix(heads, 3, begin // P_SIZE, width)
        factor = mm(remain, spread[: 2 * heads])
        weighted = (xs[:, lanes].astype(F32) * factor).astype(BF16)
        state = mm(b_t, weighted)
        end[:, lanes] = state
        sent[:n, lanes] = state.astype(BF16)
        whole = mm(lasting, spread)
        through[:, lanes] = whole
        sent[n:, lanes] = jnp.concatenate(
            [split(whole[:1], 3, 0), jnp.zeros((13, width), BF16)], axis=0
        )


def end_state(new_len, decay_t, b_in, xs, after):
    span, channels = xs.shape
    heads = decay_t.shape[0]
    n = b_in.shape[1]
    return call(
        end_state_kernel,
        "end_state",
        (
            struct(n + 16, channels, dtype=BF16),
            struct(n, channels),
            struct(8, channels),
            struct(span, heads),
            struct(heads, span),
        ),
        [SMEM, VMEM, VMEM, VMEM],
        (VMEM,) * 5,
        after=after,
    )(new_len, decay_t, b_in, xs)


def local_scan_kernel(
    begin, new_len, running, running_t, b_in, c_in, xs, d_skip, out, cols, inter, skips
):
    span, channels = xs.shape
    heads = running.shape[1]
    here_channels = out.shape[1]
    width = min(512, here_channels)
    group = width // P_SIZE
    blocks = span // BQ
    r = running[...]
    for g in range(here_channels // width):
        first = begin // P_SIZE + g * group
        cols[g] = r[:, first : first + group]
    b = jnp.where(valid_rows(new_len, span), b_in[...].astype(F32), 0.0).astype(BF16)
    inter[...] = mm_nt(c_in[...], b)
    spread = spread_matrix(heads, 3, begin // P_SIZE, here_channels)
    skips[...] = mm(split(jnp.broadcast_to(d_skip[...], (8, heads)), 3), spread)
    lower = lax.broadcasted_iota(jnp.int32, (BQ, BQ), 0) >= lax.broadcasted_iota(
        jnp.int32, (BQ, BQ), 1
    )
    left = lax.broadcasted_iota(jnp.int32, (span, 2 * P_SIZE), 1) < P_SIZE

    def heads_of(step, unused):
        col = cols[step]
        row = running_t[pl.ds(pl.multiple_of(begin // P_SIZE + step * group, group), group), :]
        for pair in range(group // 2):
            offset = step * width + pair * 2 * P_SIZE
            lanes = pl.ds(pl.multiple_of(offset, 2 * P_SIZE), 2 * P_SIZE)
            x_pair = xs[:, pl.ds(pl.multiple_of(begin + offset, 2 * P_SIZE), 2 * P_SIZE)]
            zero = jnp.zeros_like(x_pair)
            sides = (jnp.where(left, x_pair, zero), jnp.where(left, zero, x_pair))
            for i in range(blocks):
                here = slice(i * BQ, (i + 1) * BQ)
                lhs, rhs = [], []
                for side in range(2):
                    h = pair * 2 + side
                    at_t = jnp.broadcast_to(col[here, h : h + 1], (BQ, BQ))
                    for j in range(i + 1):
                        there = slice(j * BQ, (j + 1) * BQ)
                        gap = at_t - row[h : h + 1, there]
                        if j == i:
                            gap = jnp.where(lower, gap, NEGATIVE)
                        lhs.append((jnp.exp(gap) * inter[here, there]).astype(BF16))
                        rhs.append(sides[side][there])
                y = mm(jnp.concatenate(lhs, axis=1), jnp.concatenate(rhs, axis=0))
                out[here, lanes] = y + skips[:1, lanes] * x_pair[here].astype(F32)
        return unused

    lax.fori_loop(0, here_channels // width, heads_of, 0)


def local_scan(begin, size, operands, after):
    span = operands[-2].shape[0]
    width = min(512, size)
    return call(
        functools.partial(local_scan_kernel, begin),
        "local_scan",
        struct(span, size),
        [SMEM] + [VMEM] * 6,
        VMEM,
        [
            pltpu.VMEM((size // width, span, width // P_SIZE), F32),
            pltpu.VMEM((span, span), F32),
            pltpu.VMEM((8, size), F32),
        ],
        after=after,
    )(*operands)


def kept_factors(sent, n, lanes=slice(None)):
    return jnp.sum(sent[n : n + 16, lanes].astype(F32), axis=0, keepdims=True)


def middle_kernel(received, end, through, sent):
    seq = lax.axis_index("seq")
    n, channels = end.shape
    half = channels // 2

    def combine(lanes, early_e, early_t, late_e, late_t):
        sent[:n, :] = (late_t * early_e[:n, lanes].astype(F32) + late_e[:n, lanes]).astype(BF16)
        rest = jnp.zeros((13, half), BF16)
        sent[n:, :] = jnp.concatenate([split(late_t * early_t, 3, 0), rest], axis=0)

    @pl.when(seq == 0)
    def _():
        lanes = slice(0, half)
        combine(lanes, end, through[:1, lanes], received, kept_factors(received, n, lanes))

    @pl.when(seq == 1)
    def _():
        lanes = slice(half, channels)
        combine(lanes, received, kept_factors(received, n, lanes), end, through[:1, lanes])


def middle_state(received, end, through, after):
    return call(
        middle_kernel,
        "middle_state",
        struct(received.shape[0], received.shape[1] // 2, dtype=BF16),
        [VMEM] * 3,
        VMEM,
        after=after,
    )(received, end, through)


def cached_kernel(base, total, lists, kept_in, taken_in, out):
    pieces, heads = kept_in.shape[:2]
    places = [place_of(lists, base, pieces, j, total) for j in range(pieces)]
    for h in range(0, heads, 2):
        parts = [
            jnp.where(mine, kept_in[j, h + k], taken_in[taken, h + k])
            for k in range(2)
            for j, (mine, taken) in enumerate(places)
        ]
        lanes = slice(h * P_SIZE, (h + 2) * P_SIZE)
        out[:, lanes] = jnp.concatenate(parts, axis=0).astype(F32).T.astype(BF16)


def cached_state(lists, base, total, kept, received, after):
    pieces, heads, rows, n = kept.shape
    channels = heads * pieces * rows
    if rows % 16 == 0:
        return call(
            functools.partial(cached_kernel, base, total),
            "cached_state",
            struct(n, channels, dtype=BF16),
            [SMEM, VMEM, VMEM],
            VMEM,
            after=after,
        )(lists, kept, received)
    owners = lists[base : base + pieces]
    shift = (owners - lax.axis_index("batch")) % total
    order = jnp.arange(pieces)
    same = (owners[:, None] == owners[None, :]) & (order[:, None] > order[None, :])
    rank = jnp.minimum(jnp.sum(same.astype(jnp.int32), axis=1), CAP - 1)
    mine = shift == 0
    taken = received[jnp.where(mine, 0, (shift - 1) * CAP + rank)]
    found = jnp.where(mine[:, None, None, None], kept, taken)
    return jnp.transpose(found, (3, 1, 0, 2)).reshape(n, channels)


def gate_kernel(count, running, c_in, gate, cached, met, middle, swapped, *rest):
    locals_in, (gated, squares) = rest[:count], rest[count:]
    span, channels = gate.shape
    heads = running.shape[1]
    n = c_in.shape[1]
    width = 256
    seq = lax.axis_index("seq")
    far, odd = seq >= 2, seq % 2 == 1

    def entering(begin):
        state = cached[:, begin : begin + width].astype(F32)
        side, at = divmod(begin, channels // 2)
        lanes = slice(at, at + width)
        part = jnp.where(odd == (side == 1), middle[:, lanes], swapped[:, lanes])
        kept = jnp.where(far, kept_factors(part, n), 1.0)
        state = kept * state + jnp.where(far, part[:n].astype(F32), 0.0)
        lanes = slice(begin, begin + width)
        kept = jnp.where(odd, kept_factors(met, n, lanes), 1.0)
        state = kept * state + jnp.where(odd, met[:n, lanes].astype(F32), 0.0)
        return state.astype(BF16)

    factors = split(jnp.exp(running[...]), 2)
    c = c_in[...]
    total = jnp.zeros((span, 128), F32)
    begin = 0
    for local in locals_in:
        for at in range(0, local.shape[1], width):
            lanes = slice(begin + at, begin + at + width)
            factor = mm(factors, spread_matrix(heads, 2, (begin + at) // P_SIZE, width))
            carried = mm(c, entering(begin + at))
            z = gate[:, lanes].astype(F32)
            value = (local[:, at : at + width] + factor * carried) * (z / (1.0 + jnp.exp(-z)))
            gated[:, lanes] = value.astype(BF16)
            square = value * value
            for k in range(width // 128):
                total = total + square[:, k * 128 : (k + 1) * 128]
        begin += local.shape[1]
    ones = jnp.ones((8, 128), F32)
    squares[...] = lax.dot_general(
        ones, total, (((1,), (1,)), ((), ())), precision=HIGHEST, preferred_element_type=F32
    )


def gate_output(running, c_in, gate, cached, met, middle, swapped, local):
    span, channels = gate.shape
    return call(
        functools.partial(gate_kernel, len(local)),
        "gate",
        (struct(span, channels, dtype=BF16), struct(8, span)),
        [VMEM] * (7 + len(local)),
        (VMEM, VMEM),
    )(running, c_in, gate, cached, met, middle, swapped, *local)


def norm_kernel(all_channels, count, new_len, gated, gain, *rest):
    sums, (out, staged, sems) = rest[:count], rest[count:]
    span, channels = gated.shape
    width = min(512, channels)
    total = sums[0][...]
    for part in sums[1:]:
        total = total + part[...]
    scale = lax.rsqrt(total / all_channels + EPSILON).T[:, :1]
    scale = jnp.where(valid_rows(new_len, span), scale, 0.0)
    copies = []
    for k, begin in enumerate(range(0, channels, width)):
        lanes = slice(begin, begin + width)
        staged[:, lanes] = (gated[:, lanes].astype(F32) * scale * gain[:, lanes]).astype(BF16)
        at = pl.ds(begin, width)
        copies.append(pltpu.make_async_copy(staged.at[:, at], out.at[:, at], sems.at[k]))
        copies[-1].start()
    for copy in copies:
        copy.wait()


def norm_output(new_len, gated, gain, sums, all_channels, after):
    span, channels = gated.shape
    return call(
        functools.partial(norm_kernel, all_channels, len(sums)),
        "norm",
        struct(span, channels, dtype=BF16),
        [SMEM] + [VMEM] * (2 + len(sums)),
        HBM,
        [
            pltpu.VMEM((span, channels), BF16),
            pltpu.SemaphoreType.DMA((channels // min(512, channels),)),
        ],
        after=after,
    )(new_len, gated, gain, *sums)


def attention_kernel(
    kv_head, heads, groups, total, new_len, cached, lists, q, own_k, own_v, far, near, kept,
    received, *rest
):
    out, token, keys, values, scores, weights, staged, sems = rest[-8:]
    span = own_k.shape[0]
    entries, rows_each = kept.shape[0], kept.shape[2]
    seq = lax.axis_index("seq")
    lanes = slice(kv_head * HD, (kv_head + 1) * HD)
    cached_len = entries * rows_each
    few = 2 * span + cached_len
    factor = HD ** (-0.5) * LOG2E
    token[...] = jnp.zeros_like(token)

    def put(begin, key_rows, value_rows):
        rows = slice(begin, begin + key_rows.shape[0])
        keys[rows] = key_rows
        values[rows, :HD] = value_rows
        values[rows, HD:] = jnp.ones_like(value_rows)

    put(0, own_k[:, lanes], own_v[:, lanes])
    put(span + cached_len, near[0, :, lanes], near[1, :, lanes])
    for e in range(entries):
        mine, taken = place_of(lists, 0, entries, e, total)
        record = [jnp.where(mine, kept[e, k, :, lanes], received[taken, k, :, lanes]) for k in (0, 1)]
        put(span + e * rows_each, *record)
    key = lax.broadcasted_iota(jnp.int32, (1, few - span), 1)
    open_keys = (key < cached[0] * rows_each) | ((key >= cached_len) & (seq % 2 == 1))
    bias = jnp.where(open_keys, 0.0, NEGATIVE)
    valid = valid_rows(new_len, span)

    def copy_out(k):
        at = pl.ds((kv_head * groups + heads[k]) * HD, HD)
        return pltpu.make_async_copy(staged.at[:, pl.ds(k * HD, HD)], out.at[:, at], sems.at[k])

    def attend(count):
        for k, g in enumerate(heads):
            slot = k % 2
            head = slice((kv_head * groups + g) * HD, (kv_head * groups + g + 1) * HD)
            scores[slot, :, :count] = mm_nt(q[:, head], keys[:count])
            for begin in range(0, span, BQ):
                rows = slice(begin, begin + BQ)
                s = scores[slot, rows, :count]
                at = lax.broadcasted_iota(jnp.int32, (BQ, span), 0) + begin
                past = at >= lax.broadcasted_iota(jnp.int32, (BQ, span), 1)
                parts = [jnp.where(past, s[:, :span], NEGATIVE), s[:, span:few] + bias]
                if count > few:
                    parts.append(s[:, few:])
                s = jnp.concatenate(parts, axis=1)
                high = jnp.max(s, axis=1, keepdims=True)
                weights[slot, rows, :count] = jnp.exp2(s * factor - high * factor).astype(BF16)
            summed = mm(weights[slot, :, :count], values[:count])
            ratio = summed[:, :HD] / summed[:, HD:]
            staged[:, k * HD : (k + 1) * HD] = jnp.where(valid, ratio, 0.0).astype(BF16)
            copy_out(k).start()

    @pl.when(seq < 2)
    def _():
        attend(few)

    @pl.when(seq >= 2)
    def _():
        put(few, far[0, :, lanes], far[1, :, lanes])
        put(few + span, near[2, :, lanes], near[3, :, lanes])
        attend(few + 2 * span)

    for k in range(len(heads)):
        copy_out(k).wait()


def attention(
    kv_head, heads, total, new_len, cached, lists, q, keys, values, far, near, kept,
    received, out, after,
):
    span = q.shape[0]
    groups = q.shape[1] // keys.shape[1]
    most = 4 * span + kept.shape[0] * kept.shape[2]
    operands = (new_len, cached, lists, q, keys, values, far, near, kept, received)
    ins = [SMEM] * 3 + [VMEM] * 7
    aliases = {}
    if out is not None:
        aliases = {len(operands): 0}
        operands += (out,)
        ins += [HBM]
    return call(
        functools.partial(attention_kernel, kv_head, heads, groups, total),
        "attention",
        (struct(*q.shape, dtype=BF16), struct(8, 128)),
        ins,
        (HBM, VMEM),
        [
            pltpu.VMEM((most, HD), BF16),
            pltpu.VMEM((most, 2 * HD), BF16),
            pltpu.VMEM((2, span, most), F32),
            pltpu.VMEM((2, span, most), BF16),
            pltpu.VMEM((span, len(heads) * HD), BF16),
            pltpu.SemaphoreType.DMA((len(heads),)),
        ],
        mib=14 + most * span * 12 // 2**20,
        aliases=aliases,
        after=after,
    )(*operands)


def per_device(
    xs, gate_z, b_in, c_in, log_decay, d_skip, norm_gain, queries, keys_new, values_new, kv_pool,
    state_pool, new_len, cached_blocks, kv_owner, kv_slot, state_owner, state_slot,
):
    total = lax.axis_size("batch")
    mp = lax.axis_size("mp")
    channels_all = xs.shape[2] * mp
    entries, pieces = kv_slot.shape[1], state_slot.shape[1]
    xs, gate_z, b_in, c_in, decay = xs[0], gate_z[0], b_in[0], c_in[0], log_decay[0]
    queries, keys_new, values_new = queries[0], keys_new[0], values_new[0]

    beside = [(0, 1), (1, 0), (2, 3), (3, 2)]
    across = [(0, 2), (1, 3)]

    lists = jnp.concatenate(
        [kv_owner.reshape(-1), kv_slot.reshape(-1), state_owner.reshape(-1), state_slot.reshape(-1)]
    )
    lists = lists + zeros(lists.shape[0])
    fresh = laid_together([keys_new, values_new], (lists,))
    far = lax.ppermute(fresh, "seq", across)
    sent, end, through, running, running_t = end_state(new_len, decay.T, b_in, xs, (fresh,))
    met = lax.ppermute(sent, "seq", beside)

    scan_operands = (new_len, running, running_t, b_in, c_in, xs, d_skip[None])
    half = xs.shape[1] // 2
    kv_received, st_received, kept = [], [], None
    for shift in range(1, total):
        there = [(i, (i + shift) % total) for i in range(total)]
        back = [(j, i) for i, j in there]
        asked = lax.ppermute(lists, "batch", there)
        found = look_up(
            asked, lists, entries, pieces, kv_pool, state_pool, kept is None, (sent,)
        )
        if kept is None:
            kept = found[2:]
        kv_received.append(lax.ppermute(found[0], "batch", back))
        st_received.append(lax.ppermute(found[1], "batch", back))
    if total > 2:
        kv_received = jnp.concatenate(kv_received, axis=0)
        st_received = jnp.concatenate(st_received, axis=0)
    else:
        kv_received, st_received = kv_received[0], st_received[0]
    kv_kept, st_kept = kept

    sent = middle_state(met, end, through, (kv_kept,))
    middle = lax.ppermute(sent, "seq", across)
    both = laid_together([fresh, far], (sent,))
    near = lax.ppermute(both, "seq", beside)

    groups = queries.shape[1] // keys_new.shape[1]
    kv_heads = keys_new.shape[1] // HD

    def attend(kv_head, out, after):
        return attention(
            kv_head, tuple(range(groups)), total, new_len, cached_blocks, lists, queries, keys_new,
            values_new, far, near, kv_kept, kv_received, out, after,
        )

    local = [local_scan(0, half, scan_operands, (both,))]
    local.append(local_scan(half, half // 2, scan_operands, (local[0],)))
    out, token = None, local[1]
    for kv_head in range(kv_heads - 1):
        out, token = attend(kv_head, out, (token,))
    held = laid_together([middle], (token,))
    swapped = lax.ppermute(held, "seq", beside)[0]
    local.append(local_scan(half + half // 2, half // 2, scan_operands, (held,)))
    cached = cached_state(lists, 2 * entries, total, st_kept, st_received, (local[2],))
    gated, squares = gate_output(running, c_in, gate_z, cached, met, middle, swapped, local)
    sums = [squares]
    for shift in range(1, mp):
        sums.append(lax.ppermute(squares, "mp", [(i, (i + shift) % mp) for i in range(mp)]))
    attended, token = attend(kv_heads - 1, out, (squares,))
    ssm_out = norm_output(new_len, gated, norm_gain[None], sums, channels_all, (token,))
    return (ssm_out[None], attended[None])


def solution(mesh):
    in_specs = (
        P("batch", "seq", "mp"),
        P("batch", "seq", "mp"),
        P("batch", "seq", None),
        P("batch", "seq", None),
        P("batch", "seq", "mp"),
        P("mp"),
        P("mp"),
        P("batch", "seq", "mp"),
        P("batch", "seq", "mp"),
        P("batch", "seq", "mp"),
        P("batch", None, None, "mp"),
        P("batch", "mp", None, None),
        P("batch"),
        P("batch"),
        P("batch", None, None),
        P("batch", None),
        P("batch", None, None),
        P("batch", None),
    )
    out_specs = (P("batch", "seq", "mp"), P("batch", "seq", "mp"))
    return jax.shard_map(
        per_device, mesh=mesh, in_specs=in_specs, out_specs=out_specs, check_vma=False
    )
```

time: 336 us -> 44.1 us (0.13)
  the two profiles are of different devices: /device:TPU:0 before, /device:TPU:10 now
where the time goes in v2:
time: 44.1 us; the launch traced here: 43.9 us
  Pallas kernels  23.3 us (53%)
  starting transfers between devices  12.8 us (29%)
  waiting for transfers between devices  3.58 us (8%)
  between operations  2.6 us (6%)
  local copies, waits for them, and re-layouts  1.6 us (4%)
    pallas_call x15, Pallas kernels, call(): return lambda *operands: run(*operands, *after)  23.3 us
    ppermute x3, starting transfers between devices, per_device(): lax.ppermute(squares, 'mp', [(i, (i + shift) % mp) for i in range(mp)])  5.54 us
    ppermute x1, waiting for transfers between devices, per_device(): far = lax.ppermute(fresh, 'seq', across)  3.55 us
    unnamed x34, local copies, waits for them, and re-layouts  1.6 us
    ppermute x1, starting transfers between devices, per_device(): far = lax.ppermute(fresh, 'seq', across)  1.56 us
    ppermute x1, starting transfers between devices, per_device(): asked = lax.ppermute(lists, 'batch', there)  1.52 us
    ppermute x1, starting transfers between devices, per_device(): st_received.append(lax.ppermute(found[1], 'batch', back))  1.52 us
    ppermute x1, starting transfers between devices, per_device(): middle = lax.ppermute(sent, 'seq', across)  1.42 us
  transfers between devices with their start and end apart: 11, of which 1 were waited for; matrix products, arithmetic and copies ran while one was open for 0% of the time, Pallas kernels for 44%

profile of v2, /device:TPU:10, one launch (start us, length us, event | category | flops | bytes accessed | tf_op | source)
XLA Modules:
  0.0 43.9 jit_solution(16614725054185178334)
XLA Ops:
  0.6 0.0 copy-start.11
  0.6 0.0 copy-start.12
  0.7 0.0 copy-start.13
  0.7 0.0 copy-start.14
  0.7 0.0 copy-start.5
  0.7 0.0 copy-start.4
  0.7 0.6 %copy-done.11 = s32[1,4]{1,0:T(1,128)S(1)} copy-done((s32[1,4]{1,0:T(1,128)S(1)}, s32[1,4]{1,0:T(1,128)}, u32[]{:S(2)}) %copy-start.11) | copy-done | bytes 40
  1.3 0.0 copy-done.12
  1.3 0.0 copy-done.13
  1.3 0.0 copy-done.14
  1.3 0.1 add_add_fusion.refs_2_.refs_1_.refs_0_
  1.4 1.5 %collective-permute-start = (s32[16]{0:T(128)S(1)}, s32[16]{0:T(128)S(1)}, u32[]{:S(2)}, u32[]{:S(2)}) collective-permute-start(s32[16]{0:T(128)S(1)} %add_add_fusion.refs_2_.refs_1_.refs_0_), channel_id=1, source_target_pairs={{0,4},{4,0},{1,5},{5,1},{2,6},{6,2},{3,7},{7,3},{8,12},{12,8},{9,1... | collective-permute-start | bytes 200 | tf_op jit(solution)/shard_map/ppermute | solution.py:582
  2.9 0.0 copy-done.5
  2.9 0.0 copy-done.4
  2.9 0.0 copy-start.1
  2.9 0.0 copy-start.8
  3.0 0.0 slice-start
  3.0 1.6 %collective-permute-start.4 = (bf16[2,384,256]{2,1,0:T(8,128)(2,1)S(1)}, bf16[2,384,256]{2,1,0:T(8,128)(2,1)S(1)}, u32[]{:S(2)}, u32[]{:S(2)}) collective-permute-start(bf16[2,384,256]{2,1,0:T(8,128)(2,1)S(1)} %laid_together.3.refs_4_.refs_0_), channel_id=1, source_target_pairs={{0,16},{8,24},{1,17},{9,25},{2,18},{10,26},{3,19},{11,27},{4,20},{... | collective-permute-start | bytes 1179656 | tf_op jit(solution)/shard_map/ppermute | solution.py:572
  5.3 0.0 slice-start.1
  5.3 0.0 copy-done.1
  5.4 0.0 copy-done.6
  5.4 0.0 copy-done.8
  5.4 0.0 copy-start
  5.4 1.6 %end_state.1 = (bf16[144,2048]{1,0:T(8,128)(2,1)S(1)}, f32[128,2048]{1,0:T(8,128)S(1)}, f32[8,2048]{1,0:T(8,128)S(1)}, f32[384,32]{1,0:T(8,128)S(1)}, f32[32,384]{1,0:T(8,128)S(1)}) custom-call(s32[1]{0:T(128)S(6)} %copy.22.refs_0_, f32[32,384]{1,0:T(8,128)S(1)} %bitcast.45, bf16[384,128]{1,0:T(8,128)(2,1)S(1)} %bitcast.37, bf16[384,2048]{1,0:T(8,128)(2,1)S(1)} %bitcast.23, ...), custom_call_target="tpu_custom_call" | custom-call | flops 10000000000 | bytes 10000000 | tf_op jit(solution)/shard_map/end_state/pallas_call | solution.py:44
  7.0 0.1 collective-permute-start.2
  7.8 0.0 collective-permute-done.refs_0_
  7.8 0.0 slice-done
  7.8 0.0 slice-done.1
  7.8 0.4 copy-done
  8.2 0.7 %look_up.1 = (bf16[3,2,64,256]{3,2,1,0:T(8,128)(2,1)S(1)}, bf16[3,32,16,128]{3,2,1,0:T(8,128)(2,1)S(1)}, bf16[4,2,64,256]{3,2,1,0:T(8,128)(2,1)S(1)}, bf16[4,32,16,128]{3,2,1,0:T(8,128)(2,1)S(1)}) custom-call(s32[16]{0:T(128)S(1)} %collective-permute-done.refs_0_, s32[16]{0:T(128)S(1)} %add_add_fusion.refs_2_.refs_1_.refs_0_, ...), custom_call_target="tpu_custom_call" | custom-call | flops 10000000000 | bytes 10000000 | tf_op jit(solution)/shard_map/look_up/pallas_call | solution.py:44
  8.9 0.6 %collective-permute-start.6 = (bf16[3,2,64,256]{3,2,1,0:T(8,128)(2,1)S(1)}, bf16[3,2,64,256]{3,2,1,0:T(8,128)(2,1)S(1)}, u32[]{:S(2)}, u32[]{:S(2)}) collective-permute-start(bf16[3,2,64,256]{3,2,1,0:T(8,128)(2,1)S(1)} %get-tuple-element.25), channel_id=1, source_target_pairs={{4,0},{0,4},{5,1},{1,5},{6,2},{2,6},{7,3},{3,7},{12,8},{8,12},{13,... | collective-permute-start | bytes 589832 | tf_op jit(solution)/shard_map/ppermute | solution.py:588
  9.4 1.5 %collective-permute-start.1 = (bf16[3,32,16,128]{3,2,1,0:T(8,128)(2,1)S(1)}, bf16[3,32,16,128]{3,2,1,0:T(8,128)(2,1)S(1)}, u32[]{:S(2)}, u32[]{:S(2)}) collective-permute-start(bf16[3,32,16,128]{3,2,1,0:T(8,128)(2,1)S(1)} %get-tuple-element.20), channel_id=1, source_target_pairs={{4,0},{0,4},{5,1},{1,5},{6,2},{2,6},{7,3},{3,7},{12,8},{8,12},{13,... | collective-permute-start | bytes 1179656 | tf_op jit(solution)/shard_map/ppermute | solution.py:589
  10.9 0.0 collective-permute-done.2.refs_0_.refs_4_
  11.0 1.4 %collective-permute-start.3 = (bf16[144,1024]{1,0:T(8,128)(2,1)S(1)}, bf16[144,1024]{1,0:T(8,128)(2,1)S(1)}, u32[]{:S(2)}, u32[]{:S(2)}) collective-permute-start(bf16[144,1024]{1,0:T(8,128)(2,1)S(1)} %middle_state.1.refs_2_), channel_id=1, source_target_pairs={{0,16},{8,24},{1,17},{9,25},{2,18},{10,26},{3,19},{11,27},{4,20},{... | collective-permute-start | bytes 884744 | tf_op jit(solution)/shard_map/ppermute | solution.py:598
  12.4 3.5 %collective-permute-done.4.refs_1_.refs_6_ = bf16[2,384,256]{2,1,0:T(8,128)(2,1)S(1)} collective-permute-done((bf16[2,384,256]{2,1,0:T(8,128)(2,1)S(1)}, bf16[2,384,256]{2,1,0:T(8,128)(2,1)S(1)}, u32[]{:S(2)}, u32[]{:S(2)}) %collective-permute-start.4) | collective-permute-done | bytes 393248 | tf_op jit(solution)/shard_map/ppermute | solution.py:572
  15.9 0.1 laid_together.4.refs_7_
  16.0 0.1 collective-permute-start.5
  16.1 0.0 copy-done.7
  16.1 0.0 copy-done.10
  16.1 2.3 %local_scan.3.refs_7_ = f32[384,1024]{1,0:T(8,128)S(1)} custom-call(s32[1]{0:T(128)S(6)} %copy.22.refs_0_, f32[384,32]{1,0:T(8,128)S(1)} %get-tuple-element.17.refs_1_.refs_0_, f32[32,384]{1,0:T(8,128)S(1)} %get-tuple-element.21.refs_2_, bf16[384,128]{1,0:T(8,128)(2,1)S(1)} %bitcast.38, bf16[384,128]{1,0:T(8,128)(2,1)S(1)} %bitcast.41, ...), custom_call_target="tpu_custom_call" | custom-call | flops 10000000000 | bytes 10000000 | tf_op jit(solution)/shard_map/local_scan/pallas_call | solution.py:44
  18.4 0.0 copy-start.3
  18.4 1.1 %local_scan.4.refs_10_.refs_8_ = f32[384,512]{1,0:T(8,128)S(1)} custom-call(s32[1]{0:T(128)S(6)} %copy.22.refs_0_, f32[384,32]{1,0:T(8,128)S(1)} %get-tuple-element.17.refs_1_.refs_0_, f32[32,384]{1,0:T(8,128)S(1)} %get-tuple-element.21.refs_2_, bf16[384,128]{1,0:T(8,128)(2,1)S(1)} %bitcast.39, bf16[384,128]{1,0:T(8,128)(2,1)S(1)} %bitcast.42, ...), custom_call_target="tpu_custom_call" | custom-call | flops 10000000000 | bytes 10000000 | tf_op jit(solution)/shard_map/local_scan/pallas_call | solution.py:44
  19.6 0.0 collective-permute-done.6.refs_9_
  19.6 0.0 collective-permute-done.5.refs_7_
  19.6 0.0 copy-done.3
  19.6 5.7 %attention.2 = (bf16[384,1024]{1,0:T(8,128)(2,1)}, f32[8,128]{1,0:T(8,128)S(1)}) custom-call(s32[1]{0:T(128)S(6)} %copy.22.refs_0_, s32[1]{0:T(128)S(6)} %copy.23.refs_1_, s32[16]{0:T(128)S(1)} %add_add_fusion.refs_2_.refs_1_.refs_0_, bf16[384,1024]{1,0:T(8,128)(2,1)S(1)} %bitcast.28, bf16[384,256]{1,0:T(8,128)(2,1)S(1)} %bitcast.32, ...), custom_call_target="tpu_custom_call" | custom-call | flops 10000000000 | bytes 10000000 | tf_op jit(solution)/shard_map/attention/pallas_call | solution.py:44
  25.3 0.0 collective-permute-done.3.refs_0_.refs_5_
  25.4 0.5 %collective-permute-start.7 = (bf16[1,144,1024]{2,1,0:T(8,128)(2,1)S(1)}, bf16[1,144,1024]{2,1,0:T(8,128)(2,1)S(1)}, u32[]{:S(2)}, u32[]{:S(2)}) collective-permute-start(bf16[1,144,1024]{2,1,0:T(8,128)(2,1)S(1)} %laid_together.5.refs_7_), channel_id=1, source_target_pairs={{0,8},{8,0},{16,24},{24,16},{1,9},{9,1},{17,25},{25,17},{2,10},{10... | collective-permute-start | bytes 884744 | tf_op jit(solution)/shard_map/ppermute | solution.py:617
  25.9 1.1 %local_scan.5.refs_3_.refs_9_ = f32[384,512]{1,0:T(8,128)S(1)} custom-call(s32[1]{0:T(128)S(6)} %copy.22.refs_0_, f32[384,32]{1,0:T(8,128)S(1)} %get-tuple-element.17.refs_1_.refs_0_, f32[32,384]{1,0:T(8,128)S(1)} %get-tuple-element.21.refs_2_, bf16[384,128]{1,0:T(8,128)(2,1)S(1)} %bitcast.40, bf16[384,128]{1,0:T(8,128)(2,1)S(1)} %bitcast.43, ...), custom_call_target="tpu_custom_call" | custom-call | flops 10000000000 | bytes 10000000 | tf_op jit(solution)/shard_map/local_scan/pallas_call | solution.py:44
  27.0 0.0 collective-permute-done.1.refs_2_
  27.1 0.0 copy-start.2
  27.1 0.8 %cached_state.1.refs_3_ = bf16[128,2048]{1,0:T(8,128)(2,1)S(1)} custom-call(s32[16]{0:T(128)S(1)} %add_add_fusion.refs_2_.refs_1_.refs_0_, bf16[4,32,16,128]{3,2,1,0:T(8,128)(2,1)S(1)} %get-tuple-element.19.refs_1_, bf16[3,32,16,128]{3,2,1,0:T(8,128)(2,1)S(1)} %collective-permute-done.1.refs_2_, f32[384,512]{1,0:T(8,128)S(1)} %local_scan.5.refs_3_.refs_9_), custom_call_target="tpu_custom_call" | custom-call | flops 10000000000 | bytes 10000000 | tf_op jit(solution)/shard_map/cached_state/pallas_call | solution.py:44
  27.9 0.0 collective-permute-done.7
  27.9 0.5 %copy-done.2 = bf16[1,384,2048]{2,1,0:T(8,128)(2,1)S(1)} copy-done((bf16[1,384,2048]{2,1,0:T(8,128)(2,1)S(1)}, bf16[1,384,2048]{2,1,0:T(8,128)(2,1)}, u32[]{:S(2)}) %copy-start.2) | copy-done | bytes 1572888
  28.5 2.3 %gate.1 = (bf16[384,2048]{1,0:T(8,128)(2,1)S(1)}, f32[8,384]{1,0:T(8,128)S(1)}) custom-call(f32[384,32]{1,0:T(8,128)S(1)} %get-tuple-element.17.refs_1_.refs_0_, bf16[384,128]{1,0:T(8,128)(2,1)S(1)} %bitcast.44, bf16[384,2048]{1,0:T(8,128)(2,1)S(1)} %bitcast.27, bf16[128,2048]{1,0:T(8,128)(2,1)S(1)} %cached_state.1.refs_3_, ...), custom_call_target="tpu_custom_call" | custom-call | flops 10000000000 | bytes 10000000 | tf_op jit(solution)/shard_map/gate/pallas_call | solution.py:44
  30.8 0.5 %collective-permute-start.10 = (f32[8,384]{1,0:T(8,128)S(1)}, f32[8,384]{1,0:T(8,128)S(1)}, u32[]{:S(2)}, u32[]{:S(2)}) collective-permute-start(f32[8,384]{1,0:T(8,128)S(1)} %get-tuple-element.28.refs_11_.refs_3_), channel_id=1, source_target_pairs={{0,3},{1,0},{2,1},{3,2},{4,7},{5,4},{6,5},{7,6},{8,11},{9,8},{10,9... | collective-permute-start | bytes 36872 | tf_op jit(solution)/shard_map/ppermute | solution.py:623
  31.2 2.6 %collective-permute-start.9 = (f32[8,384]{1,0:T(8,128)S(1)}, f32[8,384]{1,0:T(8,128)S(1)}, u32[]{:S(2)}, u32[]{:S(2)}) collective-permute-start(f32[8,384]{1,0:T(8,128)S(1)} %get-tuple-element.28.refs_11_.refs_3_), channel_id=1, source_target_pairs={{0,2},{1,3},{2,0},{3,1},{4,6},{5,7},{6,4},{7,5},{8,10},{9,11},{10,... | collective-permute-start | bytes 36872 | tf_op jit(solution)/shard_map/ppermute | solution.py:623
  33.8 2.5 %collective-permute-start.8 = (f32[8,384]{1,0:T(8,128)S(1)}, f32[8,384]{1,0:T(8,128)S(1)}, u32[]{:S(2)}, u32[]{:S(2)}) collective-permute-start(f32[8,384]{1,0:T(8,128)S(1)} %get-tuple-element.28.refs_11_.refs_3_), channel_id=1, source_target_pairs={{0,1},{1,2},{2,3},{3,0},{4,5},{5,6},{6,7},{7,4},{8,9},{9,10},{10,1... | collective-permute-start | bytes 36872 | tf_op jit(solution)/shard_map/ppermute | solution.py:623
  36.3 5.7 %attention.3 = (bf16[384,1024]{1,0:T(8,128)(2,1)}, f32[8,128]{1,0:T(8,128)S(1)}) custom-call(s32[1]{0:T(128)S(6)} %copy.22.refs_0_, s32[1]{0:T(128)S(6)} %copy.23.refs_1_, s32[16]{0:T(128)S(1)} %add_add_fusion.refs_2_.refs_1_.refs_0_, bf16[384,1024]{1,0:T(8,128)(2,1)S(1)} %bitcast.29, ...), custom_call_target="tpu_custom_call", output_to_operand_aliasing={{0}: (10, {})} | custom-call | flops 10000000000 | bytes 10000000 | tf_op jit(solution)/shard_map/attention/pallas_call | solution.py:44
  42.0 0.0 collective-permute-done.10.refs_6_
  42.0 0.0 collective-permute-done.9.refs_5_
  42.0 0.0 collective-permute-done.8.refs_4_
  42.1 0.0 copy-done.9
  42.1 1.7 %norm.1 = bf16[384,2048]{1,0:T(8,128)(2,1)} custom-call(s32[1]{0:T(128)S(6)} %copy.22.refs_0_, bf16[384,2048]{1,0:T(8,128)(2,1)S(1)} %get-tuple-element.27.refs_1_, f32[1,2048]{1,0:T(1,128)S(1)} %bitcast.46, f32[8,384]{1,0:T(8,128)S(1)} %get-tuple-element.28.refs_11_.refs_3_, f32[8,384]{1,0:T(8,128)S(1)} %collective-permute-done.8.refs_4_, ...), custom_call_target="tpu_custom_call" | custom-call | flops 10000000000 | bytes 10000000 | tf_op jit(solution)/shard_map/norm/pallas_call | solution.py:44
  (9 shorter events, 0.1 us)
Async XLA Ops:
  0.6 0.7 %copy-start.11 = (s32[1,4]{1,0:T(1,128)S(1)}, s32[1,4]{1,0:T(1,128)}, u32[]{:S(2)}) copy-start(s32[1,4]{1,0:T(1,128)} %param.35) | copy-start | bytes 52
  0.6 0.7 %copy-start.12 = (s32[1,4,1]{1,2,0:T(1,128)S(1)}, s32[1,4,1]{1,2,0:T(1,128)}, u32[]{:S(2)}) copy-start(s32[1,4,1]{1,2,0:T(1,128)} %param.34) | copy-start | bytes 52
  0.7 0.7 %copy-start.13 = (s32[1,4]{1,0:T(1,128)S(1)}, s32[1,4]{1,0:T(1,128)}, u32[]{:S(2)}) copy-start(s32[1,4]{1,0:T(1,128)} %param.33) | copy-start | bytes 52
  0.7 0.7 %copy-start.14 = (s32[1,4,1]{1,2,0:T(1,128)S(1)}, s32[1,4,1]{1,2,0:T(1,128)}, u32[]{:S(2)}) copy-start(s32[1,4,1]{1,2,0:T(1,128)} %param.32) | copy-start | bytes 52
  0.7 2.3 %copy-start.5 = (bf16[1,384,256]{2,1,0:T(8,128)(2,1)S(1)}, bf16[1,384,256]{2,1,0:T(8,128)(2,1)}, u32[]{:S(2)}) copy-start(bf16[1,384,256]{2,1,0:T(8,128)(2,1)} %param.27) | copy-start | bytes 589828
  0.7 2.3 %copy-start.4 = (bf16[1,384,256]{2,1,0:T(8,128)(2,1)S(1)}, bf16[1,384,256]{2,1,0:T(8,128)(2,1)}, u32[]{:S(2)}) copy-start(bf16[1,384,256]{2,1,0:T(8,128)(2,1)} %param.26) | copy-start | bytes 589828
  1.4 6.4 %collective-permute-start = (s32[16]{0:T(128)S(1)}, s32[16]{0:T(128)S(1)}, u32[]{:S(2)}, u32[]{:S(2)}) collective-permute-start(s32[16]{0:T(128)S(1)} %add_add_fusion.refs_2_.refs_1_.refs_0_), channel_id=1, source_target_pairs={{0,4},{4,0},{1,5},{5,1},{2,6},{6,2},{3,7},{7,3},{8,12},{12,8},{9,1... | collective-permute-start | bytes 200 | tf_op jit(solution)/shard_map/ppermute | solution.py:582
  2.9 2.4 %copy-start.1 = (bf16[1,384,2048]{2,1,0:T(8,128)(2,1)S(1)}, bf16[1,384,2048]{2,1,0:T(8,128)(2,1)}, u32[]{:S(2)}) copy-start(bf16[1,384,2048]{2,1,0:T(8,128)(2,1)} %param.18) | copy-start | bytes 4718596
  2.9 2.4 %copy-start.6 = (bf16[1,384,128]{2,1,0:T(8,128)(2,1)S(1)}, bf16[1,384,128]{2,1,0:T(8,128)(2,1)}, u32[]{:S(2)}) copy-start(bf16[1,384,128]{2,1,0:T(8,128)(2,1)} %param.20) | copy-start | bytes 294916
  2.9 2.4 %copy-start.8 = (f32[1,384,32]{1,2,0:T(8,128)S(1)}, f32[1,384,32]{1,2,0:T(8,128)}, u32[]{:S(2)}) copy-start(f32[1,384,32]{1,2,0:T(8,128)} %param.22) | copy-start | bytes 147460
  3.0 4.8 %slice-start = ((s8[8388608]{0:T(1024)(128)(4,1)}), s8[4194304]{0:T(1024)(128)(4,1)S(1)}, s32[]{:S(2)}) async-start(s8[8388608]{0:T(1024)(128)(4,1)} %bitcast.21), calls=%async_computation | async-start | bytes 8388608
  3.0 12.9 %collective-permute-start.4 = (bf16[2,384,256]{2,1,0:T(8,128)(2,1)S(1)}, bf16[2,384,256]{2,1,0:T(8,128)(2,1)S(1)}, u32[]{:S(2)}, u32[]{:S(2)}) collective-permute-start(bf16[2,384,256]{2,1,0:T(8,128)(2,1)S(1)} %laid_together.3.refs_4_.refs_0_), channel_id=1, source_target_pairs={{0,16},{8,24},{1,17},{9,25},{2,18},{10,26},{3,19},{11,27},{4,20},{... | collective-permute-start | bytes 1179656 | tf_op jit(solution)/shard_map/ppermute | solution.py:572
  5.3 2.5 %slice-start.1 = ((s8[8388608]{0:T(1024)(128)(4,1)}), s8[4194304]{0:T(1024)(128)(4,1)S(1)}, s32[]{:S(2)}) async-start(s8[8388608]{0:T(1024)(128)(4,1)} %bitcast.21), calls=%async_computation.1 | async-start | bytes 8388608
  5.4 2.8 %copy-start = (bf16[32,2,64,256]{3,2,1,0:T(8,128)(2,1)S(1)}, bf16[32,2,64,256]{3,2,1,0:T(8,128)(2,1)}, u32[]{:S(2)}) copy-start(bf16[32,2,64,256]{3,2,1,0:T(8,128)(2,1)} %refs_2_.1) | copy-start | bytes 6291460
  7.0 3.9 %collective-permute-start.2 = (bf16[144,2048]{1,0:T(8,128)(2,1)S(1)}, bf16[144,2048]{1,0:T(8,128)(2,1)S(1)}, u32[]{:S(2)}, u32[]{:S(2)}) collective-permute-start(bf16[144,2048]{1,0:T(8,128)(2,1)S(1)} %get-tuple-element.18.refs_4_), channel_id=1, source_target_pairs={{0,8},{8,0},{16,24},{24,16},{1,9},{9,1},{17,25},{25,17},{2,10},{10... | collective-permute-start | bytes 1769480 | tf_op jit(solution)/shard_map/ppermute | solution.py:574
  8.9 10.7 %collective-permute-start.6 = (bf16[3,2,64,256]{3,2,1,0:T(8,128)(2,1)S(1)}, bf16[3,2,64,256]{3,2,1,0:T(8,128)(2,1)S(1)}, u32[]{:S(2)}, u32[]{:S(2)}) collective-permute-start(bf16[3,2,64,256]{3,2,1,0:T(8,128)(2,1)S(1)} %get-tuple-element.25), channel_id=1, source_target_pairs={{4,0},{0,4},{5,1},{1,5},{6,2},{2,6},{7,3},{3,7},{12,8},{8,12},{13,... | collective-permute-start | bytes 589832 | tf_op jit(solution)/shard_map/ppermute | solution.py:588
  9.4 17.6 %collective-permute-start.1 = (bf16[3,32,16,128]{3,2,1,0:T(8,128)(2,1)S(1)}, bf16[3,32,16,128]{3,2,1,0:T(8,128)(2,1)S(1)}, u32[]{:S(2)}, u32[]{:S(2)}) collective-permute-start(bf16[3,32,16,128]{3,2,1,0:T(8,128)(2,1)S(1)} %get-tuple-element.20), channel_id=1, source_target_pairs={{4,0},{0,4},{5,1},{1,5},{6,2},{2,6},{7,3},{3,7},{12,8},{8,12},{13,... | collective-permute-start | bytes 1179656 | tf_op jit(solution)/shard_map/ppermute | solution.py:589
  11.0 5.1 %copy-start.7 = (bf16[1,384,128]{2,1,0:T(8,128)(2,1)S(1)}, bf16[1,384,128]{2,1,0:T(8,128)(2,1)}, u32[]{:S(2)}) copy-start(bf16[1,384,128]{2,1,0:T(8,128)(2,1)} %param.21) | copy-start | bytes 294916
  11.0 5.1 %copy-start.10 = (f32[32]{0:T(128)S(1)}, f32[32]{0:T(128)}, u32[]{:S(2)}) copy-start(f32[32]{0:T(128)} %param.23) | copy-start | bytes 388
  11.0 14.4 %collective-permute-start.3 = (bf16[144,1024]{1,0:T(8,128)(2,1)S(1)}, bf16[144,1024]{1,0:T(8,128)(2,1)S(1)}, u32[]{:S(2)}, u32[]{:S(2)}) collective-permute-start(bf16[144,1024]{1,0:T(8,128)(2,1)S(1)} %middle_state.1.refs_2_), channel_id=1, source_target_pairs={{0,16},{8,24},{1,17},{9,25},{2,18},{10,26},{3,19},{11,27},{4,20},{... | collective-permute-start | bytes 884744 | tf_op jit(solution)/shard_map/ppermute | solution.py:598
  16.0 3.6 %collective-permute-start.5 = (bf16[4,384,256]{2,1,0:T(8,128)(2,1)S(1)}, bf16[4,384,256]{2,1,0:T(8,128)(2,1)S(1)}, u32[]{:S(2)}, u32[]{:S(2)}) collective-permute-start(bf16[4,384,256]{2,1,0:T(8,128)(2,1)S(1)} %laid_together.4.refs_7_), channel_id=1, source_target_pairs={{0,8},{8,0},{16,24},{24,16},{1,9},{9,1},{17,25},{25,17},{2,10},{10... | collective-permute-start | bytes 2359304 | tf_op jit(solution)/shard_map/ppermute | solution.py:600
  18.4 1.2 %copy-start.3 = (bf16[1,384,1024]{2,1,0:T(8,128)(2,1)S(1)}, bf16[1,384,1024]{2,1,0:T(8,128)(2,1)}, u32[]{:S(2)}) copy-start(bf16[1,384,1024]{2,1,0:T(8,128)(2,1)} %param.25) | copy-start | bytes 2359300
  25.4 2.6 %collective-permute-start.7 = (bf16[1,144,1024]{2,1,0:T(8,128)(2,1)S(1)}, bf16[1,144,1024]{2,1,0:T(8,128)(2,1)S(1)}, u32[]{:S(2)}, u32[]{:S(2)}) collective-permute-start(bf16[1,144,1024]{2,1,0:T(8,128)(2,1)S(1)} %laid_together.5.refs_7_), channel_id=1, source_target_pairs={{0,8},{8,0},{16,24},{24,16},{1,9},{9,1},{17,25},{25,17},{2,10},{10... | collective-permute-start | bytes 884744 | tf_op jit(solution)/shard_map/ppermute | solution.py:617
  27.1 1.4 %copy-start.2 = (bf16[1,384,2048]{2,1,0:T(8,128)(2,1)S(1)}, bf16[1,384,2048]{2,1,0:T(8,128)(2,1)}, u32[]{:S(2)}) copy-start(bf16[1,384,2048]{2,1,0:T(8,128)(2,1)} %param.19) | copy-start | bytes 4718596
  30.8 11.3 %collective-permute-start.10 = (f32[8,384]{1,0:T(8,128)S(1)}, f32[8,384]{1,0:T(8,128)S(1)}, u32[]{:S(2)}, u32[]{:S(2)}) collective-permute-start(f32[8,384]{1,0:T(8,128)S(1)} %get-tuple-element.28.refs_11_.refs_3_), channel_id=1, source_target_pairs={{0,3},{1,0},{2,1},{3,2},{4,7},{5,4},{6,5},{7,6},{8,11},{9,8},{10,9... | collective-permute-start | bytes 36872 | tf_op jit(solution)/shard_map/ppermute | solution.py:623
  31.2 10.8 %collective-permute-start.9 = (f32[8,384]{1,0:T(8,128)S(1)}, f32[8,384]{1,0:T(8,128)S(1)}, u32[]{:S(2)}, u32[]{:S(2)}) collective-permute-start(f32[8,384]{1,0:T(8,128)S(1)} %get-tuple-element.28.refs_11_.refs_3_), channel_id=1, source_target_pairs={{0,2},{1,3},{2,0},{3,1},{4,6},{5,7},{6,4},{7,5},{8,10},{9,11},{10,... | collective-permute-start | bytes 36872 | tf_op jit(solution)/shard_map/ppermute | solution.py:623
  33.8 8.2 %collective-permute-start.8 = (f32[8,384]{1,0:T(8,128)S(1)}, f32[8,384]{1,0:T(8,128)S(1)}, u32[]{:S(2)}, u32[]{:S(2)}) collective-permute-start(f32[8,384]{1,0:T(8,128)S(1)} %get-tuple-element.28.refs_11_.refs_3_), channel_id=1, source_target_pairs={{0,1},{1,2},{2,3},{3,0},{4,5},{5,6},{6,7},{7,4},{8,9},{9,10},{10,1... | collective-permute-start | bytes 36872 | tf_op jit(solution)/shard_map/ppermute | solution.py:623
  36.3 5.8 %copy-start.9 = (f32[2048]{0:T(1024)S(1)}, f32[2048]{0:T(1024)}, u32[]{:S(2)}) copy-start(f32[2048]{0:T(1024)} %param.24) | copy-start | bytes 24580

commit v3 on v2

--- a/solution.py
+++ b/solution.py
@@ -11,6 +11,7 @@
 HD = 128
 CAP = 3
 BQ = 128
+NORM_PARTS = 8
 EPSILON = 1e-05
 NEGATIVE = -1e30
 LOG2E = 1.4426950408889634
@@ -24,16 +25,17 @@
 HBM = pl.BlockSpec(memory_space=pltpu.HBM)
 
 
-def call(kernel, name, out, ins, outs, scratch=(), mib=16, aliases=None, after=()):
+def call(kernel, name, out, ins, outs, scratch=(), mib=16, after=(), held=(), aliases=None):
     count = len(ins)
+    unread = (*after, *held)
 
     def body(*refs):
-        kernel(*refs[:count], *refs[count + len(after) :])
+        kernel(*refs[:count], *refs[count + len(unread) :])
 
     run = pl.pallas_call(
         body,
         out_shape=out,
-        in_specs=list(ins) + [ANY] * len(after),
+        in_specs=list(ins) + [ANY] * len(after) + [VMEM] * len(held),
         out_specs=outs,
         scratch_shapes=list(scratch),
         input_output_aliases=aliases or {},
@@ -41,7 +43,7 @@
         cost_estimate=pl.CostEstimate(flops=10**10, bytes_accessed=10**7, transcendentals=0),
         name=name,
     )
-    return lambda *operands: run(*operands, *after)
+    return lambda *operands: run(*operands, *unread)
 
 
 def struct(*shape, dtype=F32):
@@ -76,7 +78,7 @@
 
 def valid_rows(new_len, span):
     position = lax.axis_index("seq") * span + lax.broadcasted_iota(jnp.int32, (span, 1), 0)
-    return position < new_len[0]
+    return position < new_len[...]
 
 
 def slots_of(lists, base, count, owner):
@@ -166,7 +168,7 @@
     heads = decay_t.shape[0]
     n = b_in.shape[1]
     lane = lax.axis_index("seq") * span + lax.broadcasted_iota(jnp.int32, (1, span), 1)
-    dec = jnp.where(lane < new_len[0], decay_t[...], 0.0)
+    dec = jnp.where(lane < new_len[...], decay_t[...], 0.0)
     row = lax.broadcasted_iota(jnp.int32, (span, span), 0)
     col = lax.broadcasted_iota(jnp.int32, (span, span), 1)
     upper = jnp.where(row <= col, 1.0, 0.0).astype(BF16)
@@ -209,14 +211,14 @@
             struct(span, heads),
             struct(heads, span),
         ),
-        [SMEM, VMEM, VMEM, VMEM],
+        [VMEM] * 4,
         (VMEM,) * 5,
         after=after,
     )(new_len, decay_t, b_in, xs)
 
 
 def local_scan_kernel(
-    begin, new_len, running, running_t, b_in, c_in, xs, d_skip, out, cols, inter, skips
+    begin, new_len, running, running_t, b_in, c_in, xs, d_skip, out, cols, inter, skips, into, outof
 ):
     span, channels = xs.shape
     heads = running.shape[1]
@@ -228,6 +230,10 @@
     for g in range(here_channels // width):
         first = begin // P_SIZE + g * group
         cols[g] = r[:, first : first + group]
+    for i in range(1, blocks):
+        edge = r[i * BQ - 1 : i * BQ, :]
+        into[i - 1, : i * BQ] = split(jnp.exp(edge - r[: i * BQ]), 2)
+        outof[i - 1] = split(jnp.exp(r[i * BQ : (i + 1) * BQ] - edge), 2)
     b = jnp.where(valid_rows(new_len, span), b_in[...].astype(F32), 0.0).astype(BF16)
     inter[...] = mm_nt(c_in[...], b)
     spread = spread_matrix(heads, 3, begin // P_SIZE, here_channels)
@@ -239,11 +245,21 @@
 
     def heads_of(step, unused):
         col = cols[step]
-        row = running_t[pl.ds(pl.multiple_of(begin // P_SIZE + step * group, group), group), :]
+        first = begin // P_SIZE + step * group
+        row = running_t[pl.ds(pl.multiple_of(first, group), group), :]
+        x_group = xs[:, pl.ds(pl.multiple_of(begin + step * width, width), width)]
+        spread = spread_matrix(heads, 2, first, width)
+        earlier = [None]
+        for i in range(1, blocks):
+            factor = mm(into[i - 1, : i * BQ], spread)
+            weighted = (x_group[: i * BQ].astype(F32) * factor).astype(BF16)
+            product = mm(inter[i * BQ : (i + 1) * BQ, : i * BQ].astype(BF16), weighted)
+            earlier.append(product * mm(outof[i - 1], spread))
         for pair in range(group // 2):
+            at = slice(pair * 2 * P_SIZE, (pair + 1) * 2 * P_SIZE)
             offset = step * width + pair * 2 * P_SIZE
             lanes = pl.ds(pl.multiple_of(offset, 2 * P_SIZE), 2 * P_SIZE)
-            x_pair = xs[:, pl.ds(pl.multiple_of(begin + offset, 2 * P_SIZE), 2 * P_SIZE)]
+            x_pair = x_group[:, at]
             zero = jnp.zeros_like(x_pair)
             sides = (jnp.where(left, x_pair, zero), jnp.where(left, zero, x_pair))
             for i in range(blocks):
@@ -251,16 +267,13 @@
                 lhs, rhs = [], []
                 for side in range(2):
                     h = pair * 2 + side
-                    at_t = jnp.broadcast_to(col[here, h : h + 1], (BQ, BQ))
-                    for j in range(i + 1):
-                        there = slice(j * BQ, (j + 1) * BQ)
-                        gap = at_t - row[h : h + 1, there]
-                        if j == i:
-                            gap = jnp.where(lower, gap, NEGATIVE)
-                        lhs.append((jnp.exp(gap) * inter[here, there]).astype(BF16))
-                        rhs.append(sides[side][there])
+                    gap = jnp.broadcast_to(col[here, h : h + 1], (BQ, BQ)) - row[h : h + 1, here]
+                    gap = jnp.where(lower, gap, NEGATIVE)
+                    lhs.append((jnp.exp(gap) * inter[here, here]).astype(BF16))
+                    rhs.append(sides[side][here])
                 y = mm(jnp.concatenate(lhs, axis=1), jnp.concatenate(rhs, axis=0))
-                out[here, lanes] = y + skips[:1, lanes] * x_pair[here].astype(F32)
+                y = y + skips[:1, lanes] * x_pair[here].astype(F32)
+                out[here, lanes] = y if i == 0 else y + earlier[i][:, at]
         return unused
 
     lax.fori_loop(0, here_channels // width, heads_of, 0)
@@ -268,17 +281,21 @@
 
 def local_scan(begin, size, operands, after):
     span = operands[-2].shape[0]
+    heads = operands[1].shape[1]
     width = min(512, size)
+    blocks = span // BQ
     return call(
         functools.partial(local_scan_kernel, begin),
         "local_scan",
         struct(span, size),
-        [SMEM] + [VMEM] * 6,
+        [VMEM] * 7,
         VMEM,
         [
             pltpu.VMEM((size // width, span, width // P_SIZE), F32),
             pltpu.VMEM((span, span), F32),
             pltpu.VMEM((8, size), F32),
+            pltpu.VMEM((blocks - 1, span, 2 * heads), BF16),
+            pltpu.VMEM((blocks - 1, BQ, 2 * heads), BF16),
         ],
         after=after,
     )(*operands)
@@ -410,82 +427,86 @@
     )(running, c_in, gate, cached, met, middle, swapped, *local)
 
 
-def norm_kernel(all_channels, count, new_len, gated, gain, *rest):
-    sums, (out, staged, sems) = rest[:count], rest[count:]
+def norm_kernel(all_channels, count, new_len, gated, gain, late, *rest):
+    sums, (out, attended, staged, sems) = rest[:count], rest[count + 1 :]
     span, channels = gated.shape
-    width = min(512, channels)
+    rows_each = span // NORM_PARTS
+    begin = attended.shape[1] - late.shape[1]
+    copies = [
+        pltpu.make_async_copy(late, attended.at[:, pl.ds(begin, late.shape[1])], sems.at[0])
+    ]
+    copies[0].start()
     total = sums[0][...]
     for part in sums[1:]:
         total = total + part[...]
     scale = lax.rsqrt(total / all_channels + EPSILON).T[:, :1]
     scale = jnp.where(valid_rows(new_len, span), scale, 0.0)
-    copies = []
-    for k, begin in enumerate(range(0, channels, width)):
-        lanes = slice(begin, begin + width)
-        staged[:, lanes] = (gated[:, lanes].astype(F32) * scale * gain[:, lanes]).astype(BF16)
-        at = pl.ds(begin, width)
-        copies.append(pltpu.make_async_copy(staged.at[:, at], out.at[:, at], sems.at[k]))
+    for begin in range(0, span, rows_each):
+        rows = slice(begin, begin + rows_each)
+        staged[rows] = (gated[rows].astype(F32) * scale[rows] * gain[...]).astype(BF16)
+        at = pl.ds(begin, rows_each)
+        copies.append(pltpu.make_async_copy(staged.at[at], out.at[at], sems.at[len(copies)]))
         copies[-1].start()
     for copy in copies:
         copy.wait()
 
 
-def norm_output(new_len, gated, gain, sums, all_channels, after):
+def norm_output(new_len, gated, gain, sums, all_channels, late, attended):
     span, channels = gated.shape
+    copies = 1 + NORM_PARTS
     return call(
         functools.partial(norm_kernel, all_channels, len(sums)),
         "norm",
-        struct(span, channels, dtype=BF16),
-        [SMEM] + [VMEM] * (2 + len(sums)),
-        HBM,
-        [
-            pltpu.VMEM((span, channels), BF16),
-            pltpu.SemaphoreType.DMA((channels // min(512, channels),)),
-        ],
-        after=after,
-    )(new_len, gated, gain, *sums)
+        (struct(span, channels, dtype=BF16), struct(*attended.shape, dtype=BF16)),
+        [VMEM] * (4 + len(sums)) + [HBM],
+        (HBM, HBM),
+        [pltpu.VMEM((span, channels), BF16), pltpu.SemaphoreType.DMA((copies,))],
+        aliases={4 + len(sums): 1},
+    )(new_len, gated, gain, late, *sums, attended)
 
 
 def attention_kernel(
-    kv_head, heads, groups, total, new_len, cached, lists, q, own_k, own_v, far, near, kept,
-    received, *rest
+    heads, groups, total, new_len, cached, lists, q, own_k, own_v, far, near, kept, received, *rest
 ):
-    out, token, keys, values, scores, weights, staged, sems = rest[-8:]
+    if len(rest) > 5:
+        before, out, staged, keys, values, scores, weights, sem = rest
+        done = before.shape[1]
+        copy = pltpu.make_async_copy(before, out.at[:, pl.ds(0, done)], sem)
+        copy.start()
+    else:
+        copy = None
+        staged, keys, values, scores, weights = rest
     span = own_k.shape[0]
     entries, rows_each = kept.shape[0], kept.shape[2]
+    kv_heads = sorted({head // groups for head in heads})
     seq = lax.axis_index("seq")
-    lanes = slice(kv_head * HD, (kv_head + 1) * HD)
     cached_len = entries * rows_each
     few = 2 * span + cached_len
     factor = HD ** (-0.5) * LOG2E
-    token[...] = jnp.zeros_like(token)
 
     def put(begin, key_rows, value_rows):
         rows = slice(begin, begin + key_rows.shape[0])
-        keys[rows] = key_rows
-        values[rows, :HD] = value_rows
-        values[rows, HD:] = jnp.ones_like(value_rows)
-
-    put(0, own_k[:, lanes], own_v[:, lanes])
-    put(span + cached_len, near[0, :, lanes], near[1, :, lanes])
+        for h, kv_head in enumerate(kv_heads):
+            lanes = slice(kv_head * HD, (kv_head + 1) * HD)
+            keys[h, rows] = key_rows[:, lanes]
+            values[h, rows, :HD] = value_rows[:, lanes]
+            values[h, rows, HD:] = jnp.ones_like(value_rows[:, lanes])
+
+    put(0, own_k[...], own_v[...])
+    put(span + cached_len, near[0], near[1])
     for e in range(entries):
         mine, taken = place_of(lists, 0, entries, e, total)
-        record = [jnp.where(mine, kept[e, k, :, lanes], received[taken, k, :, lanes]) for k in (0, 1)]
+        record = [jnp.where(mine, kept[e, k], received[taken, k]) for k in (0, 1)]
         put(span + e * rows_each, *record)
     key = lax.broadcasted_iota(jnp.int32, (1, few - span), 1)
-    open_keys = (key < cached[0] * rows_each) | ((key >= cached_len) & (seq % 2 == 1))
+    open_keys = (key < cached[...] * rows_each) | ((key >= cached_len) & (seq % 2 == 1))
     bias = jnp.where(open_keys, 0.0, NEGATIVE)
     valid = valid_rows(new_len, span)
 
-    def copy_out(k):
-        at = pl.ds((kv_head * groups + heads[k]) * HD, HD)
-        return pltpu.make_async_copy(staged.at[:, pl.ds(k * HD, HD)], out.at[:, at], sems.at[k])
-
     def attend(count):
-        for k, g in enumerate(heads):
-            slot = k % 2
-            head = slice((kv_head * groups + g) * HD, (kv_head * groups + g + 1) * HD)
-            scores[slot, :, :count] = mm_nt(q[:, head], keys[:count])
+        for k, head in enumerate(heads):
+            slot, kv_head = k % 2, kv_heads.index(head // groups)
+            scores[slot, :, :count] = mm_nt(q[:, head * HD : (head + 1) * HD], keys[kv_head, :count])
             for begin in range(0, span, BQ):
                 rows = slice(begin, begin + BQ)
                 s = scores[slot, rows, :count]
@@ -497,10 +518,9 @@
                 s = jnp.concatenate(parts, axis=1)
                 high = jnp.max(s, axis=1, keepdims=True)
                 weights[slot, rows, :count] = jnp.exp2(s * factor - high * factor).astype(BF16)
-            summed = mm(weights[slot, :, :count], values[:count])
+            summed = mm(weights[slot, :, :count], values[kv_head, :count])
             ratio = summed[:, :HD] / summed[:, HD:]
             staged[:, k * HD : (k + 1) * HD] = jnp.where(valid, ratio, 0.0).astype(BF16)
-            copy_out(k).start()
 
     @pl.when(seq < 2)
     def _():
@@ -508,45 +528,46 @@
 
     @pl.when(seq >= 2)
     def _():
-        put(few, far[0, :, lanes], far[1, :, lanes])
-        put(few + span, near[2, :, lanes], near[3, :, lanes])
+        put(few, far[0], far[1])
+        put(few + span, near[2], near[3])
         attend(few + 2 * span)
 
-    for k in range(len(heads)):
-        copy_out(k).wait()
+    if copy is not None:
+        copy.wait()
 
 
 def attention(
-    kv_head, heads, total, new_len, cached, lists, q, keys, values, far, near, kept,
-    received, out, after,
+    heads, total, new_len, cached, lists, q, keys, values, far, near, kept, received, before, after,
+    held,
 ):
     span = q.shape[0]
     groups = q.shape[1] // keys.shape[1]
+    kv_heads = len({head // groups for head in heads})
     most = 4 * span + kept.shape[0] * kept.shape[2]
-    operands = (new_len, cached, lists, q, keys, values, far, near, kept, received)
-    ins = [SMEM] * 3 + [VMEM] * 7
-    aliases = {}
-    if out is not None:
-        aliases = {len(operands): 0}
-        operands += (out,)
-        ins += [HBM]
-    return call(
-        functools.partial(attention_kernel, kv_head, heads, groups, total),
+    operands = [new_len, cached, lists, q, keys, values, far, near, kept, received]
+    ins = [VMEM, VMEM, SMEM] + [VMEM] * 7
+    out, out_specs = struct(span, len(heads) * HD, dtype=BF16), VMEM
+    scratch = [
+        pltpu.VMEM((kv_heads, most, HD), BF16),
+        pltpu.VMEM((kv_heads, most, 2 * HD), BF16),
+        pltpu.VMEM((2, span, most), F32),
+        pltpu.VMEM((2, span, most), BF16),
+    ]
+    if before is not None:
+        operands.append(before)
+        ins.append(VMEM)
+        out, out_specs = (struct(*q.shape, dtype=BF16), out), (HBM, VMEM)
+        scratch.append(pltpu.SemaphoreType.DMA)
+    return call(
+        functools.partial(attention_kernel, heads, groups, total),
         "attention",
-        (struct(*q.shape, dtype=BF16), struct(8, 128)),
+        out,
         ins,
-        (HBM, VMEM),
-        [
-            pltpu.VMEM((most, HD), BF16),
-            pltpu.VMEM((most, 2 * HD), BF16),
-            pltpu.VMEM((2, span, most), F32),
-            pltpu.VMEM((2, span, most), BF16),
-            pltpu.VMEM((span, len(heads) * HD), BF16),
-            pltpu.SemaphoreType.DMA((len(heads),)),
-        ],
-        mib=14 + most * span * 12 // 2**20,
-        aliases=aliases,
+        out_specs,
+        scratch,
+        mib=16 + most * span * 12 // 2**20,
         after=after,
+        held=held,
     )(*operands)
 
 
@@ -560,6 +581,7 @@
     entries, pieces = kv_slot.shape[1], state_slot.shape[1]
     xs, gate_z, b_in, c_in, decay = xs[0], gate_z[0], b_in[0], c_in[0], log_decay[0]
     queries, keys_new, values_new = queries[0], keys_new[0], values_new[0]
+    new_len, cached_blocks = new_len.reshape(1, 1), cached_blocks.reshape(1, 1)
 
     beside = [(0, 1), (1, 0), (2, 3), (3, 2)]
     across = [(0, 2), (1, 3)]
@@ -574,7 +596,6 @@
     met = lax.ppermute(sent, "seq", beside)
 
     scan_operands = (new_len, running, running_t, b_in, c_in, xs, d_skip[None])
-    half = xs.shape[1] // 2
     kv_received, st_received, kept = [], [], None
     for shift in range(1, total):
         there = [(i, (i + shift) % total) for i in range(total)]
@@ -596,33 +617,33 @@
 
     sent = middle_state(met, end, through, (kv_kept,))
     middle = lax.ppermute(sent, "seq", across)
-    both = laid_together([fresh, far], (sent,))
+    quarter = xs.shape[1] // 4
+    local = [local_scan(0, 2 * quarter, scan_operands, (sent,))]
+    both = laid_together([fresh, far], (local[0],))
     near = lax.ppermute(both, "seq", beside)
-
-    groups = queries.shape[1] // keys_new.shape[1]
-    kv_heads = keys_new.shape[1] // HD
-
-    def attend(kv_head, out, after):
+    local.append(local_scan(2 * quarter, quarter, scan_operands, (both,)))
+    q_heads = queries.shape[1] // HD
+    later = q_heads // 4
+
+    def attend(heads, before, after, held):
         return attention(
-            kv_head, tuple(range(groups)), total, new_len, cached_blocks, lists, queries, keys_new,
-            values_new, far, near, kv_kept, kv_received, out, after,
+            heads, total, new_len, cached_blocks, lists, queries, keys_new, values_new, far, near,
+            kv_kept, kv_received, before, after, held,
         )
 
-    local = [local_scan(0, half, scan_operands, (both,))]
-    local.append(local_scan(half, half // 2, scan_operands, (local[0],)))
-    out, token = None, local[1]
-    for kv_head in range(kv_heads - 1):
-        out, token = attend(kv_head, out, (token,))
-    held = laid_together([middle], (token,))
+    early = attend(tuple(range(q_heads - later)), None, (local[1],), (gate_z,))
+    held = laid_together([middle], (early,))
     swapped = lax.ppermute(held, "seq", beside)[0]
-    local.append(local_scan(half + half // 2, half // 2, scan_operands, (held,)))
+    local.append(local_scan(3 * quarter, quarter, scan_operands, (held,)))
     cached = cached_state(lists, 2 * entries, total, st_kept, st_received, (local[2],))
     gated, squares = gate_output(running, c_in, gate_z, cached, met, middle, swapped, local)
     sums = [squares]
     for shift in range(1, mp):
         sums.append(lax.ppermute(squares, "mp", [(i, (i + shift) % mp) for i in range(mp)]))
-    attended, token = attend(kv_heads - 1, out, (squares,))
-    ssm_out = norm_output(new_len, gated, norm_gain[None], sums, channels_all, (token,))
+    attended, late = attend(tuple(range(q_heads - later, q_heads)), early, (squares,), ())
+    ssm_out, attended = norm_output(
+        new_len, gated, norm_gain[None], sums, channels_all, late, attended
+    )
     return (ssm_out[None], attended[None])
 
 

time: 44.1 us -> 41.9 us (0.950)
  the two profiles are of different devices: /device:TPU:10 before, /device:TPU:0 now
where the time goes in v3:
time: 41.9 us; the launch traced here: 41.7 us
  Pallas kernels  19.5 us (47%)
  starting transfers between devices  15.1 us (36%)
  waiting for transfers between devices  3.56 us (8%)
  between operations  2.47 us (6%)
  local copies, waits for them, and re-layouts  1.02 us (2%)
    pallas_call x15, Pallas kernels, call(): return lambda *operands: run(*operands, *unread)  19.5 us
    ppermute x3, starting transfers between devices, per_device(): lax.ppermute(squares, 'mp', [(i, (i + shift) % mp) for i in range(mp)])  4.64 us
    ppermute x1, starting transfers between devices, per_device(): far = lax.ppermute(fresh, 'seq', across)  3.68 us
    ppermute x1, starting transfers between devices, per_device(): asked = lax.ppermute(lists, 'batch', there)  2.97 us
    ppermute x3, waiting for transfers between devices, per_device(): lax.ppermute(squares, 'mp', [(i, (i + shift) % mp) for i in range(mp)])  1.73 us
    ppermute x1, starting transfers between devices, per_device(): st_received.append(lax.ppermute(found[1], 'batch', back))  1.52 us
    ppermute x1, starting transfers between devices, per_device(): middle = lax.ppermute(sent, 'seq', across)  1.4 us
    unnamed x34, local copies, waits for them, and re-layouts  1.02 us
  transfers between devices with their start and end apart: 11, of which 5 were waited for; matrix products, arithmetic and copies ran while one was open for 0% of the time, Pallas kernels for 38%

profile of v3, /device:TPU:0, one launch (start us, length us, event | category | flops | bytes accessed | tf_op | source)
XLA Modules:
  0.0 41.7 jit_solution(80036673966805717)
XLA Ops:
  0.6 0.0 copy-start.11
  0.6 0.0 copy-start.12
  0.7 0.0 copy-start.13
  0.7 0.0 copy-start.14
  0.7 0.0 copy-start.5
  0.7 0.0 copy-start.4
  0.7 0.6 %copy-done.11 = s32[1,4]{1,0:T(1,128)S(1)} copy-done((s32[1,4]{1,0:T(1,128)S(1)}, s32[1,4]{1,0:T(1,128)}, u32[]{:S(2)}) %copy-start.11) | copy-done | bytes 40
  1.3 0.0 copy-done.12
  1.3 0.0 copy-done.13
  1.3 0.0 copy-done.14
  1.3 0.1 add_add_fusion.refs_2_.refs_1_.refs_0_
  1.4 3.0 %collective-permute-start = (s32[16]{0:T(128)S(1)}, s32[16]{0:T(128)S(1)}, u32[]{:S(2)}, u32[]{:S(2)}) collective-permute-start(s32[16]{0:T(128)S(1)} %add_add_fusion.refs_2_.refs_1_.refs_0_), channel_id=1, source_target_pairs={{0,4},{4,0},{1,5},{5,1},{2,6},{6,2},{3,7},{7,3},{8,12},{12,8},{9,1... | collective-permute-start | bytes 200 | tf_op jit(solution)/shard_map/ppermute | solution.py:603
  4.4 0.0 copy-done.5
  4.4 0.0 copy-done.4
  4.4 0.0 copy-start.8
  4.4 0.0 slice-start
  4.5 3.7 %collective-permute-start.4 = (bf16[2,384,256]{2,1,0:T(8,128)(2,1)S(1)}, bf16[2,384,256]{2,1,0:T(8,128)(2,1)S(1)}, u32[]{:S(2)}, u32[]{:S(2)}) collective-permute-start(bf16[2,384,256]{2,1,0:T(8,128)(2,1)S(1)} %laid_together.3.refs_4_.refs_0_), channel_id=1, source_target_pairs={{0,16},{8,24},{1,17},{9,25},{2,18},{10,26},{3,19},{11,27},{4,20},{... | collective-permute-start | bytes 1179656 | tf_op jit(solution)/shard_map/ppermute | solution.py:594
  8.8 0.0 slice-start.1
  8.8 0.0 copy-done.1
  8.8 0.0 copy-done.6
  8.8 0.0 copy-done.8
  8.8 0.0 copy-start
  8.9 1.7 %end_state.1 = (bf16[144,2048]{1,0:T(8,128)(2,1)S(1)}, f32[128,2048]{1,0:T(8,128)S(1)}, f32[8,2048]{1,0:T(8,128)S(1)}, f32[384,32]{1,0:T(8,128)S(1)}, f32[32,384]{1,0:T(8,128)S(1)}) custom-call(s32[1,1]{1,0:T(1,128)} %bitcast.23.refs_0_, f32[32,384]{1,0:T(8,128)S(1)} %bitcast.57, bf16[384,128]{1,0:T(8,128)(2,1)S(1)} %bitcast.49, ...), custom_call_target="tpu_custom_call" | custom-call | flops 10000000000 | bytes 10000000 | tf_op jit(solution)/shard_map/end_state/pallas_call | solution.py:46
  10.6 0.1 collective-permute-start.2
  11.3 0.0 collective-permute-done.refs_0_
  11.3 0.0 slice-done
  11.4 0.0 slice-done.1
  11.4 0.3 copy-done
  11.7 0.7 %look_up.1 = (bf16[3,2,64,256]{3,2,1,0:T(8,128)(2,1)S(1)}, bf16[3,32,16,128]{3,2,1,0:T(8,128)(2,1)S(1)}, bf16[4,2,64,256]{3,2,1,0:T(8,128)(2,1)S(1)}, bf16[4,32,16,128]{3,2,1,0:T(8,128)(2,1)S(1)}) custom-call(s32[16]{0:T(128)S(1)} %collective-permute-done.refs_0_, s32[16]{0:T(128)S(1)} %add_add_fusion.refs_2_.refs_1_.refs_0_, ...), custom_call_target="tpu_custom_call" | custom-call | flops 10000000000 | bytes 10000000 | tf_op jit(solution)/shard_map/look_up/pallas_call | solution.py:46
  12.3 0.6 %collective-permute-start.6 = (bf16[3,2,64,256]{3,2,1,0:T(8,128)(2,1)S(1)}, bf16[3,2,64,256]{3,2,1,0:T(8,128)(2,1)S(1)}, u32[]{:S(2)}, u32[]{:S(2)}) collective-permute-start(bf16[3,2,64,256]{3,2,1,0:T(8,128)(2,1)S(1)} %get-tuple-element.25), channel_id=1, source_target_pairs={{4,0},{0,4},{5,1},{1,5},{6,2},{2,6},{7,3},{3,7},{12,8},{8,12},{13,... | collective-permute-start | bytes 589832 | tf_op jit(solution)/shard_map/ppermute | solution.py:609
  12.9 1.5 %collective-permute-start.1 = (bf16[3,32,16,128]{3,2,1,0:T(8,128)(2,1)S(1)}, bf16[3,32,16,128]{3,2,1,0:T(8,128)(2,1)S(1)}, u32[]{:S(2)}, u32[]{:S(2)}) collective-permute-start(bf16[3,32,16,128]{3,2,1,0:T(8,128)(2,1)S(1)} %get-tuple-element.20), channel_id=1, source_target_pairs={{4,0},{0,4},{5,1},{1,5},{6,2},{2,6},{7,3},{3,7},{12,8},{8,12},{13,... | collective-permute-start | bytes 1179656 | tf_op jit(solution)/shard_map/ppermute | solution.py:610
  14.4 0.0 collective-permute-done.2.refs_0_.refs_4_
  14.4 0.1 middle_state.1.refs_7_
  14.6 1.4 %collective-permute-start.3 = (bf16[144,1024]{1,0:T(8,128)(2,1)S(1)}, bf16[144,1024]{1,0:T(8,128)(2,1)S(1)}, u32[]{:S(2)}, u32[]{:S(2)}) collective-permute-start(bf16[144,1024]{1,0:T(8,128)(2,1)S(1)} %middle_state.1.refs_7_), channel_id=1, source_target_pairs={{0,16},{8,24},{1,17},{9,25},{2,18},{10,26},{3,19},{11,27},{4,20},{... | collective-permute-start | bytes 884744 | tf_op jit(solution)/shard_map/ppermute | solution.py:619
  16.0 0.0 copy-done.7
  16.0 0.0 copy-done.10
  16.0 2.3 %local_scan.3.refs_2_.refs_7_ = f32[384,1024]{1,0:T(8,128)S(1)} custom-call(s32[1,1]{1,0:T(1,128)} %bitcast.24.refs_0_, f32[384,32]{1,0:T(8,128)S(1)} %get-tuple-element.17.refs_1_.refs_0_, f32[32,384]{1,0:T(8,128)S(1)} %get-tuple-element.21.refs_2_, bf16[384,128]{1,0:T(8,128)(2,1)S(1)} %bitcast.50, bf16[384,128]{1,0:T(8,128)(2,1)S(1)} %bitcast.53, ...), custom_call_target="tpu_custom_call" | custom-call | flops 10000000000 | bytes 10000000 | tf_op jit(solution)/shard_map/local_scan/pallas_call | solution.py:46
  18.3 0.0 collective-permute-done.4.refs_1_.refs_6_
  18.3 0.1 laid_together.4.refs_7_
  18.4 0.1 collective-permute-start.5
  18.5 0.0 copy-start.2
  18.5 0.0 copy-start.3
  18.5 1.2 %local_scan.4.refs_10_.refs_8_ = f32[384,512]{1,0:T(8,128)S(1)} custom-call(s32[1,1]{1,0:T(1,128)} %bitcast.25.refs_0_, f32[384,32]{1,0:T(8,128)S(1)} %get-tuple-element.17.refs_1_.refs_0_, f32[32,384]{1,0:T(8,128)S(1)} %get-tuple-element.21.refs_2_, bf16[384,128]{1,0:T(8,128)(2,1)S(1)} %bitcast.51, bf16[384,128]{1,0:T(8,128)(2,1)S(1)} %bitcast.54, ...), custom_call_target="tpu_custom_call" | custom-call | flops 10000000000 | bytes 10000000 | tf_op jit(solution)/shard_map/local_scan/pallas_call | solution.py:46
  19.7 0.5 %collective-permute-done.6.refs_9_ = bf16[3,2,64,256]{3,2,1,0:T(8,128)(2,1)S(1)} collective-permute-done((bf16[3,2,64,256]{3,2,1,0:T(8,128)(2,1)S(1)}, bf16[3,2,64,256]{3,2,1,0:T(8,128)(2,1)S(1)}, u32[]{:S(2)}, u32[]{:S(2)}) %collective-permute-start.6) | collective-permute-done | bytes 196640 | tf_op jit(solution)/shard_map/ppermute | solution.py:609
  20.1 0.6 %collective-permute-done.5.refs_7_ = bf16[4,384,256]{2,1,0:T(8,128)(2,1)S(1)} collective-permute-done((bf16[4,384,256]{2,1,0:T(8,128)(2,1)S(1)}, bf16[4,384,256]{2,1,0:T(8,128)(2,1)S(1)}, u32[]{:S(2)}, u32[]{:S(2)}) %collective-permute-start.5) | collective-permute-done | bytes 786464 | tf_op jit(solution)/shard_map/ppermute | solution.py:623
  20.7 0.0 copy-done.2
  20.7 0.0 copy-done.3
  20.7 4.9 %attention.2.refs_1_.refs_10_ = bf16[384,768]{1,0:T(8,128)(2,1)S(1)} custom-call(s32[1,1]{1,0:T(1,128)} %bitcast.26.refs_0_, s32[1,1]{1,0:T(1,128)} %bitcast.30.refs_1_, s32[16]{0:T(128)S(1)} %add_add_fusion.refs_2_.refs_1_.refs_0_, bf16[384,1024]{1,0:T(8,128)(2,1)S(1)} %bitcast.40, bf16[384,256]{1,0:T(8,128)(2,1)S(1)} %bitcast.44, ...), custom_call_target="tpu_custom_call" | custom-call | flops 10000000000 | bytes 10000000 | tf_op jit(solution)/shard_map/attention/pallas_call | solution.py:46
  25.7 0.0 collective-permute-done.3.refs_0_.refs_5_
  25.7 0.2 collective-permute-start.7
  25.9 1.2 %local_scan.5.refs_3_.refs_9_ = f32[384,512]{1,0:T(8,128)S(1)} custom-call(s32[1,1]{1,0:T(1,128)} %bitcast.27.refs_0_, f32[384,32]{1,0:T(8,128)S(1)} %get-tuple-element.17.refs_1_.refs_0_, f32[32,384]{1,0:T(8,128)S(1)} %get-tuple-element.21.refs_2_, bf16[384,128]{1,0:T(8,128)(2,1)S(1)} %bitcast.52, bf16[384,128]{1,0:T(8,128)(2,1)S(1)} %bitcast.55, ...), custom_call_target="tpu_custom_call" | custom-call | flops 10000000000 | bytes 10000000 | tf_op jit(solution)/shard_map/local_scan/pallas_call | solution.py:46
  27.1 0.7 %collective-permute-done.1.refs_2_ = bf16[3,32,16,128]{3,2,1,0:T(8,128)(2,1)S(1)} collective-permute-done((bf16[3,32,16,128]{3,2,1,0:T(8,128)(2,1)S(1)}, bf16[3,32,16,128]{3,2,1,0:T(8,128)(2,1)S(1)}, u32[]{:S(2)}, u32[]{:S(2)}) %collective-permute-start.1) | collective-permute-done | bytes 393248 | tf_op jit(solution)/shard_map/ppermute | solution.py:610
  27.8 0.8 %cached_state.1.refs_3_ = bf16[128,2048]{1,0:T(8,128)(2,1)S(1)} custom-call(s32[16]{0:T(128)S(1)} %add_add_fusion.refs_2_.refs_1_.refs_0_, bf16[4,32,16,128]{3,2,1,0:T(8,128)(2,1)S(1)} %get-tuple-element.19.refs_1_, bf16[3,32,16,128]{3,2,1,0:T(8,128)(2,1)S(1)} %collective-permute-done.1.refs_2_, f32[384,512]{1,0:T(8,128)S(1)} %local_scan.5.refs_3_.refs_9_), custom_call_target="tpu_custom_call" | custom-call | flops 10000000000 | bytes 10000000 | tf_op jit(solution)/shard_map/cached_state/pallas_call | solution.py:46
  28.6 0.0 collective-permute-done.7
  28.7 2.3 %gate.1 = (bf16[384,2048]{1,0:T(8,128)(2,1)S(1)}, f32[8,384]{1,0:T(8,128)S(1)}) custom-call(f32[384,32]{1,0:T(8,128)S(1)} %get-tuple-element.17.refs_1_.refs_0_, bf16[384,128]{1,0:T(8,128)(2,1)S(1)} %bitcast.56, bf16[384,2048]{1,0:T(8,128)(2,1)S(1)} %bitcast.39, bf16[128,2048]{1,0:T(8,128)(2,1)S(1)} %cached_state.1.refs_3_, ...), custom_call_target="tpu_custom_call" | custom-call | flops 10000000000 | bytes 10000000 | tf_op jit(solution)/shard_map/gate/pallas_call | solution.py:46
  31.0 3.6 %collective-permute-start.10 = (f32[8,384]{1,0:T(8,128)S(1)}, f32[8,384]{1,0:T(8,128)S(1)}, u32[]{:S(2)}, u32[]{:S(2)}) collective-permute-start(f32[8,384]{1,0:T(8,128)S(1)} %get-tuple-element.27.refs_11_.refs_4_), channel_id=1, source_target_pairs={{0,3},{1,0},{2,1},{3,2},{4,7},{5,4},{6,5},{7,6},{8,11},{9,8},{10,9... | collective-permute-start | bytes 36872 | tf_op jit(solution)/shard_map/ppermute | solution.py:642
  34.6 0.0 collective-permute-start.9
  34.6 1.0 %collective-permute-start.8 = (f32[8,384]{1,0:T(8,128)S(1)}, f32[8,384]{1,0:T(8,128)S(1)}, u32[]{:S(2)}, u32[]{:S(2)}) collective-permute-start(f32[8,384]{1,0:T(8,128)S(1)} %get-tuple-element.27.refs_11_.refs_4_), channel_id=1, source_target_pairs={{0,1},{1,2},{2,3},{3,0},{4,5},{5,6},{6,7},{7,4},{8,9},{9,10},{10,1... | collective-permute-start | bytes 36872 | tf_op jit(solution)/shard_map/ppermute | solution.py:642
  35.6 2.7 %attention.3 = (bf16[384,1024]{1,0:T(8,128)(2,1)}, bf16[384,256]{1,0:T(8,128)(2,1)S(1)}) custom-call(s32[1,1]{1,0:T(1,128)} %bitcast.28.refs_0_, s32[1,1]{1,0:T(1,128)} %bitcast.31.refs_1_, s32[16]{0:T(128)S(1)} %add_add_fusion.refs_2_.refs_1_.refs_0_, bf16[384,1024]{1,0:T(8,128)(2,1)S(1)} %bitcast.41, bf16[384,256]{1,0:T(8,128)(2,1)S(1)} %bitcast.45, ...), custom_call_target="tpu_custom_call" | custom-call | flops 10000000000 | bytes 10000000 | tf_op jit(solution)/shard_map/attention/pallas_call | solution.py:46
  38.4 0.0 collective-permute-done.10.refs_7_
  38.4 0.8 %collective-permute-done.9.refs_6_ = f32[8,384]{1,0:T(8,128)S(1)} collective-permute-done((f32[8,384]{1,0:T(8,128)S(1)}, f32[8,384]{1,0:T(8,128)S(1)}, u32[]{:S(2)}, u32[]{:S(2)}) %collective-permute-start.9) | collective-permute-done | bytes 12320 | tf_op jit(solution)/shard_map/ppermute | solution.py:642
  39.2 0.9 %collective-permute-done.8.refs_5_ = f32[8,384]{1,0:T(8,128)S(1)} collective-permute-done((f32[8,384]{1,0:T(8,128)S(1)}, f32[8,384]{1,0:T(8,128)S(1)}, u32[]{:S(2)}, u32[]{:S(2)}) %collective-permute-start.8) | collective-permute-done | bytes 12320 | tf_op jit(solution)/shard_map/ppermute | solution.py:642
  40.1 0.0 copy-done.9
  40.1 1.5 %norm.1 = (bf16[384,2048]{1,0:T(8,128)(2,1)}, bf16[384,1024]{1,0:T(8,128)(2,1)}) custom-call(s32[1,1]{1,0:T(1,128)} %bitcast.29.refs_0_, bf16[384,2048]{1,0:T(8,128)(2,1)S(1)} %get-tuple-element.26.refs_1_, f32[1,2048]{1,0:T(1,128)S(1)} %bitcast.58, bf16[384,256]{1,0:T(8,128)(2,1)S(1)} %get-tuple-element.28.refs_3_, ...), custom_call_target="tpu_custom_call", output_to_operand_aliasing={{1}: (8, {})} | custom-call | flops 10000000000 | bytes 10000000 | tf_op jit(solution)/shard_map/norm/pallas_call | solution.py:46
  (9 shorter events, 0.1 us)
Async XLA Ops:
  0.6 0.7 %copy-start.11 = (s32[1,4]{1,0:T(1,128)S(1)}, s32[1,4]{1,0:T(1,128)}, u32[]{:S(2)}) copy-start(s32[1,4]{1,0:T(1,128)} %param.35) | copy-start | bytes 52
  0.6 0.7 %copy-start.12 = (s32[1,4,1]{1,2,0:T(1,128)S(1)}, s32[1,4,1]{1,2,0:T(1,128)}, u32[]{:S(2)}) copy-start(s32[1,4,1]{1,2,0:T(1,128)} %param.34) | copy-start | bytes 52
  0.7 0.7 %copy-start.13 = (s32[1,4]{1,0:T(1,128)S(1)}, s32[1,4]{1,0:T(1,128)}, u32[]{:S(2)}) copy-start(s32[1,4]{1,0:T(1,128)} %param.33) | copy-start | bytes 52
  0.7 0.7 %copy-start.14 = (s32[1,4,1]{1,2,0:T(1,128)S(1)}, s32[1,4,1]{1,2,0:T(1,128)}, u32[]{:S(2)}) copy-start(s32[1,4,1]{1,2,0:T(1,128)} %param.32) | copy-start | bytes 52
  0.7 3.7 %copy-start.5 = (bf16[1,384,256]{2,1,0:T(8,128)(2,1)S(1)}, bf16[1,384,256]{2,1,0:T(8,128)(2,1)}, u32[]{:S(2)}) copy-start(bf16[1,384,256]{2,1,0:T(8,128)(2,1)} %param.27) | copy-start | bytes 589828
  0.7 3.7 %copy-start.4 = (bf16[1,384,256]{2,1,0:T(8,128)(2,1)S(1)}, bf16[1,384,256]{2,1,0:T(8,128)(2,1)}, u32[]{:S(2)}) copy-start(bf16[1,384,256]{2,1,0:T(8,128)(2,1)} %param.26) | copy-start | bytes 589828
  1.4 9.9 %collective-permute-start = (s32[16]{0:T(128)S(1)}, s32[16]{0:T(128)S(1)}, u32[]{:S(2)}, u32[]{:S(2)}) collective-permute-start(s32[16]{0:T(128)S(1)} %add_add_fusion.refs_2_.refs_1_.refs_0_), channel_id=1, source_target_pairs={{0,4},{4,0},{1,5},{5,1},{2,6},{6,2},{3,7},{7,3},{8,12},{12,8},{9,1... | collective-permute-start | bytes 200 | tf_op jit(solution)/shard_map/ppermute | solution.py:603
  4.4 4.4 %copy-start.1 = (bf16[1,384,2048]{2,1,0:T(8,128)(2,1)S(1)}, bf16[1,384,2048]{2,1,0:T(8,128)(2,1)}, u32[]{:S(2)}) copy-start(bf16[1,384,2048]{2,1,0:T(8,128)(2,1)} %param.18) | copy-start | bytes 4718596
  4.4 4.4 %copy-start.6 = (bf16[1,384,128]{2,1,0:T(8,128)(2,1)S(1)}, bf16[1,384,128]{2,1,0:T(8,128)(2,1)}, u32[]{:S(2)}) copy-start(bf16[1,384,128]{2,1,0:T(8,128)(2,1)} %param.20) | copy-start | bytes 294916
  4.4 4.4 %copy-start.8 = (f32[1,384,32]{1,2,0:T(8,128)S(1)}, f32[1,384,32]{1,2,0:T(8,128)}, u32[]{:S(2)}) copy-start(f32[1,384,32]{1,2,0:T(8,128)} %param.22) | copy-start | bytes 147460
  4.4 6.9 %slice-start = ((s8[8388608]{0:T(1024)(128)(4,1)}), s8[4194304]{0:T(1024)(128)(4,1)S(1)}, s32[]{:S(2)}) async-start(s8[8388608]{0:T(1024)(128)(4,1)} %bitcast.32), calls=%async_computation | async-start | bytes 8388608
  4.5 13.9 %collective-permute-start.4 = (bf16[2,384,256]{2,1,0:T(8,128)(2,1)S(1)}, bf16[2,384,256]{2,1,0:T(8,128)(2,1)S(1)}, u32[]{:S(2)}, u32[]{:S(2)}) collective-permute-start(bf16[2,384,256]{2,1,0:T(8,128)(2,1)S(1)} %laid_together.3.refs_4_.refs_0_), channel_id=1, source_target_pairs={{0,16},{8,24},{1,17},{9,25},{2,18},{10,26},{3,19},{11,27},{4,20},{... | collective-permute-start | bytes 1179656 | tf_op jit(solution)/shard_map/ppermute | solution.py:594
  8.8 2.6 %slice-start.1 = ((s8[8388608]{0:T(1024)(128)(4,1)}), s8[4194304]{0:T(1024)(128)(4,1)S(1)}, s32[]{:S(2)}) async-start(s8[8388608]{0:T(1024)(128)(4,1)} %bitcast.32), calls=%async_computation.1 | async-start | bytes 8388608
  8.8 2.8 %copy-start = (bf16[32,2,64,256]{3,2,1,0:T(8,128)(2,1)S(1)}, bf16[32,2,64,256]{3,2,1,0:T(8,128)(2,1)}, u32[]{:S(2)}) copy-start(bf16[32,2,64,256]{3,2,1,0:T(8,128)(2,1)} %refs_2_.1) | copy-start | bytes 6291460
  10.6 3.9 %collective-permute-start.2 = (bf16[144,2048]{1,0:T(8,128)(2,1)S(1)}, bf16[144,2048]{1,0:T(8,128)(2,1)S(1)}, u32[]{:S(2)}, u32[]{:S(2)}) collective-permute-start(bf16[144,2048]{1,0:T(8,128)(2,1)S(1)} %get-tuple-element.18.refs_4_), channel_id=1, source_target_pairs={{0,8},{8,0},{16,24},{24,16},{1,9},{9,1},{17,25},{25,17},{2,10},{10... | collective-permute-start | bytes 1769480 | tf_op jit(solution)/shard_map/ppermute | solution.py:596
  12.3 7.8 %collective-permute-start.6 = (bf16[3,2,64,256]{3,2,1,0:T(8,128)(2,1)S(1)}, bf16[3,2,64,256]{3,2,1,0:T(8,128)(2,1)S(1)}, u32[]{:S(2)}, u32[]{:S(2)}) collective-permute-start(bf16[3,2,64,256]{3,2,1,0:T(8,128)(2,1)S(1)} %get-tuple-element.25), channel_id=1, source_target_pairs={{4,0},{0,4},{5,1},{1,5},{6,2},{2,6},{7,3},{3,7},{12,8},{8,12},{13,... | collective-permute-start | bytes 589832 | tf_op jit(solution)/shard_map/ppermute | solution.py:609
  12.9 14.9 %collective-permute-start.1 = (bf16[3,32,16,128]{3,2,1,0:T(8,128)(2,1)S(1)}, bf16[3,32,16,128]{3,2,1,0:T(8,128)(2,1)S(1)}, u32[]{:S(2)}, u32[]{:S(2)}) collective-permute-start(bf16[3,32,16,128]{3,2,1,0:T(8,128)(2,1)S(1)} %get-tuple-element.20), channel_id=1, source_target_pairs={{4,0},{0,4},{5,1},{1,5},{6,2},{2,6},{7,3},{3,7},{12,8},{8,12},{13,... | collective-permute-start | bytes 1179656 | tf_op jit(solution)/shard_map/ppermute | solution.py:610
  14.4 1.5 %copy-start.7 = (bf16[1,384,128]{2,1,0:T(8,128)(2,1)S(1)}, bf16[1,384,128]{2,1,0:T(8,128)(2,1)}, u32[]{:S(2)}) copy-start(bf16[1,384,128]{2,1,0:T(8,128)(2,1)} %param.21) | copy-start | bytes 294916
  14.4 1.5 %copy-start.10 = (f32[32]{0:T(128)S(1)}, f32[32]{0:T(128)}, u32[]{:S(2)}) copy-start(f32[32]{0:T(128)} %param.23) | copy-start | bytes 388
  14.6 11.1 %collective-permute-start.3 = (bf16[144,1024]{1,0:T(8,128)(2,1)S(1)}, bf16[144,1024]{1,0:T(8,128)(2,1)S(1)}, u32[]{:S(2)}, u32[]{:S(2)}) collective-permute-start(bf16[144,1024]{1,0:T(8,128)(2,1)S(1)} %middle_state.1.refs_7_), channel_id=1, source_target_pairs={{0,16},{8,24},{1,17},{9,25},{2,18},{10,26},{3,19},{11,27},{4,20},{... | collective-permute-start | bytes 884744 | tf_op jit(solution)/shard_map/ppermute | solution.py:619
  18.4 2.4 %collective-permute-start.5 = (bf16[4,384,256]{2,1,0:T(8,128)(2,1)S(1)}, bf16[4,384,256]{2,1,0:T(8,128)(2,1)S(1)}, u32[]{:S(2)}, u32[]{:S(2)}) collective-permute-start(bf16[4,384,256]{2,1,0:T(8,128)(2,1)S(1)} %laid_together.4.refs_7_), channel_id=1, source_target_pairs={{0,8},{8,0},{16,24},{24,16},{1,9},{9,1},{17,25},{25,17},{2,10},{10... | collective-permute-start | bytes 2359304 | tf_op jit(solution)/shard_map/ppermute | solution.py:623
  18.5 2.3 %copy-start.2 = (bf16[1,384,2048]{2,1,0:T(8,128)(2,1)S(1)}, bf16[1,384,2048]{2,1,0:T(8,128)(2,1)}, u32[]{:S(2)}) copy-start(bf16[1,384,2048]{2,1,0:T(8,128)(2,1)} %param.19) | copy-start | bytes 4718596
  18.5 2.3 %copy-start.3 = (bf16[1,384,1024]{2,1,0:T(8,128)(2,1)S(1)}, bf16[1,384,1024]{2,1,0:T(8,128)(2,1)}, u32[]{:S(2)}) copy-start(bf16[1,384,1024]{2,1,0:T(8,128)(2,1)} %param.25) | copy-start | bytes 2359300
  25.7 2.9 %collective-permute-start.7 = (bf16[1,144,1024]{2,1,0:T(8,128)(2,1)S(1)}, bf16[1,144,1024]{2,1,0:T(8,128)(2,1)S(1)}, u32[]{:S(2)}, u32[]{:S(2)}) collective-permute-start(bf16[1,144,1024]{2,1,0:T(8,128)(2,1)S(1)} %laid_together.5.refs_7_), channel_id=1, source_target_pairs={{0,8},{8,0},{16,24},{24,16},{1,9},{9,1},{17,25},{25,17},{2,10},{10... | collective-permute-start | bytes 884744 | tf_op jit(solution)/shard_map/ppermute | solution.py:636
  31.0 7.4 %collective-permute-start.10 = (f32[8,384]{1,0:T(8,128)S(1)}, f32[8,384]{1,0:T(8,128)S(1)}, u32[]{:S(2)}, u32[]{:S(2)}) collective-permute-start(f32[8,384]{1,0:T(8,128)S(1)} %get-tuple-element.27.refs_11_.refs_4_), channel_id=1, source_target_pairs={{0,3},{1,0},{2,1},{3,2},{4,7},{5,4},{6,5},{7,6},{8,11},{9,8},{10,9... | collective-permute-start | bytes 36872 | tf_op jit(solution)/shard_map/ppermute | solution.py:642
  34.6 4.6 %collective-permute-start.9 = (f32[8,384]{1,0:T(8,128)S(1)}, f32[8,384]{1,0:T(8,128)S(1)}, u32[]{:S(2)}, u32[]{:S(2)}) collective-permute-start(f32[8,384]{1,0:T(8,128)S(1)} %get-tuple-element.27.refs_11_.refs_4_), channel_id=1, source_target_pairs={{0,2},{1,3},{2,0},{3,1},{4,6},{5,7},{6,4},{7,5},{8,10},{9,11},{10,... | collective-permute-start | bytes 36872 | tf_op jit(solution)/shard_map/ppermute | solution.py:642
  34.6 5.5 %collective-permute-start.8 = (f32[8,384]{1,0:T(8,128)S(1)}, f32[8,384]{1,0:T(8,128)S(1)}, u32[]{:S(2)}, u32[]{:S(2)}) collective-permute-start(f32[8,384]{1,0:T(8,128)S(1)} %get-tuple-element.27.refs_11_.refs_4_), channel_id=1, source_target_pairs={{0,1},{1,2},{2,3},{3,0},{4,5},{5,6},{6,7},{7,4},{8,9},{9,10},{10,1... | collective-permute-start | bytes 36872 | tf_op jit(solution)/shard_map/ppermute | solution.py:642
  35.6 4.5 %copy-start.9 = (f32[2048]{0:T(1024)S(1)}, f32[2048]{0:T(1024)}, u32[]{:S(2)}) copy-start(f32[2048]{0:T(1024)} %param.24) | copy-start | bytes 24580

commit v4 on v3

--- a/solution.py
+++ b/solution.py
@@ -276,7 +276,7 @@
                 out[here, lanes] = y if i == 0 else y + earlier[i][:, at]
         return unused
 
-    lax.fori_loop(0, here_channels // width, heads_of, 0)
+    lax.fori_loop(0, here_channels // width, heads_of, 0, unroll=True)
 
 
 def local_scan(begin, size, operands, after):
@@ -639,7 +639,8 @@
     gated, squares = gate_output(running, c_in, gate_z, cached, met, middle, swapped, local)
     sums = [squares]
     for shift in range(1, mp):
-        sums.append(lax.ppermute(squares, "mp", [(i, (i + shift) % mp) for i in range(mp)]))
+        pairs = [(i, i ^ shift if mp & (mp - 1) == 0 else (i + shift) % mp) for i in range(mp)]
+        sums.append(lax.ppermute(squares, "mp", pairs))
     attended, late = attend(tuple(range(q_heads - later, q_heads)), early, (squares,), ())
     ssm_out, attended = norm_output(
         new_len, gated, norm_gain[None], sums, channels_all, late, attended

time: 41.9 us -> 41 us (0.979)
  waiting for transfers between devices: 3.56 us -> 3.05 us
    ppermute x3, waiting for transfers between devices: 1.73 us -> 1.05 us  [per_device(): sums.append(lax.ppermute(squares, 'mp', pairs))]
  transfers between devices with their start and end apart: 11 -> 11, of which waited for: 5 -> 4; matrix products, arithmetic and copies ran while one was open for 0% -> 0% of each run, Pallas kernels for 38% -> 38%
where the time goes in v4:
time: 41 us; the launch traced here: 40.8 us
  Pallas kernels  19.3 us (47%)
  starting transfers between devices  14.9 us (36%)
  waiting for transfers between devices  3.05 us (7%)
  between operations  2.47 us (6%)
  local copies, waits for them, and re-layouts  1.02 us (2%)
    pallas_call x15, Pallas kernels, call(): return lambda *operands: run(*operands, *unread)  19.3 us
    ppermute x3, starting transfers between devices, per_device(): sums.append(lax.ppermute(squares, 'mp', pairs))  4.42 us
    ppermute x1, starting transfers between devices, per_device(): far = lax.ppermute(fresh, 'seq', across)  3.68 us
    ppermute x1, starting transfers between devices, per_device(): asked = lax.ppermute(lists, 'batch', there)  2.97 us
    ppermute x1, starting transfers between devices, per_device(): st_received.append(lax.ppermute(found[1], 'batch', back))  1.52 us
    ppermute x1, starting transfers between devices, per_device(): middle = lax.ppermute(sent, 'seq', across)  1.4 us
    ppermute x3, waiting for transfers between devices, per_device(): sums.append(lax.ppermute(squares, 'mp', pairs))  1.05 us
    unnamed x34, local copies, waits for them, and re-layouts  1.02 us
  transfers between devices with their start and end apart: 11, of which 4 were waited for; matrix products, arithmetic and copies ran while one was open for 0% of the time, Pallas kernels for 38%

profile of v4, /device:TPU:0, one launch (start us, length us, event | category | flops | bytes accessed | tf_op | source)
XLA Modules:
  0.0 40.8 jit_solution(7795780670560943547)
XLA Ops:
  0.6 0.0 copy-start.11
  0.6 0.0 copy-start.12
  0.7 0.0 copy-start.13
  0.7 0.0 copy-start.14
  0.7 0.0 copy-start.5
  0.7 0.0 copy-start.4
  0.7 0.6 %copy-done.11 = s32[1,4]{1,0:T(1,128)S(1)} copy-done((s32[1,4]{1,0:T(1,128)S(1)}, s32[1,4]{1,0:T(1,128)}, u32[]{:S(2)}) %copy-start.11) | copy-done | bytes 40
  1.3 0.0 copy-done.12
  1.3 0.0 copy-done.13
  1.3 0.0 copy-done.14
  1.3 0.1 add_add_fusion.refs_2_.refs_1_.refs_0_
  1.4 3.0 %collective-permute-start = (s32[16]{0:T(128)S(1)}, s32[16]{0:T(128)S(1)}, u32[]{:S(2)}, u32[]{:S(2)}) collective-permute-start(s32[16]{0:T(128)S(1)} %add_add_fusion.refs_2_.refs_1_.refs_0_), channel_id=1, source_target_pairs={{0,4},{4,0},{1,5},{5,1},{2,6},{6,2},{3,7},{7,3},{8,12},{12,8},{9,1... | collective-permute-start | bytes 200 | tf_op jit(solution)/shard_map/ppermute | solution.py:603
  4.4 0.0 copy-done.5
  4.4 0.0 copy-done.4
  4.4 0.0 copy-start.8
  4.4 0.0 slice-start
  4.5 3.7 %collective-permute-start.4 = (bf16[2,384,256]{2,1,0:T(8,128)(2,1)S(1)}, bf16[2,384,256]{2,1,0:T(8,128)(2,1)S(1)}, u32[]{:S(2)}, u32[]{:S(2)}) collective-permute-start(bf16[2,384,256]{2,1,0:T(8,128)(2,1)S(1)} %laid_together.3.refs_4_.refs_0_), channel_id=1, source_target_pairs={{0,16},{8,24},{1,17},{9,25},{2,18},{10,26},{3,19},{11,27},{4,20},{... | collective-permute-start | bytes 1179656 | tf_op jit(solution)/shard_map/ppermute | solution.py:594
  8.8 0.0 slice-start.1
  8.8 0.0 copy-done.1
  8.8 0.0 copy-done.6
  8.8 0.0 copy-done.8
  8.8 0.0 copy-start
  8.9 1.7 %end_state.1 = (bf16[144,2048]{1,0:T(8,128)(2,1)S(1)}, f32[128,2048]{1,0:T(8,128)S(1)}, f32[8,2048]{1,0:T(8,128)S(1)}, f32[384,32]{1,0:T(8,128)S(1)}, f32[32,384]{1,0:T(8,128)S(1)}) custom-call(s32[1,1]{1,0:T(1,128)} %bitcast.23.refs_0_, f32[32,384]{1,0:T(8,128)S(1)} %bitcast.57, bf16[384,128]{1,0:T(8,128)(2,1)S(1)} %bitcast.49, ...), custom_call_target="tpu_custom_call" | custom-call | flops 10000000000 | bytes 10000000 | tf_op jit(solution)/shard_map/end_state/pallas_call | solution.py:46
  10.6 0.1 collective-permute-start.2
  11.3 0.0 collective-permute-done.refs_0_
  11.3 0.0 slice-done
  11.4 0.0 slice-done.1
  11.4 0.3 copy-done
  11.7 0.7 %look_up.1 = (bf16[3,2,64,256]{3,2,1,0:T(8,128)(2,1)S(1)}, bf16[3,32,16,128]{3,2,1,0:T(8,128)(2,1)S(1)}, bf16[4,2,64,256]{3,2,1,0:T(8,128)(2,1)S(1)}, bf16[4,32,16,128]{3,2,1,0:T(8,128)(2,1)S(1)}) custom-call(s32[16]{0:T(128)S(1)} %collective-permute-done.refs_0_, s32[16]{0:T(128)S(1)} %add_add_fusion.refs_2_.refs_1_.refs_0_, ...), custom_call_target="tpu_custom_call" | custom-call | flops 10000000000 | bytes 10000000 | tf_op jit(solution)/shard_map/look_up/pallas_call | solution.py:46
  12.3 0.6 %collective-permute-start.6 = (bf16[3,2,64,256]{3,2,1,0:T(8,128)(2,1)S(1)}, bf16[3,2,64,256]{3,2,1,0:T(8,128)(2,1)S(1)}, u32[]{:S(2)}, u32[]{:S(2)}) collective-permute-start(bf16[3,2,64,256]{3,2,1,0:T(8,128)(2,1)S(1)} %get-tuple-element.25), channel_id=1, source_target_pairs={{4,0},{0,4},{5,1},{1,5},{6,2},{2,6},{7,3},{3,7},{12,8},{8,12},{13,... | collective-permute-start | bytes 589832 | tf_op jit(solution)/shard_map/ppermute | solution.py:609
  12.9 1.5 %collective-permute-start.1 = (bf16[3,32,16,128]{3,2,1,0:T(8,128)(2,1)S(1)}, bf16[3,32,16,128]{3,2,1,0:T(8,128)(2,1)S(1)}, u32[]{:S(2)}, u32[]{:S(2)}) collective-permute-start(bf16[3,32,16,128]{3,2,1,0:T(8,128)(2,1)S(1)} %get-tuple-element.20), channel_id=1, source_target_pairs={{4,0},{0,4},{5,1},{1,5},{6,2},{2,6},{7,3},{3,7},{12,8},{8,12},{13,... | collective-permute-start | bytes 1179656 | tf_op jit(solution)/shard_map/ppermute | solution.py:610
  14.4 0.0 collective-permute-done.2.refs_0_.refs_4_
  14.4 0.1 middle_state.1.refs_7_
  14.6 1.4 %collective-permute-start.3 = (bf16[144,1024]{1,0:T(8,128)(2,1)S(1)}, bf16[144,1024]{1,0:T(8,128)(2,1)S(1)}, u32[]{:S(2)}, u32[]{:S(2)}) collective-permute-start(bf16[144,1024]{1,0:T(8,128)(2,1)S(1)} %middle_state.1.refs_7_), channel_id=1, source_target_pairs={{0,16},{8,24},{1,17},{9,25},{2,18},{10,26},{3,19},{11,27},{4,20},{... | collective-permute-start | bytes 884744 | tf_op jit(solution)/shard_map/ppermute | solution.py:619
  16.0 0.0 copy-done.7
  16.0 0.0 copy-done.10
  16.0 2.2 %local_scan.3.refs_2_.refs_7_ = f32[384,1024]{1,0:T(8,128)S(1)} custom-call(s32[1,1]{1,0:T(1,128)} %bitcast.24.refs_0_, f32[384,32]{1,0:T(8,128)S(1)} %get-tuple-element.17.refs_1_.refs_0_, f32[32,384]{1,0:T(8,128)S(1)} %get-tuple-element.21.refs_2_, bf16[384,128]{1,0:T(8,128)(2,1)S(1)} %bitcast.50, bf16[384,128]{1,0:T(8,128)(2,1)S(1)} %bitcast.53, ...), custom_call_target="tpu_custom_call" | custom-call | flops 10000000000 | bytes 10000000 | tf_op jit(solution)/shard_map/local_scan/pallas_call | solution.py:46
  18.1 0.0 collective-permute-done.4.refs_1_.refs_6_
  18.2 0.1 laid_together.4.refs_7_
  18.2 0.1 collective-permute-start.5
  18.3 0.0 copy-start.2
  18.3 0.0 copy-start.3
  18.3 1.2 %local_scan.4.refs_10_.refs_8_ = f32[384,512]{1,0:T(8,128)S(1)} custom-call(s32[1,1]{1,0:T(1,128)} %bitcast.25.refs_0_, f32[384,32]{1,0:T(8,128)S(1)} %get-tuple-element.17.refs_1_.refs_0_, f32[32,384]{1,0:T(8,128)S(1)} %get-tuple-element.21.refs_2_, bf16[384,128]{1,0:T(8,128)(2,1)S(1)} %bitcast.51, bf16[384,128]{1,0:T(8,128)(2,1)S(1)} %bitcast.54, ...), custom_call_target="tpu_custom_call" | custom-call | flops 10000000000 | bytes 10000000 | tf_op jit(solution)/shard_map/local_scan/pallas_call | solution.py:46
  19.5 0.7 %collective-permute-done.6.refs_9_ = bf16[3,2,64,256]{3,2,1,0:T(8,128)(2,1)S(1)} collective-permute-done((bf16[3,2,64,256]{3,2,1,0:T(8,128)(2,1)S(1)}, bf16[3,2,64,256]{3,2,1,0:T(8,128)(2,1)S(1)}, u32[]{:S(2)}, u32[]{:S(2)}) %collective-permute-start.6) | collective-permute-done | bytes 196640 | tf_op jit(solution)/shard_map/ppermute | solution.py:609
  20.1 0.4 %collective-permute-done.5.refs_7_ = bf16[4,384,256]{2,1,0:T(8,128)(2,1)S(1)} collective-permute-done((bf16[4,384,256]{2,1,0:T(8,128)(2,1)S(1)}, bf16[4,384,256]{2,1,0:T(8,128)(2,1)S(1)}, u32[]{:S(2)}, u32[]{:S(2)}) %collective-permute-start.5) | collective-permute-done | bytes 786464 | tf_op jit(solution)/shard_map/ppermute | solution.py:623
  20.6 0.0 copy-done.2
  20.6 0.0 copy-done.3
  20.6 4.9 %attention.2.refs_1_.refs_10_ = bf16[384,768]{1,0:T(8,128)(2,1)S(1)} custom-call(s32[1,1]{1,0:T(1,128)} %bitcast.26.refs_0_, s32[1,1]{1,0:T(1,128)} %bitcast.30.refs_1_, s32[16]{0:T(128)S(1)} %add_add_fusion.refs_2_.refs_1_.refs_0_, bf16[384,1024]{1,0:T(8,128)(2,1)S(1)} %bitcast.40, bf16[384,256]{1,0:T(8,128)(2,1)S(1)} %bitcast.44, ...), custom_call_target="tpu_custom_call" | custom-call | flops 10000000000 | bytes 10000000 | tf_op jit(solution)/shard_map/attention/pallas_call | solution.py:46
  25.5 0.0 collective-permute-done.3.refs_0_.refs_5_
  25.5 0.2 collective-permute-start.7
  25.7 1.2 %local_scan.5.refs_3_.refs_9_ = f32[384,512]{1,0:T(8,128)S(1)} custom-call(s32[1,1]{1,0:T(1,128)} %bitcast.27.refs_0_, f32[384,32]{1,0:T(8,128)S(1)} %get-tuple-element.17.refs_1_.refs_0_, f32[32,384]{1,0:T(8,128)S(1)} %get-tuple-element.21.refs_2_, bf16[384,128]{1,0:T(8,128)(2,1)S(1)} %bitcast.52, bf16[384,128]{1,0:T(8,128)(2,1)S(1)} %bitcast.55, ...), custom_call_target="tpu_custom_call" | custom-call | flops 10000000000 | bytes 10000000 | tf_op jit(solution)/shard_map/local_scan/pallas_call | solution.py:46
  26.9 0.9 %collective-permute-done.1.refs_2_ = bf16[3,32,16,128]{3,2,1,0:T(8,128)(2,1)S(1)} collective-permute-done((bf16[3,32,16,128]{3,2,1,0:T(8,128)(2,1)S(1)}, bf16[3,32,16,128]{3,2,1,0:T(8,128)(2,1)S(1)}, u32[]{:S(2)}, u32[]{:S(2)}) %collective-permute-start.1) | collective-permute-done | bytes 393248 | tf_op jit(solution)/shard_map/ppermute | solution.py:610
  27.8 0.8 %cached_state.1.refs_3_ = bf16[128,2048]{1,0:T(8,128)(2,1)S(1)} custom-call(s32[16]{0:T(128)S(1)} %add_add_fusion.refs_2_.refs_1_.refs_0_, bf16[4,32,16,128]{3,2,1,0:T(8,128)(2,1)S(1)} %get-tuple-element.19.refs_1_, bf16[3,32,16,128]{3,2,1,0:T(8,128)(2,1)S(1)} %collective-permute-done.1.refs_2_, f32[384,512]{1,0:T(8,128)S(1)} %local_scan.5.refs_3_.refs_9_), custom_call_target="tpu_custom_call" | custom-call | flops 10000000000 | bytes 10000000 | tf_op jit(solution)/shard_map/cached_state/pallas_call | solution.py:46
  28.6 0.0 collective-permute-done.7
  28.7 2.3 %gate.1 = (bf16[384,2048]{1,0:T(8,128)(2,1)S(1)}, f32[8,384]{1,0:T(8,128)S(1)}) custom-call(f32[384,32]{1,0:T(8,128)S(1)} %get-tuple-element.17.refs_1_.refs_0_, bf16[384,128]{1,0:T(8,128)(2,1)S(1)} %bitcast.56, bf16[384,2048]{1,0:T(8,128)(2,1)S(1)} %bitcast.39, bf16[128,2048]{1,0:T(8,128)(2,1)S(1)} %cached_state.1.refs_3_, ...), custom_call_target="tpu_custom_call" | custom-call | flops 10000000000 | bytes 10000000 | tf_op jit(solution)/shard_map/gate/pallas_call | solution.py:46
  31.0 3.6 %collective-permute-start.10 = (f32[8,384]{1,0:T(8,128)S(1)}, f32[8,384]{1,0:T(8,128)S(1)}, u32[]{:S(2)}, u32[]{:S(2)}) collective-permute-start(f32[8,384]{1,0:T(8,128)S(1)} %get-tuple-element.27.refs_11_.refs_4_), channel_id=1, source_target_pairs={{0,3},{1,2},{2,1},{3,0},{4,7},{5,6},{6,5},{7,4},{8,11},{9,10},{10,... | collective-permute-start | bytes 36872 | tf_op jit(solution)/shard_map/ppermute | solution.py:643
  34.6 0.0 collective-permute-start.9
  34.6 0.8 %collective-permute-start.8 = (f32[8,384]{1,0:T(8,128)S(1)}, f32[8,384]{1,0:T(8,128)S(1)}, u32[]{:S(2)}, u32[]{:S(2)}) collective-permute-start(f32[8,384]{1,0:T(8,128)S(1)} %get-tuple-element.27.refs_11_.refs_4_), channel_id=1, source_target_pairs={{0,1},{1,0},{2,3},{3,2},{4,5},{5,4},{6,7},{7,6},{8,9},{9,8},{10,11... | collective-permute-start | bytes 36872 | tf_op jit(solution)/shard_map/ppermute | solution.py:643
  35.4 2.7 %attention.3 = (bf16[384,1024]{1,0:T(8,128)(2,1)}, bf16[384,256]{1,0:T(8,128)(2,1)S(1)}) custom-call(s32[1,1]{1,0:T(1,128)} %bitcast.28.refs_0_, s32[1,1]{1,0:T(1,128)} %bitcast.31.refs_1_, s32[16]{0:T(128)S(1)} %add_add_fusion.refs_2_.refs_1_.refs_0_, bf16[384,1024]{1,0:T(8,128)(2,1)S(1)} %bitcast.41, bf16[384,256]{1,0:T(8,128)(2,1)S(1)} %bitcast.45, ...), custom_call_target="tpu_custom_call" | custom-call | flops 10000000000 | bytes 10000000 | tf_op jit(solution)/shard_map/attention/pallas_call | solution.py:46
  38.1 0.0 collective-permute-done.10.refs_7_
  38.1 1.0 %collective-permute-done.9.refs_6_ = f32[8,384]{1,0:T(8,128)S(1)} collective-permute-done((f32[8,384]{1,0:T(8,128)S(1)}, f32[8,384]{1,0:T(8,128)S(1)}, u32[]{:S(2)}, u32[]{:S(2)}) %collective-permute-start.9) | collective-permute-done | bytes 12320 | tf_op jit(solution)/shard_map/ppermute | solution.py:643
  39.2 0.0 collective-permute-done.8.refs_5_
  39.2 0.0 copy-done.9
  39.2 1.5 %norm.1 = (bf16[384,2048]{1,0:T(8,128)(2,1)}, bf16[384,1024]{1,0:T(8,128)(2,1)}) custom-call(s32[1,1]{1,0:T(1,128)} %bitcast.29.refs_0_, bf16[384,2048]{1,0:T(8,128)(2,1)S(1)} %get-tuple-element.26.refs_1_, f32[1,2048]{1,0:T(1,128)S(1)} %bitcast.58, bf16[384,256]{1,0:T(8,128)(2,1)S(1)} %get-tuple-element.28.refs_3_, ...), custom_call_target="tpu_custom_call", output_to_operand_aliasing={{1}: (8, {})} | custom-call | flops 10000000000 | bytes 10000000 | tf_op jit(solution)/shard_map/norm/pallas_call | solution.py:46
  (9 shorter events, 0.1 us)
Async XLA Ops:
  0.6 0.7 %copy-start.11 = (s32[1,4]{1,0:T(1,128)S(1)}, s32[1,4]{1,0:T(1,128)}, u32[]{:S(2)}) copy-start(s32[1,4]{1,0:T(1,128)} %param.35) | copy-start | bytes 52
  0.6 0.7 %copy-start.12 = (s32[1,4,1]{1,2,0:T(1,128)S(1)}, s32[1,4,1]{1,2,0:T(1,128)}, u32[]{:S(2)}) copy-start(s32[1,4,1]{1,2,0:T(1,128)} %param.34) | copy-start | bytes 52
  0.7 0.7 %copy-start.13 = (s32[1,4]{1,0:T(1,128)S(1)}, s32[1,4]{1,0:T(1,128)}, u32[]{:S(2)}) copy-start(s32[1,4]{1,0:T(1,128)} %param.33) | copy-start | bytes 52
  0.7 0.7 %copy-start.14 = (s32[1,4,1]{1,2,0:T(1,128)S(1)}, s32[1,4,1]{1,2,0:T(1,128)}, u32[]{:S(2)}) copy-start(s32[1,4,1]{1,2,0:T(1,128)} %param.32) | copy-start | bytes 52
  0.7 3.7 %copy-start.5 = (bf16[1,384,256]{2,1,0:T(8,128)(2,1)S(1)}, bf16[1,384,256]{2,1,0:T(8,128)(2,1)}, u32[]{:S(2)}) copy-start(bf16[1,384,256]{2,1,0:T(8,128)(2,1)} %param.27) | copy-start | bytes 589828
  0.7 3.7 %copy-start.4 = (bf16[1,384,256]{2,1,0:T(8,128)(2,1)S(1)}, bf16[1,384,256]{2,1,0:T(8,128)(2,1)}, u32[]{:S(2)}) copy-start(bf16[1,384,256]{2,1,0:T(8,128)(2,1)} %param.26) | copy-start | bytes 589828
  1.4 9.9 %collective-permute-start = (s32[16]{0:T(128)S(1)}, s32[16]{0:T(128)S(1)}, u32[]{:S(2)}, u32[]{:S(2)}) collective-permute-start(s32[16]{0:T(128)S(1)} %add_add_fusion.refs_2_.refs_1_.refs_0_), channel_id=1, source_target_pairs={{0,4},{4,0},{1,5},{5,1},{2,6},{6,2},{3,7},{7,3},{8,12},{12,8},{9,1... | collective-permute-start | bytes 200 | tf_op jit(solution)/shard_map/ppermute | solution.py:603
  4.4 4.4 %copy-start.1 = (bf16[1,384,2048]{2,1,0:T(8,128)(2,1)S(1)}, bf16[1,384,2048]{2,1,0:T(8,128)(2,1)}, u32[]{:S(2)}) copy-start(bf16[1,384,2048]{2,1,0:T(8,128)(2,1)} %param.18) | copy-start | bytes 4718596
  4.4 4.4 %copy-start.6 = (bf16[1,384,128]{2,1,0:T(8,128)(2,1)S(1)}, bf16[1,384,128]{2,1,0:T(8,128)(2,1)}, u32[]{:S(2)}) copy-start(bf16[1,384,128]{2,1,0:T(8,128)(2,1)} %param.20) | copy-start | bytes 294916
  4.4 4.4 %copy-start.8 = (f32[1,384,32]{1,2,0:T(8,128)S(1)}, f32[1,384,32]{1,2,0:T(8,128)}, u32[]{:S(2)}) copy-start(f32[1,384,32]{1,2,0:T(8,128)} %param.22) | copy-start | bytes 147460
  4.4 6.9 %slice-start = ((s8[8388608]{0:T(1024)(128)(4,1)}), s8[4194304]{0:T(1024)(128)(4,1)S(1)}, s32[]{:S(2)}) async-start(s8[8388608]{0:T(1024)(128)(4,1)} %bitcast.32), calls=%async_computation | async-start | bytes 8388608
  4.5 13.7 %collective-permute-start.4 = (bf16[2,384,256]{2,1,0:T(8,128)(2,1)S(1)}, bf16[2,384,256]{2,1,0:T(8,128)(2,1)S(1)}, u32[]{:S(2)}, u32[]{:S(2)}) collective-permute-start(bf16[2,384,256]{2,1,0:T(8,128)(2,1)S(1)} %laid_together.3.refs_4_.refs_0_), channel_id=1, source_target_pairs={{0,16},{8,24},{1,17},{9,25},{2,18},{10,26},{3,19},{11,27},{4,20},{... | collective-permute-start | bytes 1179656 | tf_op jit(solution)/shard_map/ppermute | solution.py:594
  8.8 2.6 %slice-start.1 = ((s8[8388608]{0:T(1024)(128)(4,1)}), s8[4194304]{0:T(1024)(128)(4,1)S(1)}, s32[]{:S(2)}) async-start(s8[8388608]{0:T(1024)(128)(4,1)} %bitcast.32), calls=%async_computation.1 | async-start | bytes 8388608
  8.8 2.8 %copy-start = (bf16[32,2,64,256]{3,2,1,0:T(8,128)(2,1)S(1)}, bf16[32,2,64,256]{3,2,1,0:T(8,128)(2,1)}, u32[]{:S(2)}) copy-start(bf16[32,2,64,256]{3,2,1,0:T(8,128)(2,1)} %refs_2_.1) | copy-start | bytes 6291460
  10.6 3.9 %collective-permute-start.2 = (bf16[144,2048]{1,0:T(8,128)(2,1)S(1)}, bf16[144,2048]{1,0:T(8,128)(2,1)S(1)}, u32[]{:S(2)}, u32[]{:S(2)}) collective-permute-start(bf16[144,2048]{1,0:T(8,128)(2,1)S(1)} %get-tuple-element.18.refs_4_), channel_id=1, source_target_pairs={{0,8},{8,0},{16,24},{24,16},{1,9},{9,1},{17,25},{25,17},{2,10},{10... | collective-permute-start | bytes 1769480 | tf_op jit(solution)/shard_map/ppermute | solution.py:596
  12.3 7.8 %collective-permute-start.6 = (bf16[3,2,64,256]{3,2,1,0:T(8,128)(2,1)S(1)}, bf16[3,2,64,256]{3,2,1,0:T(8,128)(2,1)S(1)}, u32[]{:S(2)}, u32[]{:S(2)}) collective-permute-start(bf16[3,2,64,256]{3,2,1,0:T(8,128)(2,1)S(1)} %get-tuple-element.25), channel_id=1, source_target_pairs={{4,0},{0,4},{5,1},{1,5},{6,2},{2,6},{7,3},{3,7},{12,8},{8,12},{13,... | collective-permute-start | bytes 589832 | tf_op jit(solution)/shard_map/ppermute | solution.py:609
  12.9 14.9 %collective-permute-start.1 = (bf16[3,32,16,128]{3,2,1,0:T(8,128)(2,1)S(1)}, bf16[3,32,16,128]{3,2,1,0:T(8,128)(2,1)S(1)}, u32[]{:S(2)}, u32[]{:S(2)}) collective-permute-start(bf16[3,32,16,128]{3,2,1,0:T(8,128)(2,1)S(1)} %get-tuple-element.20), channel_id=1, source_target_pairs={{4,0},{0,4},{5,1},{1,5},{6,2},{2,6},{7,3},{3,7},{12,8},{8,12},{13,... | collective-permute-start | bytes 1179656 | tf_op jit(solution)/shard_map/ppermute | solution.py:610
  14.4 1.5 %copy-start.7 = (bf16[1,384,128]{2,1,0:T(8,128)(2,1)S(1)}, bf16[1,384,128]{2,1,0:T(8,128)(2,1)}, u32[]{:S(2)}) copy-start(bf16[1,384,128]{2,1,0:T(8,128)(2,1)} %param.21) | copy-start | bytes 294916
  14.4 1.5 %copy-start.10 = (f32[32]{0:T(128)S(1)}, f32[32]{0:T(128)}, u32[]{:S(2)}) copy-start(f32[32]{0:T(128)} %param.23) | copy-start | bytes 388
  14.6 10.9 %collective-permute-start.3 = (bf16[144,1024]{1,0:T(8,128)(2,1)S(1)}, bf16[144,1024]{1,0:T(8,128)(2,1)S(1)}, u32[]{:S(2)}, u32[]{:S(2)}) collective-permute-start(bf16[144,1024]{1,0:T(8,128)(2,1)S(1)} %middle_state.1.refs_7_), channel_id=1, source_target_pairs={{0,16},{8,24},{1,17},{9,25},{2,18},{10,26},{3,19},{11,27},{4,20},{... | collective-permute-start | bytes 884744 | tf_op jit(solution)/shard_map/ppermute | solution.py:619
  18.2 2.4 %collective-permute-start.5 = (bf16[4,384,256]{2,1,0:T(8,128)(2,1)S(1)}, bf16[4,384,256]{2,1,0:T(8,128)(2,1)S(1)}, u32[]{:S(2)}, u32[]{:S(2)}) collective-permute-start(bf16[4,384,256]{2,1,0:T(8,128)(2,1)S(1)} %laid_together.4.refs_7_), channel_id=1, source_target_pairs={{0,8},{8,0},{16,24},{24,16},{1,9},{9,1},{17,25},{25,17},{2,10},{10... | collective-permute-start | bytes 2359304 | tf_op jit(solution)/shard_map/ppermute | solution.py:623
  18.3 2.3 %copy-start.2 = (bf16[1,384,2048]{2,1,0:T(8,128)(2,1)S(1)}, bf16[1,384,2048]{2,1,0:T(8,128)(2,1)}, u32[]{:S(2)}) copy-start(bf16[1,384,2048]{2,1,0:T(8,128)(2,1)} %param.19) | copy-start | bytes 4718596
  18.3 2.3 %copy-start.3 = (bf16[1,384,1024]{2,1,0:T(8,128)(2,1)S(1)}, bf16[1,384,1024]{2,1,0:T(8,128)(2,1)}, u32[]{:S(2)}) copy-start(bf16[1,384,1024]{2,1,0:T(8,128)(2,1)} %param.25) | copy-start | bytes 2359300
  25.5 3.1 %collective-permute-start.7 = (bf16[1,144,1024]{2,1,0:T(8,128)(2,1)S(1)}, bf16[1,144,1024]{2,1,0:T(8,128)(2,1)S(1)}, u32[]{:S(2)}, u32[]{:S(2)}) collective-permute-start(bf16[1,144,1024]{2,1,0:T(8,128)(2,1)S(1)} %laid_together.5.refs_7_), channel_id=1, source_target_pairs={{0,8},{8,0},{16,24},{24,16},{1,9},{9,1},{17,25},{25,17},{2,10},{10... | collective-permute-start | bytes 884744 | tf_op jit(solution)/shard_map/ppermute | solution.py:636
  31.0 7.2 %collective-permute-start.10 = (f32[8,384]{1,0:T(8,128)S(1)}, f32[8,384]{1,0:T(8,128)S(1)}, u32[]{:S(2)}, u32[]{:S(2)}) collective-permute-start(f32[8,384]{1,0:T(8,128)S(1)} %get-tuple-element.27.refs_11_.refs_4_), channel_id=1, source_target_pairs={{0,3},{1,2},{2,1},{3,0},{4,7},{5,6},{6,5},{7,4},{8,11},{9,10},{10,... | collective-permute-start | bytes 36872 | tf_op jit(solution)/shard_map/ppermute | solution.py:643
  34.6 4.6 %collective-permute-start.9 = (f32[8,384]{1,0:T(8,128)S(1)}, f32[8,384]{1,0:T(8,128)S(1)}, u32[]{:S(2)}, u32[]{:S(2)}) collective-permute-start(f32[8,384]{1,0:T(8,128)S(1)} %get-tuple-element.27.refs_11_.refs_4_), channel_id=1, source_target_pairs={{0,2},{1,3},{2,0},{3,1},{4,6},{5,7},{6,4},{7,5},{8,10},{9,11},{10,... | collective-permute-start | bytes 36872 | tf_op jit(solution)/shard_map/ppermute | solution.py:643
  34.6 4.6 %collective-permute-start.8 = (f32[8,384]{1,0:T(8,128)S(1)}, f32[8,384]{1,0:T(8,128)S(1)}, u32[]{:S(2)}, u32[]{:S(2)}) collective-permute-start(f32[8,384]{1,0:T(8,128)S(1)} %get-tuple-element.27.refs_11_.refs_4_), channel_id=1, source_target_pairs={{0,1},{1,0},{2,3},{3,2},{4,5},{5,4},{6,7},{7,6},{8,9},{9,8},{10,11... | collective-permute-start | bytes 36872 | tf_op jit(solution)/shard_map/ppermute | solution.py:643
  35.4 3.8 %copy-start.9 = (f32[2048]{0:T(1024)S(1)}, f32[2048]{0:T(1024)}, u32[]{:S(2)}) copy-start(f32[2048]{0:T(1024)} %param.24) | copy-start | bytes 24580
